TPU v7x, 512 devices: a whole 4x8x8 slice. The times are simulated.
512 devices in a mesh: grp: 8 (over y_lo, x), ep: 64 (over y_hi, z, core).
Axes of the slice: x: 4, y: 8 (y_hi: 4, y_lo: 2; y = y_hi * 2 + y_lo), z: 8, core: 2. Of those that a mesh axis runs over, the one named last changes fastest.
Arguments:
- tokens: bfloat16 [256, 6144], P('grp', 'ep'), may hold values from -6 to 6
- query_weight: bfloat16 [6144, 8192], P('grp', 'ep'), may hold values from -0.078125 to 0.078125
- key_weight: bfloat16 [6144, 8192], P('grp', 'ep'), may hold values from -0.078125 to 0.078125
- value_weight: bfloat16 [6144, 8192], P('grp', 'ep'), may hold values from -0.078125 to 0.078125
- output_weight: bfloat16 [6144, 8192], P('grp', 'ep'), may hold values from -0.0625 to 0.0625
- gate_weight: bfloat16 [6144, 18432], P('grp', 'ep'), may hold values from -0.078125 to 0.078125
- up_weight: bfloat16 [6144, 18432], P('grp', 'ep'), may hold values from -0.078125 to 0.078125
- down_weight: bfloat16 [6144, 18432], P('grp', 'ep'), may hold values from -0.0625 to 0.0625
- router_weight: bfloat16 [6144, 32], replicated, may hold values from -0.078125 to 0.078125
- attn_gain: float32 [6144], replicated, may hold values from 0.1 to 1.9
- expert_gain: float32 [6144], replicated, may hold values from 0.1 to 1.9
- decay_rate: float32 [64], P('ep'), may hold values from 0.02 to 2
- states: float32 [256, 64, 128, 128], P('grp', 'ep'), may hold values from -12 to 12
- expert_ids: int32 [256, 2], P('grp'), may hold values from 0 to 31, all different within a row
- row_slot: int32 [256], P('grp'), may hold values from 0 to 31, as said below
- migration: int32 [16, 3], replicated, may hold values from 0 to 31, as said below
Outputs:
- layer_out: bfloat16 [256, 6144], P('grp', 'ep')
Inputs may be any that keep to these rules, and one draw needn't show every extreme that they name: Within each group's 32 rows, row_slot is a permutation of 0 to 31. `migration`: column 0 names a group below the last, column 1 any slot, column 2 distinct slots of the last group.
All inputs are finite; a program needn't handle non-finite values.
Results may differ from a plain program's by a relative error of at most 0.017.
Values may be sent and summed in bfloat16 or wider, within the bound.
No kernel may reach another device: no remote copies, remote signals or barrier semaphores. Data moves between devices by JAX's collectives and lax.ppermute only.
A program may use at most 64 MiB of HBM per device.

v0:
```python
import jax
import jax.numpy as jnp
from jax import lax
from jax.sharding import PartitionSpec as P

FF = 9216


def normed(rows, gain):
    wide = rows.astype(jnp.float32)
    return wide * lax.rsqrt(jnp.mean(wide * wide, axis=-1, keepdims=True) + 1e-06) * gain


def contract_last(left, right):
    return lax.dot_general(
        left, right, (((1,), (1,)), ((), ())), preferred_element_type=jnp.float32
    )


def shards(
    tokens,
    query_weight,
    key_weight,
    value_weight,
    output_weight,
    gate_weight,
    up_weight,
    down_weight,
    router_weight,
    attn_gain,
    expert_gain,
    decay_rate,
    states,
    expert_ids,
    row_slot,
    migration,
):
    group = lax.axis_index("grp")
    groups = lax.axis_size("grp")
    device = lax.axis_index("ep")
    width = tokens.shape[1]
    held_units = gate_weight.shape[1]
    whole = lax.all_gather(tokens, "ep", axis=1, tiled=True)
    attn_in = normed(whole, attn_gain).astype(jnp.bfloat16)
    query_full, key_full, value_full, output_full, gate_full, up_full, down_full = (
        lax.all_gather(query_weight, "grp", axis=0, tiled=True),
        lax.all_gather(key_weight, "grp", axis=0, tiled=True),
        lax.all_gather(value_weight, "grp", axis=0, tiled=True),
        lax.all_gather(output_weight, "grp", axis=0, tiled=True),
        lax.all_gather(gate_weight, "grp", axis=0, tiled=True),
        lax.all_gather(up_weight, "grp", axis=0, tiled=True),
        lax.all_gather(down_weight, "grp", axis=0, tiled=True),
    )
    query_rows = jax.nn.silu(jnp.dot(attn_in, query_full, preferred_element_type=jnp.float32))
    key_rows = jax.nn.silu(jnp.dot(attn_in, key_full, preferred_element_type=jnp.float32))
    value_rows = jax.nn.silu(jnp.dot(attn_in, value_full, preferred_element_type=jnp.float32))
    stored = states[:, 0]
    source_group = migration[:, 0]
    source_slot = migration[:, 1]
    target_slot = migration[:, 2]
    packet = jnp.where((source_group == group)[:, None, None], stored[source_slot], 0.0)
    moved = lax.psum(packet.astype(jnp.bfloat16), "grp").astype(jnp.float32)
    joined = jnp.where(group == groups - 1, stored.at[target_slot].set(moved), stored)
    current = joined[row_slot]
    retain = jnp.exp(-decay_rate[0])
    fresh = retain * current + key_rows[:, :, None] * value_rows[:, None, :]
    mixed = jnp.einsum("si,sij->sj", query_rows, fresh, precision=lax.Precision.HIGHEST)
    heads_out = (mixed * lax.rsqrt(jnp.mean(mixed * mixed, axis=-1, keepdims=True) + 1e-06)).astype(
        jnp.bfloat16
    )
    partial_attn = contract_last(heads_out, output_full)
    attn_sum = lax.psum(partial_attn, "ep")
    resid_full = (whole.astype(jnp.float32) + attn_sum).astype(jnp.bfloat16)
    resid_share = lax.dynamic_slice_in_dim(resid_full, device * width, width, 1)
    expert_in = normed(resid_full, expert_gain).astype(jnp.bfloat16)
    logits = jnp.dot(expert_in, router_weight, preferred_element_type=jnp.float32)
    chosen = jnp.take_along_axis(logits, expert_ids, axis=1)
    lifted = jax.nn.sigmoid(chosen)
    shares = lifted / jnp.sum(lifted, axis=1, keepdims=True)
    own_expert = device * held_units // FF
    row_weight = jnp.sum(jnp.where(expert_ids == own_expert, shares, 0.0), axis=1)
    gate = jnp.dot(expert_in, gate_full, preferred_element_type=jnp.float32)
    upper = jnp.dot(expert_in, up_full, preferred_element_type=jnp.float32)
    hidden = (jax.nn.silu(gate) * upper).astype(jnp.bfloat16)
    expert_part = contract_last(hidden, down_full) * row_weight[:, None]
    expert_share = lax.psum_scatter(expert_part, "ep", scatter_dimension=1, tiled=True)
    return (resid_share.astype(jnp.float32) + expert_share).astype(jnp.bfloat16)


def solution(mesh):
    placed = (
        P("grp", "ep"),
        P("grp", "ep"),
        P("grp", "ep"),
        P("grp", "ep"),
        P("grp", "ep"),
        P("grp", "ep"),
        P("grp", "ep"),
        P("grp", "ep"),
        P(),
        P(),
        P(),
        P("ep"),
        P("grp", "ep", None, None),
        P("grp", None),
        P("grp"),
        P(),
    )
    return jax.shard_map(
        shards, mesh=mesh, in_specs=placed, out_specs=P("grp", "ep"), check_vma=False
    )
```

profile of v0, /device:TPU:2, one launch (start us, length us, event | category | flops | bytes accessed | tf_op | source)
XLA Modules:
  0.0 1156.8 jit_solution(16587274960861065871)
XLA Ops:
  8.0 2.2 gather_fusion
  15.6 90.3 %all-gather = bf16[64,96,32]{1,2,0:T(8,128)(2,1)S(1)} all-gather(bf16[1,96,32]{1,2,0:T(8,128)(2,1)S(1)} %bitcast.57), channel_id=1, replica_groups=mesh['grp'=8,'ep'=64] {'ep'}, dimensions={0}, use_global_device_ids=true | all-gather | bytes 399360 | tf_op jit(solution)/shard_map/all_gather | solution.py:43
  107.0 1.8 reshape.87
  110.6 2.1 convert_element_type.37
  112.7 2.3 scatter_fusion
  115.0 3.2 broadcast_select_fusion
  118.2 2.3 gather_fusion.1
  120.5 26.3 %all-gather.9.cloned.1.call-done = bf16[6144,128]{1,0:T(8,128)(2,1)} async-done(((bf16[768,128]{1,0:T(8,128)(2,1)}), bf16[6144,128]{1,0:T(8,128)(2,1)}) %all-gather.9.cloned.1.call-update) | async-done | bytes 1572880 | tf_op jit(solution)/shard_map/all_gather | solution.py:46
  146.8 1.9 divide_multiply_fusion.2
  148.7 45.6 %all-gather.13.cloned.1.call-done = bf16[6144,128]{1,0:T(8,128)(2,1)} async-done(((bf16[768,128]{1,0:T(8,128)(2,1)}), bf16[6144,128]{1,0:T(8,128)(2,1)}) %all-gather.13.cloned.1.call-update) | async-done | bytes 1572880 | tf_op jit(solution)/shard_map/all_gather | solution.py:48
  194.2 1.9 divide_multiply_fusion
  196.2 45.4 %all-gather.11.cloned.1.call-done = bf16[6144,128]{1,0:T(8,128)(2,1)} async-done(((bf16[768,128]{1,0:T(8,128)(2,1)}), bf16[6144,128]{1,0:T(8,128)(2,1)}) %all-gather.11.cloned.1.call-update) | async-done | bytes 1572880 | tf_op jit(solution)/shard_map/all_gather | solution.py:47
  241.6 1.9 divide_multiply_fusion.1
  243.5 2.1 fusion
  245.7 43.2 %all-gather.15.cloned.1.call-done = bf16[6144,128]{1,0:T(8,128)(2,1)} async-done(((bf16[768,128]{1,0:T(8,128)(2,1)}), bf16[6144,128]{1,0:T(8,128)(2,1)}) %all-gather.15.cloned.1.call-update) | async-done | bytes 1572880 | tf_op jit(solution)/shard_map/all_gather | solution.py:49
  288.9 3.0 fusion.21
  294.4 535.5 %all-reduce.5.cloned.1.call-done = f32[32,6144]{1,0:T(8,128)} async-done(((f32[32,6144]{1,0:T(8,128)}), f32[32,6144]{1,0:T(8,128)}) %all-reduce.5.cloned.1.call-update) | async-done | bytes 786448 | tf_op jit(solution)/shard_map/psum | solution.py:72
  832.6 45.9 %all-gather.17.cloned.1.call-done = bf16[6144,288]{0,1:T(8,128)(2,1)} async-done(((bf16[768,288]{0,1:T(8,128)(2,1)}), bf16[6144,288]{0,1:T(8,128)(2,1)}) %all-gather.17.cloned.1.call-update) | async-done | bytes 3538960 | tf_op jit(solution)/shard_map/all_gather | solution.py:50
  878.5 3.1 fusion.32
  881.7 50.3 %all-gather.19.cloned.1.call-done = bf16[6144,288]{0,1:T(8,128)(2,1)} async-done(((bf16[768,288]{0,1:T(8,128)(2,1)}), bf16[6144,288]{0,1:T(8,128)(2,1)}) %all-gather.19.cloned.1.call-update) | async-done | bytes 3538960 | tf_op jit(solution)/shard_map/all_gather | solution.py:51
  931.9 53.4 %all-gather.21.cloned.1.call-done = bf16[6144,288]{0,1:T(8,128)(2,1)} async-done(((bf16[768,288]{0,1:T(8,128)(2,1)}), bf16[6144,288]{0,1:T(8,128)(2,1)}) %all-gather.21.cloned.1.call-update) | async-done | bytes 3538960 | tf_op jit(solution)/shard_map/all_gather | solution.py:52
  985.3 5.8 convolution_multiply_fusion
  991.1 2.2 copy.70
  993.4 155.0 %reduce-scatter.4.cloned.1.call-done = f32[96,32]{1,0:T(8,128)} async-done(((f32[6144,32]{1,0:T(8,128)}), f32[96,32]{1,0:T(8,128)}) %reduce-scatter.4.cloned.1.call-update) | async-done | bytes 12304
  (59 shorter events, 15.8 us)
Async XLA Ops:
  6.5 824.7 %copy-start = (bf16[6144,32]{0,1:T(8,128)(2,1)S(1)}, bf16[6144,32]{0,1:T(8,128)(2,1)}, u32[]{:S(2)}) copy-start(bf16[6144,32]{0,1:T(8,128)(2,1)} %param.24) | copy-start | bytes 1179652
  6.5 104.1 %all-reduce.3.cloned.1.call-start = ((), (), s32[]{:S(2)}) async-start(), calls=%async_computation.2 | async-start | bytes 1048576 | tf_op jit(solution)/shard_map/psum | solution.py:62
  11.2 135.5 %all-gather.9.cloned.1.call-start = ((), (), s32[]{:S(2)}) async-start(), calls=%async_computation.1 | async-start | bytes 1769472 | tf_op jit(solution)/shard_map/all_gather | solution.py:46
  12.0 182.3 %all-gather.13.cloned.1.call-start = ((), (), s32[]{:S(2)}) async-start(), calls=%async_computation.4 | async-start | bytes 1769472 | tf_op jit(solution)/shard_map/all_gather | solution.py:48
  12.7 228.8 %all-gather.11.cloned.1.call-start = ((), (), s32[]{:S(2)}) async-start(), calls=%async_computation.3 | async-start | bytes 1769472 | tf_op jit(solution)/shard_map/all_gather | solution.py:47
  13.3 275.6 %all-gather.15.cloned.1.call-start = ((), (), s32[]{:S(2)}) async-start(), calls=%async_computation.5 | async-start | bytes 1769472 | tf_op jit(solution)/shard_map/all_gather | solution.py:49
  13.9 1.7 copy-start.5
  13.9 1.7 copy-start.4
  13.9 815.9 %all-reduce.5.cloned.1.call-start = ((), (), s32[]{:S(2)}) async-start(), calls=%async_computation.6 | async-start | bytes 1572864 | tf_op jit(solution)/shard_map/psum | solution.py:72
  105.8 3.9 copy-start.2
  245.7 48.5 %copy-start.3 = (s32[32,2]{0,1:T(2,128)S(1)}, s32[32,2]{0,1:T(2,128)}, u32[]{:S(2)}) copy-start(s32[32,2]{0,1:T(2,128)} %param.29) | copy-start | bytes 772
  291.8 539.4 %copy-start.1 = (f32[6144]{0:T(1024)S(1)}, f32[6144]{0:T(1024)}, u32[]{:S(2)}) copy-start(f32[6144]{0:T(1024)} %param.26) | copy-start | bytes 73732
  291.9 586.7 %all-gather.17.cloned.1.call-start = ((), (), s32[]{:S(2)}) async-start(), calls=%async_computation.7 | async-start | bytes 3981312 | tf_op jit(solution)/shard_map/all_gather | solution.py:50
  292.6 639.3 %all-gather.19.cloned.1.call-start = ((), (), s32[]{:S(2)}) async-start(), calls=%async_computation.8 | async-start | bytes 3981312 | tf_op jit(solution)/shard_map/all_gather | solution.py:51
  293.4 691.9 %all-gather.21.cloned.1.call-start = ((), (), s32[]{:S(2)}) async-start(), calls=%async_computation.9 | async-start | bytes 3981312 | tf_op jit(solution)/shard_map/all_gather | solution.py:52
  294.1 854.3 %reduce-scatter.4.cloned.1.call-start = ((), (), s32[]{:S(2)}) async-start(), calls=%async_computation.10 | async-start | bytes 3194880
Sparse Core Ops, SparseCore 0:
  11.4 88.2 all-reduce.2
  102.0 44.7 all-gather.8
  149.1 45.1 all-gather.12
  196.4 45.1 all-gather.10
  243.7 45.1 all-gather.14
  292.0 537.8 all-reduce.4
  831.9 46.5 all-gather.16
  880.6 51.2 all-gather.18
  934.0 51.2 all-gather.20
  993.5 154.8 reduce-scatter.3
where the time goes:
time: 1160 us
  waiting for transfers between devices  1010 us (87%)
  blocking collectives  90.3 us (8%)
  matrix products  20 us (2%)
  local copies, waits for them, and re-layouts  15.6 us (1%)
  between operations  14.4 us (1%)
    psum x1, waiting for transfers between devices, shards(): attn_sum = lax.psum(partial_attn, 'ep')  535 us
    unnamed x11, waiting for transfers between devices  160 us
    all_gather x1, blocking collectives, shards(): whole = lax.all_gather(tokens, 'ep', axis=1, tiled=True)  90.3 us
    all_gather x1, waiting for transfers between devices, shards(): lax.all_gather(down_weight, 'grp', axis=0, tiled=True)  53.4 us
    all_gather x1, waiting for transfers between devices, shards(): lax.all_gather(up_weight, 'grp', axis=0, tiled=True)  50.3 us
    all_gather x1, waiting for transfers between devices, shards(): lax.all_gather(gate_weight, 'grp', axis=0, tiled=True)  45.9 us
    all_gather x1, waiting for transfers between devices, shards(): lax.all_gather(value_weight, 'grp', axis=0, tiled=True)  45.6 us
    all_gather x1, waiting for transfers between devices, shards(): lax.all_gather(key_weight, 'grp', axis=0, tiled=True)  45.4 us
  transfers between devices with their start and end apart: 10, of which 9 were waited for; matrix products, arithmetic and copies ran while one was open for 3% of the time, Pallas kernels for 0%

commit v1 on v0

v1 whole, which is shorter than its diff:
```python
import jax
import jax.numpy as jnp
from jax import lax
from jax.experimental import pallas as pl
from jax.experimental.pallas import tpu as pltpu
from jax.sharding import PartitionSpec as P

BF16, F32 = jnp.bfloat16, jnp.float32
GRP = ("yl", "x")
EPA = ("yh", "zh", "zl", "c")
CHIPS = ("yh", "zh", "zl")
PLANE = ("yl", "x", "yh", "zh")
SWAP = [(g * 8 + h, h * 8 + g) for g in range(8) for h in range(8)]
CORES = [(0, 1), (1, 0)]
D, FF, DH = 6144, 9216, 128
EPS = 1e-6
CHUNK, SLICE, SLOTS, MIG, UNITS = 96, 768, 32, 16, 288
VMEM = pl.BlockSpec(memory_space=pltpu.VMEM)
SMEM = pl.BlockSpec(memory_space=pltpu.SMEM)


def call(kernel, outs, ins, name, smem=(), limit=48 << 20):
    specs = [SMEM if i in smem else VMEM for i in range(len(ins))]
    return pl.pallas_call(
        kernel,
        out_shape=outs,
        in_specs=specs,
        out_specs=jax.tree.map(lambda _: VMEM, outs),
        compiler_params=pltpu.CompilerParams(vmem_limit_bytes=limit),
        name=name,
    )(*ins)


def shape(dims, dtype):
    return jax.ShapeDtypeStruct(dims, dtype)


def dot_nt(left, right):
    return lax.dot_general(left, right, (((1,), (1,)), ((), ())), preferred_element_type=F32)


def silu(x):
    return x * (1.0 / (1.0 + jnp.exp(-x)))


def sort_kernel(tokens_ref, slot_row_ref, out_ref):
    place = lax.broadcasted_iota(jnp.int32, (SLOTS, SLOTS), 0) == slot_row_ref[...]
    out_ref[...] = jnp.dot(
        place.astype(F32).astype(BF16), tokens_ref[...], preferred_element_type=F32
    ).astype(BF16)


def features(own_ref, other_ref, gain_ref, where_ref):
    group, core = where_ref[0], where_ref[1]
    for pair in range(4):
        for ref, side in ((own_ref, core), (other_ref, 1 - core)):
            chunk = 2 * pair + side
            x = ref[:, pair].reshape(8 * SLOTS, CHUNK).astype(F32)
            scaled = (x * gain_ref[pl.ds(group * 8 + chunk, 1), :]).astype(BF16)
            yield pl.multiple_of(chunk * CHUNK, 32), scaled, jnp.sum(x * x, axis=1, keepdims=True)


def stats_lanes(total, lane):
    high = total.astype(BF16).astype(F32)
    at = lax.broadcasted_iota(jnp.int32, (total.shape[0], 128), 1)
    return jnp.where(at == lane, high, jnp.where(at == lane + 1, total - high, 0.0))


def qkv_kernel(own_ref, other_ref, q_ref, k_ref, v_ref, gain_ref, target_ref, where_ref, out_ref):
    q = k = v = total = 0.0
    for at, scaled, squares in features(own_ref, other_ref, gain_ref, where_ref):
        rows = pl.ds(at, CHUNK)
        q += jnp.dot(scaled, q_ref[rows, :], preferred_element_type=F32)
        k += jnp.dot(scaled, k_ref[rows, :], preferred_element_type=F32)
        v += jnp.dot(scaled, v_ref[rows, :], preferred_element_type=F32)
        total += squares
    pick = lax.broadcasted_iota(jnp.int32, (MIG, SLOTS), 1) == target_ref[...]
    pick = pick.astype(F32).astype(BF16)
    for i, part in enumerate((q, k, v, stats_lanes(total, 0))):
        part = part.astype(BF16)
        lanes = slice(128 * i, 128 * i + 128)
        out_ref[:, :SLOTS, lanes] = part.reshape(8, SLOTS, 128)
        moved = jnp.dot(pick, part[7 * SLOTS :], preferred_element_type=F32).astype(BF16)
        for d in range(8):
            out_ref[d, SLOTS:, lanes] = moved


def attention_kernel(got_ref, states_ref, source_ref, decay_ref, migration_ref, where_ref, out_ref, o_ref):
    total = got_ref[0].astype(F32)
    for i in range(1, 8):
        total += got_ref[i].astype(F32)
    squares = total[:, 384:385] + total[:, 385:386]
    scale = lax.rsqrt(squares * (1.0 / D) + EPS)
    q, k, v = (silu(scale * total[:, 128 * i : 128 * i + 128]) for i in range(3))
    rows = SLOTS + MIG
    turned = jnp.concatenate([q, jnp.zeros((128 - rows, 128), F32)], axis=0).T
    for s in range(SLOTS):
        o_ref[s : s + 1, :] = jnp.sum(turned[:, s : s + 1] * states_ref[s], axis=0, keepdims=True)
    for m in range(MIG):
        s = SLOTS + m
        o_ref[s : s + 1, :] = jnp.sum(
            turned[:, s : s + 1] * states_ref[migration_ref[m, 1]], axis=0, keepdims=True
        )
    retain = jnp.exp(-decay_ref[...])
    mixed = retain * o_ref[...] + jnp.sum(q * k, axis=1, keepdims=True) * v
    heads = mixed * lax.rsqrt(jnp.mean(mixed * mixed, axis=1, keepdims=True) + EPS)
    here = source_ref[...] == where_ref[0]
    own = heads[:SLOTS].astype(BF16)
    moved = jnp.where(here, heads[SLOTS:], 0.0).astype(BF16)
    for d in range(8):
        out_ref[d, :SLOTS] = own
        out_ref[d, SLOTS:] = moved


def output_kernel(got_ref, weight_ref, target_ref, where_ref, keep_ref, send_ref):
    core = where_ref[1]
    moved = got_ref[0, SLOTS:].astype(F32)
    for i in range(1, 8):
        moved += got_ref[i, SLOTS:].astype(F32)
    place = lax.broadcasted_iota(jnp.int32, (SLOTS, MIG), 0) == target_ref[...]
    place = place.astype(F32)
    landed = jnp.dot(place.astype(BF16), moved.astype(BF16), preferred_element_type=F32)
    taken = jnp.sum(place, axis=1, keepdims=True) > 0.0
    last = jnp.where(taken, landed, got_ref[7, :SLOTS].astype(F32)).astype(BF16)
    rows = jnp.concatenate([got_ref[:7, :SLOTS].reshape(7 * SLOTS, DH), last], axis=0)
    for pair in range(4):
        for ref, side in ((keep_ref, core), (send_ref, 1 - core)):
            at = pl.multiple_of((2 * pair + side) * CHUNK, 32)
            part = dot_nt(rows, weight_ref[pl.ds(at, CHUNK), :])
            ref[:, pair] = part.reshape(8, SLOTS, CHUNK).astype(ref.dtype)


def resid_kernel(got_ref, tokens_ref, resid_ref, spread_ref):
    total = got_ref[0].astype(F32)
    for i in range(1, 32):
        total += got_ref[i].astype(F32)
    resid = (tokens_ref[...].astype(F32) + total).astype(BF16)
    resid_ref[...] = resid
    for i in range(32):
        spread_ref[i] = resid


def gate_kernel(own_ref, other_ref, gate_ref, up_ref, tail_ref, gain_ref, where_ref, out_ref):
    gate = up = tail = total = 0.0
    for at, scaled, squares in features(own_ref, other_ref, gain_ref, where_ref):
        rows = pl.ds(at, CHUNK)
        gate += jnp.dot(scaled, gate_ref[rows, :256], preferred_element_type=F32)
        up += jnp.dot(scaled, up_ref[rows, :256], preferred_element_type=F32)
        tail += jnp.dot(scaled, tail_ref[rows, :], preferred_element_type=F32)
        total += squares
    tail += stats_lanes(total, 96)
    out_ref[:, :, :256] = gate.astype(BF16).reshape(8, SLOTS, 256)
    out_ref[:, :, 256:512] = up.astype(BF16).reshape(8, SLOTS, 256)
    out_ref[:, :, 512:] = tail.astype(BF16).reshape(8, SLOTS, 128)


def expert_kernel(got_ref, down_ref, ids_ref, slot_row_ref, where_ref, keep_ref, send_ref):
    core, expert = where_ref[1], where_ref[2]
    total = got_ref[0].astype(F32)
    for i in range(1, 8):
        total += got_ref[i].astype(F32)
    tail = total[:, 512:]
    scale = lax.rsqrt((tail[:, 96:97] + tail[:, 97:98]) * (1.0 / D) + EPS)
    main = (silu(scale * total[:, :256]) * (scale * total[:, 256:512])).astype(BF16)
    rest = (silu(scale * tail[:, :32]) * (scale * tail[:, 32:64])).astype(BF16)
    logits = scale * tail[:, 64:96]
    place = lax.broadcasted_iota(jnp.int32, (SLOTS, SLOTS), 0) == slot_row_ref[...]
    ids = jnp.dot(
        place.astype(F32).astype(BF16), ids_ref[...].astype(F32).astype(BF16), preferred_element_type=F32
    )
    ids = (ids + 0.5).astype(jnp.int32)
    at = lax.broadcasted_iota(jnp.int32, (SLOTS, 32), 1)
    lifted = []
    for i in range(2):
        chosen = jnp.sum(jnp.where(at == ids[:, i : i + 1], logits, 0.0), axis=1, keepdims=True)
        lifted.append(1.0 / (1.0 + jnp.exp(-chosen)))
    mine = jnp.where(ids[:, 0:1] == expert, lifted[0], 0.0)
    mine += jnp.where(ids[:, 1:2] == expert, lifted[1], 0.0)
    share = mine / (lifted[0] + lifted[1])
    hidden = jnp.concatenate([main, rest], axis=1)
    for chip in range(32):
        for ref, side in ((keep_ref, core), (send_ref, 1 - core)):
            row = pl.multiple_of((2 * chip + side) * CHUNK, 32)
            part = dot_nt(hidden, down_ref[pl.ds(row, CHUNK), :])
            ref[chip] = (part * share).astype(ref.dtype)


def final_kernel(got_ref, resid_ref, slot_ref, out_ref):
    total = got_ref[0].astype(F32)
    for i in range(1, 32):
        total += got_ref[i].astype(F32)
    out = (resid_ref[...].astype(F32) + total).astype(BF16)
    place = lax.broadcasted_iota(jnp.int32, (SLOTS, SLOTS), 1) == slot_ref[...]
    out_ref[...] = jnp.dot(
        place.astype(F32).astype(BF16), out, preferred_element_type=F32
    ).astype(BF16)


def exchange(x, axes):
    return lax.all_to_all(x, axes, 0, 0)


def shards(
    tokens,
    query_weight,
    key_weight,
    value_weight,
    output_weight,
    gate_weight,
    up_weight,
    down_weight,
    router_weight,
    attn_gain,
    expert_gain,
    decay_rate,
    states,
    expert_ids,
    row_slot,
    migration,
):
    group = lax.axis_index(GRP).astype(jnp.int32)
    core = lax.axis_index("c").astype(jnp.int32)
    device = lax.axis_index(EPA).astype(jnp.int32)
    where = jnp.stack([group, core, device * UNITS // FF])
    slot_row, slot_column = row_slot[None, :], row_slot[:, None]

    down_full = lax.all_gather(down_weight, GRP, axis=0, tiled=True)

    ordered = call(sort_kernel, shape((SLOTS, CHUNK), BF16), (tokens, slot_row), "sort_rows")
    block = lax.ppermute(ordered, PLANE, SWAP)

    router = lax.dynamic_slice_in_dim(router_weight, group * SLICE, SLICE, 0)
    tail = jnp.concatenate(
        [gate_weight[:, 256:], up_weight[:, 256:], router, jnp.zeros((SLICE, 32), BF16)], axis=1
    )
    attn_gain, expert_gain = attn_gain.reshape(64, CHUNK), expert_gain.reshape(64, CHUNK)

    def gather(spread):
        own = exchange(spread, CHIPS)
        other = lax.ppermute(own, "c", CORES)
        return own.reshape(8, 4, SLOTS, CHUNK), other.reshape(8, 4, SLOTS, CHUNK)

    def scatter(keep, send):
        got = lax.ppermute(send, "c", CORES)
        both = (keep + got.astype(F32)).astype(BF16)
        return exchange(both.reshape(32, SLOTS, CHUNK), CHIPS)

    own, other = gather(jnp.broadcast_to(block[None], (32, SLOTS, CHUNK)))
    parts = call(
        qkv_kernel,
        shape((8, SLOTS + MIG, 512), BF16),
        (own, other, query_weight, key_weight, value_weight, attn_gain, migration[:, 2:3], where),
        "qkv_parts",
        smem=(7,),
    )
    parts = exchange(parts, GRP)
    heads = pl.pallas_call(
        attention_kernel,
        out_shape=shape((8, SLOTS + MIG, DH), BF16),
        in_specs=[VMEM, VMEM, VMEM, VMEM, SMEM, SMEM],
        out_specs=VMEM,
        scratch_shapes=[pltpu.VMEM((SLOTS + MIG, DH), F32)],
        compiler_params=pltpu.CompilerParams(vmem_limit_bytes=48 << 20),
        name="attention",
    )(parts, states[:, 0], migration[:, 0:1], decay_rate[None], migration, where)
    heads = exchange(heads, GRP)
    keep, send = call(
        output_kernel,
        (shape((8, 4, SLOTS, CHUNK), F32), shape((8, 4, SLOTS, CHUNK), BF16)),
        (heads, output_weight, migration[:, 2][None, :], where),
        "output_parts",
        smem=(3,),
    )
    resid, spread = call(
        resid_kernel,
        (shape((SLOTS, CHUNK), BF16), shape((32, SLOTS, CHUNK), BF16)),
        (scatter(keep, send), block),
        "resid",
    )
    own, other = gather(spread)
    resid = lax.ppermute(resid, PLANE, SWAP)
    parts = call(
        gate_kernel,
        shape((8, SLOTS, 640), BF16),
        (own, other, gate_weight, up_weight, tail, expert_gain, where),
        "gate_parts",
        smem=(6,),
    )
    parts = exchange(parts, GRP)
    keep, send = call(
        expert_kernel,
        (shape((32, SLOTS, CHUNK), F32), shape((32, SLOTS, CHUNK), BF16)),
        (parts, down_full, expert_ids, slot_row, where),
        "expert_parts",
        smem=(4,),
    )
    return call(
        final_kernel,
        shape((SLOTS, CHUNK), BF16),
        (scatter(keep, send), resid, slot_column),
        "layer_out",
    )


def solution(mesh):
    fine = jax.sharding.Mesh(
        mesh.devices.reshape(2, 4, 4, 2, 4, 2), ("yl", "x", "yh", "zh", "zl", "c")
    )
    both = P(GRP, EPA)
    placed = (both,) * 8 + (
        P(),
        P(),
        P(),
        P(EPA),
        P(GRP, EPA, None, None),
        P(GRP, None),
        P(GRP),
        P(),
    )
    return jax.shard_map(shards, mesh=fine, in_specs=placed, out_specs=both, check_vma=False)
```

time: 1160 us -> 192 us (0.17)
  the two profiles are of different devices: /device:TPU:2 before, /device:TPU:10 now
where the time goes in v1:
time: 192 us; the launch traced here: 191 us
  starting transfers between devices  70.1 us (37%)
  waiting for transfers between devices  50.6 us (26%)
  blocking collectives  30.5 us (16%)
  between operations  14.3 us (7%)
  local copies, waits for them, and re-layouts  13.4 us (7%)
  Pallas kernels  11.2 us (6%)
    all_to_all x5, waiting for transfers between devices, exchange(): return lax.all_to_all(x, axes, 0, 0)  39 us
    all_to_all x5, starting transfers between devices, exchange(): return lax.all_to_all(x, axes, 0, 0)  34.5 us
    all_to_all x2, blocking collectives, exchange(): return lax.all_to_all(x, axes, 0, 0)  30.5 us
    ppermute x1, starting transfers between devices, shards(): block = lax.ppermute(ordered, PLANE, SWAP)  15.1 us
    ppermute x1, starting transfers between devices, shards(): resid = lax.ppermute(resid, PLANE, SWAP)  12.7 us
    unnamed x32, local copies, waits for them, and re-layouts  11.4 us
    pallas_call x7, Pallas kernels, call(): pl.pallas_call(kernel, out_shape=outs, in_specs=specs, out_specs=jax.tree...  9.23 us
    ppermute x1, waiting for transfers between devices, shards(): resid = lax.ppermute(resid, PLANE, SWAP)  4.31 us
  transfers between devices with their start and end apart: 12, of which 10 were waited for; matrix products, arithmetic and copies ran while one was open for 3% of the time, Pallas kernels for 4%

profile of v1, /device:TPU:10, one launch (start us, length us, event | category | flops | bytes accessed | tf_op | source)
XLA Modules:
  0.0 191.1 jit_solution(1167296217489121801)
XLA Ops:
  6.5 2.2 %copy.36 = bf16[768,288]{1,0:T(8,128)(2,1)} copy(bf16[768,288]{0,1:T(8,128)(2,1)} %param.23) | data formatting | bytes 884736 | tf_op args[7]
  10.3 15.1 %collective-permute-start = (bf16[32,96]{1,0:T(8,128)(2,1)S(1)}, bf16[32,96]{1,0:T(8,128)(2,1)S(1)}, u32[]{:S(2)}, u32[]{:S(2)}) collective-permute-start(bf16[32,96]{1,0:T(8,128)(2,1)S(1)} %sort_rows.1), channel_id=1, source_target_pairs={{0,0},{8,64},{16,128},{24,192},{32,256},{40,320},{48,384},{56,448}... | collective-permute-start | bytes 18440 | tf_op jit(solution)/shard_map/ppermute | solution.py:230
  27.8 6.0 %all-to-all-start = ((bf16[32,32,96]{2,1,0:T(8,128)(2,1)}), bf16[32,32,96]{2,1,0:T(8,128)(2,1)S(1)}, u32[]{:S(2)}, u32[]{:S(2)}) async-start(bf16[32,32,96]{2,1,0:T(8,128)(2,1)} %broadcast_in_dim.19), calls=%async_computation | async-start | bytes 524288 | tf_op jit(solution)/shard_map/all_to_all | solution.py:200
  35.5 11.5 %all-to-all-done = bf16[32,32,96]{2,1,0:T(8,128)(2,1)S(1)} async-done(((bf16[32,32,96]{2,1,0:T(8,128)(2,1)}), bf16[32,32,96]{2,1,0:T(8,128)(2,1)S(1)}, u32[]{:S(2)}, u32[]{:S(2)}) %all-to-all-start) | async-done | bytes 196640 | tf_op jit(solution)/shard_map/all_to_all | solution.py:200
  46.9 1.9 collective-permute-start.1
  53.1 2.0 %qkv_parts.1 = bf16[8,48,512]{2,1,0:T(8,128)(2,1)} custom-call(bf16[8,4,32,96]{3,2,1,0:T(8,128)(2,1)S(1)} %bitcast.16, bf16[8,4,32,96]{3,2,1,0:T(8,128)(2,1)S(1)} %bitcast.18, bf16[768,128]{1,0:T(8,128)(2,1)S(1)} %copy-done.4, bf16[768,128]{1,0:T(8,128)(2,1)S(1)} %copy-done.5, bf16[768,128]{1,0:T(8,128)(2,1)S(1)} %copy-done.6, ...), custom_call_target="tpu_custom_call" | custom-call | tf_op jit(solution)/shard_map/qkv_parts/pallas_call | solution.py:24
  55.2 13.8 %all-to-all-start.1 = ((bf16[8,48,512]{2,1,0:T(8,128)(2,1)}), bf16[8,48,512]{2,1,0:T(8,128)(2,1)S(1)}, u32[]{:S(2)}, u32[]{:S(2)}) async-start(bf16[8,48,512]{2,1,0:T(8,128)(2,1)} %qkv_parts.1), calls=%async_computation.1 | async-start | bytes 786432 | tf_op jit(solution)/shard_map/all_to_all | solution.py:200
  69.6 8.9 %all-to-all-done.1.got_ref = bf16[8,48,512]{2,1,0:T(8,128)(2,1)S(1)} async-done(((bf16[8,48,512]{2,1,0:T(8,128)(2,1)}), bf16[8,48,512]{2,1,0:T(8,128)(2,1)S(1)}, u32[]{:S(2)}, u32[]{:S(2)}) %all-to-all-start.1) | async-done | bytes 393248 | tf_op jit(solution)/shard_map/all_to_all | solution.py:200
  78.6 2.0 %attention.1 = bf16[8,48,128]{2,1,0:T(8,128)(2,1)S(1)} custom-call(bf16[8,48,512]{2,1,0:T(8,128)(2,1)S(1)} %all-to-all-done.1.got_ref, f32[32,128,128]{2,1,0:T(8,128)S(1)} %bitcast.14, s32[16,1]{1,0:T(8,128)S(1)} %get-tuple-element.18.source_ref, f32[1,1]{1,0:T(1,128)} %bitcast.13.decay_ref, s32[16,3]{1,0:T(8,128)S(1)} %copy.28.migration_ref, ...), custom_call_target="tpu_custom_call" | custom-call | tf_op jit(solution)/shard_map/attention/pallas_call | solution.py:257
  80.6 11.0 %all_to_all.35.got_ref = bf16[8,48,128]{2,1,0:T(8,128)(2,1)S(1)} all-to-all(bf16[8,48,128]{2,1,0:T(8,128)(2,1)S(1)} %attention.1), channel_id=1, replica_groups=mesh['yl'=2,'x'=4,'yh'=4,'zh'=2,'zl'=4,'c'=2] {'yl','x'}, dimensions={0} | all-to-all | bytes 196608 | tf_op jit(solution)/shard_map/all_to_all | solution.py:200
  92.5 1.9 %collective-permute-start.2 = (bf16[8,4,32,96]{3,2,1,0:T(8,128)(2,1)S(1)}, bf16[8,4,32,96]{3,2,1,0:T(8,128)(2,1)S(1)}, u32[]{:S(2)}, u32[]{:S(2)}) collective-permute-start(bf16[8,4,32,96]{3,2,1,0:T(8,128)(2,1)S(1)} %get-tuple-element.12), channel_id=1, source_target_pairs={{0,1},{1,0},{2,3},{3,2},{4,5},{5,4},{6,7},{7,6},{8,9},{9,8},{10,11... | collective-permute-start | bytes 589832 | tf_op jit(solution)/shard_map/ppermute | solution.py:244
  96.0 19.5 %all_to_all.36.got_ref = bf16[32,32,96]{2,1,0:T(8,128)(2,1)S(1)} all-to-all(bf16[32,32,96]{2,1,0:T(8,128)(2,1)S(1)} %bitcast.23), channel_id=1, replica_groups=mesh['yl'=2,'x'=4,'yh'=4,'zh'=2,'zl'=4,'c'=2] {'yh','zh','zl'}, dimensions={0} | all-to-all | bytes 393216 | tf_op jit(solution)/shard_map/all_to_all | solution.py:200
  116.3 4.6 %all-to-all-start.4 = ((bf16[32,32,96]{2,1,0:T(8,128)(2,1)}), bf16[32,32,96]{2,1,0:T(8,128)(2,1)S(1)}, u32[]{:S(2)}, u32[]{:S(2)}) async-start(bf16[32,32,96]{2,1,0:T(8,128)(2,1)} %get-tuple-element.13), calls=%async_computation.4 | async-start | bytes 524288 | tf_op jit(solution)/shard_map/all_to_all | solution.py:200
  123.0 12.2 %all-to-all-done.4 = bf16[32,32,96]{2,1,0:T(8,128)(2,1)S(1)} async-done(((bf16[32,32,96]{2,1,0:T(8,128)(2,1)}), bf16[32,32,96]{2,1,0:T(8,128)(2,1)S(1)}, u32[]{:S(2)}, u32[]{:S(2)}) %all-to-all-start.4) | async-done | bytes 196640 | tf_op jit(solution)/shard_map/all_to_all | solution.py:200
  135.1 1.9 collective-permute-start.3
  138.6 2.1 %gate_parts.1 = bf16[8,32,640]{2,1,0:T(8,128)(2,1)} custom-call(bf16[8,4,32,96]{3,2,1,0:T(8,128)(2,1)S(1)} %bitcast.15, bf16[8,4,32,96]{3,2,1,0:T(8,128)(2,1)S(1)} %bitcast.17, bf16[768,288]{1,0:T(8,128)(2,1)S(1)} %copy.34.gate_ref, bf16[768,288]{1,0:T(8,128)(2,1)S(1)} %copy.35.up_ref, bf16[768,128]{1,0:T(8,128)(2,1)S(1)} %maximum_maximum_fusion.tail_ref, ...), custom_call_target="tpu_custom_call" | custom-call | tf_op jit(solution)/shard_map/gate_parts/pallas_call | solution.py:24
  140.7 5.6 %all-to-all-start.5 = ((bf16[8,32,640]{2,1,0:T(8,128)(2,1)}), bf16[8,32,640]{2,1,0:T(8,128)(2,1)S(1)}, u32[]{:S(2)}, u32[]{:S(2)}) async-start(bf16[8,32,640]{2,1,0:T(8,128)(2,1)} %gate_parts.1), calls=%async_computation.5 | async-start | bytes 655360 | tf_op jit(solution)/shard_map/all_to_all | solution.py:200
  146.4 6.4 %all-to-all-done.5.got_ref = bf16[8,32,640]{2,1,0:T(8,128)(2,1)S(1)} async-done(((bf16[8,32,640]{2,1,0:T(8,128)(2,1)}), bf16[8,32,640]{2,1,0:T(8,128)(2,1)S(1)}, u32[]{:S(2)}, u32[]{:S(2)}) %all-to-all-start.5) | async-done | bytes 327712 | tf_op jit(solution)/shard_map/all_to_all | solution.py:200
  152.8 2.3 %copy-done.1 = bf16[6144,288]{1,0:T(8,128)(2,1)S(1)} copy-done((bf16[6144,288]{1,0:T(8,128)(2,1)S(1)}, bf16[6144,288]{1,0:T(8,128)(2,1)}, u32[]{:S(2)}) %copy-start.1) | copy-done | bytes 3538968
  155.1 2.5 %expert_parts.1 = (f32[32,32,96]{2,1,0:T(8,128)S(1)}, bf16[32,32,96]{2,1,0:T(8,128)(2,1)S(1)}) custom-call(bf16[8,32,640]{2,1,0:T(8,128)(2,1)S(1)} %all-to-all-done.5.got_ref, bf16[6144,288]{1,0:T(8,128)(2,1)S(1)} %copy-done.1, s32[32,2]{1,0:T(8,128)S(1)} %copy.37.ids_ref, s32[1,32]{1,0:T(1,128)S(1)} %bitcast.20, s32[3]{0:T(128)S(1)} %pad_add_fusion.where_ref), custom_call_target="tpu_custom_call" | custom-call | tf_op jit(solution)/shard_map/expert_parts/pallas_call | solution.py:24
  157.6 1.9 %collective-permute-start.4 = (bf16[32,32,96]{2,1,0:T(8,128)(2,1)S(1)}, bf16[32,32,96]{2,1,0:T(8,128)(2,1)S(1)}, u32[]{:S(2)}, u32[]{:S(2)}) collective-permute-start(bf16[32,32,96]{2,1,0:T(8,128)(2,1)S(1)} %get-tuple-element.15), channel_id=1, source_target_pairs={{0,1},{1,0},{2,3},{3,2},{4,5},{5,4},{6,7},{7,6},{8,9},{9,8},{10,11... | collective-permute-start | bytes 589832 | tf_op jit(solution)/shard_map/ppermute | solution.py:244
  161.8 4.6 %all-to-all-start.6 = ((bf16[32,32,96]{2,1,0:T(8,128)(2,1)}), bf16[32,32,96]{2,1,0:T(8,128)(2,1)S(1)}, u32[]{:S(2)}, u32[]{:S(2)}) async-start(bf16[32,32,96]{2,1,0:T(8,128)(2,1)} %add_convert_fusion), calls=%async_computation.6 | async-start | bytes 524288 | tf_op jit(solution)/shard_map/all_to_all | solution.py:200
  166.3 12.7 %collective-permute-start.5 = (bf16[32,96]{1,0:T(8,128)(2,1)S(1)}, bf16[32,96]{1,0:T(8,128)(2,1)S(1)}, u32[]{:S(2)}, u32[]{:S(2)}) collective-permute-start(bf16[32,96]{1,0:T(8,128)(2,1)S(1)} %get-tuple-element.16), channel_id=1, source_target_pairs={{0,0},{8,64},{16,128},{24,192},{32,256},{40,320},{48,384},{56,448}... | collective-permute-start | bytes 18440 | tf_op jit(solution)/shard_map/ppermute | solution.py:281
  179.2 4.3 %collective-permute-done.5.resid_ref = bf16[32,96]{1,0:T(8,128)(2,1)S(1)} collective-permute-done((bf16[32,96]{1,0:T(8,128)(2,1)S(1)}, bf16[32,96]{1,0:T(8,128)(2,1)S(1)}, u32[]{:S(2)}, u32[]{:S(2)}) %collective-permute-start.5) | collective-permute-done | bytes 6176 | tf_op jit(solution)/shard_map/ppermute | solution.py:281
  (57 shorter events, 19.8 us)
Async XLA Ops:
  6.5 114.4 %copy-start = (bf16[6144,32]{0,1:T(8,128)(2,1)S(1)}, bf16[6144,32]{0,1:T(8,128)(2,1)}, u32[]{:S(2)}) copy-start(bf16[6144,32]{0,1:T(8,128)(2,1)} %param.24) | copy-start | bytes 1179652
  6.5 72.0 %copy-start.2 = (f32[32,1,128,128]{3,2,1,0:T(8,128)S(1)}, f32[32,1,128,128]{3,2,1,0:T(8,128)}, u32[]{:S(2)}) copy-start(f32[32,1,128,128]{3,2,1,0:T(8,128)} %param.28) | copy-start | bytes 6291460
  6.5 85.0 %copy-start.3 = (bf16[768,128]{1,0:T(8,128)(2,1)S(1)}, bf16[768,128]{1,0:T(8,128)(2,1)}, u32[]{:S(2)}) copy-start(bf16[768,128]{1,0:T(8,128)(2,1)} %weight_ref.1) | copy-start | bytes 589828
  6.5 146.2 %all-gather.2.cloned.1.call-start = ((), (), s32[]{:S(2)}) async-start(), calls=%async_computation.7 | async-start | bytes 5308416 | tf_op jit(solution)/shard_map/all_gather | solution.py:227
  8.8 0.7 copy-start.7
  10.3 16.8 %collective-permute-start = (bf16[32,96]{1,0:T(8,128)(2,1)S(1)}, bf16[32,96]{1,0:T(8,128)(2,1)S(1)}, u32[]{:S(2)}, u32[]{:S(2)}) collective-permute-start(bf16[32,96]{1,0:T(8,128)(2,1)S(1)} %sort_rows.1), channel_id=1, source_target_pairs={{0,0},{8,64},{16,128},{24,192},{32,256},{40,320},{48,384},{56,448}... | collective-permute-start | bytes 18440 | tf_op jit(solution)/shard_map/ppermute | solution.py:230
  27.8 19.1 %all-to-all-start = ((bf16[32,32,96]{2,1,0:T(8,128)(2,1)}), bf16[32,32,96]{2,1,0:T(8,128)(2,1)S(1)}, u32[]{:S(2)}, u32[]{:S(2)}) async-start(bf16[32,32,96]{2,1,0:T(8,128)(2,1)} %broadcast_in_dim.19), calls=%async_computation | async-start | bytes 524288 | tf_op jit(solution)/shard_map/all_to_all | solution.py:200
  46.9 3.4 %collective-permute-start.1 = (bf16[32,32,96]{2,1,0:T(8,128)(2,1)S(1)}, bf16[32,32,96]{2,1,0:T(8,128)(2,1)S(1)}, u32[]{:S(2)}, u32[]{:S(2)}) collective-permute-start(bf16[32,32,96]{2,1,0:T(8,128)(2,1)S(1)} %all-to-all-done), channel_id=1, source_target_pairs={{0,1},{1,0},{2,3},{3,2},{4,5},{5,4},{6,7},{7,6},{8,9},{9,8},{10,11... | collective-permute-start | bytes 589832 | tf_op jit(solution)/shard_map/ppermute | solution.py:240
  50.3 0.9 copy-start.4
  51.3 0.9 copy-start.5
  52.2 0.9 copy-start.6
  53.1 68.0 %copy-start.10 = (bf16[768,288]{0,1:T(8,128)(2,1)S(1)}, bf16[768,288]{0,1:T(8,128)(2,1)}, u32[]{:S(2)}) copy-start(bf16[768,288]{0,1:T(8,128)(2,1)} %param.21) | copy-start | bytes 1327108
  55.2 23.4 %all-to-all-start.1 = ((bf16[8,48,512]{2,1,0:T(8,128)(2,1)}), bf16[8,48,512]{2,1,0:T(8,128)(2,1)S(1)}, u32[]{:S(2)}, u32[]{:S(2)}) async-start(bf16[8,48,512]{2,1,0:T(8,128)(2,1)} %qkv_parts.1), calls=%async_computation.1 | async-start | bytes 786432 | tf_op jit(solution)/shard_map/all_to_all | solution.py:200
  80.6 42.2 %copy-start.11 = (f32[6144]{0:T(1024)S(1)}, f32[6144]{0:T(1024)}, u32[]{:S(2)}) copy-start(f32[6144]{0:T(1024)} %param.26) | copy-start | bytes 73732
  92.5 53.8 %copy-start.12 = (s32[32,2]{0,1:T(2,128)S(1)}, s32[32,2]{0,1:T(2,128)}, u32[]{:S(2)}) copy-start(s32[32,2]{0,1:T(2,128)} %param.29) | copy-start | bytes 772
  92.5 60.3 %copy-start.9 = (s32[32]{0:T(128)S(1)}, s32[32]{0:T(128)}, u32[]{:S(2)}) copy-start(s32[32]{0:T(128)} %param.30) | copy-start | bytes 388
  92.5 3.4 %collective-permute-start.2 = (bf16[8,4,32,96]{3,2,1,0:T(8,128)(2,1)S(1)}, bf16[8,4,32,96]{3,2,1,0:T(8,128)(2,1)S(1)}, u32[]{:S(2)}, u32[]{:S(2)}) collective-permute-start(bf16[8,4,32,96]{3,2,1,0:T(8,128)(2,1)S(1)} %get-tuple-element.12), channel_id=1, source_target_pairs={{0,1},{1,0},{2,3},{3,2},{4,5},{5,4},{6,7},{7,6},{8,9},{9,8},{10,11... | collective-permute-start | bytes 589832 | tf_op jit(solution)/shard_map/ppermute | solution.py:244
  116.3 18.9 %all-to-all-start.4 = ((bf16[32,32,96]{2,1,0:T(8,128)(2,1)}), bf16[32,32,96]{2,1,0:T(8,128)(2,1)S(1)}, u32[]{:S(2)}, u32[]{:S(2)}) async-start(bf16[32,32,96]{2,1,0:T(8,128)(2,1)} %get-tuple-element.13), calls=%async_computation.4 | async-start | bytes 524288 | tf_op jit(solution)/shard_map/all_to_all | solution.py:200
  135.1 3.4 %collective-permute-start.3 = (bf16[32,32,96]{2,1,0:T(8,128)(2,1)S(1)}, bf16[32,32,96]{2,1,0:T(8,128)(2,1)S(1)}, u32[]{:S(2)}, u32[]{:S(2)}) collective-permute-start(bf16[32,32,96]{2,1,0:T(8,128)(2,1)S(1)} %all-to-all-done.4), channel_id=1, source_target_pairs={{0,1},{1,0},{2,3},{3,2},{4,5},{5,4},{6,7},{7,6},{8,9},{9,8},{10,11... | collective-permute-start | bytes 589832 | tf_op jit(solution)/shard_map/ppermute | solution.py:240
  140.7 12.1 %all-to-all-start.5 = ((bf16[8,32,640]{2,1,0:T(8,128)(2,1)}), bf16[8,32,640]{2,1,0:T(8,128)(2,1)S(1)}, u32[]{:S(2)}, u32[]{:S(2)}) async-start(bf16[8,32,640]{2,1,0:T(8,128)(2,1)} %gate_parts.1), calls=%async_computation.5 | async-start | bytes 655360 | tf_op jit(solution)/shard_map/all_to_all | solution.py:200
  152.8 2.3 %copy-start.1 = (bf16[6144,288]{1,0:T(8,128)(2,1)S(1)}, bf16[6144,288]{1,0:T(8,128)(2,1)}, u32[]{:S(2)}) copy-start(bf16[6144,288]{1,0:T(8,128)(2,1)} %all-gather.2.cloned.1.call-done.down_ref) | copy-start | bytes 10616836
  157.6 3.4 %collective-permute-start.4 = (bf16[32,32,96]{2,1,0:T(8,128)(2,1)S(1)}, bf16[32,32,96]{2,1,0:T(8,128)(2,1)S(1)}, u32[]{:S(2)}, u32[]{:S(2)}) collective-permute-start(bf16[32,32,96]{2,1,0:T(8,128)(2,1)S(1)} %get-tuple-element.15), channel_id=1, source_target_pairs={{0,1},{1,0},{2,3},{3,2},{4,5},{5,4},{6,7},{7,6},{8,9},{9,8},{10,11... | collective-permute-start | bytes 589832 | tf_op jit(solution)/shard_map/ppermute | solution.py:244
  161.8 21.7 %all-to-all-start.6 = ((bf16[32,32,96]{2,1,0:T(8,128)(2,1)}), bf16[32,32,96]{2,1,0:T(8,128)(2,1)S(1)}, u32[]{:S(2)}, u32[]{:S(2)}) async-start(bf16[32,32,96]{2,1,0:T(8,128)(2,1)} %add_convert_fusion), calls=%async_computation.6 | async-start | bytes 524288 | tf_op jit(solution)/shard_map/all_to_all | solution.py:200
  166.3 17.1 %collective-permute-start.5 = (bf16[32,96]{1,0:T(8,128)(2,1)S(1)}, bf16[32,96]{1,0:T(8,128)(2,1)S(1)}, u32[]{:S(2)}, u32[]{:S(2)}) collective-permute-start(bf16[32,96]{1,0:T(8,128)(2,1)S(1)} %get-tuple-element.16), channel_id=1, source_target_pairs={{0,0},{8,64},{16,128},{24,192},{32,256},{40,320},{48,384},{56,448}... | collective-permute-start | bytes 18440 | tf_op jit(solution)/shard_map/ppermute | solution.py:281
  (1 other events, 0.7 us)
Sparse Core Ops, SparseCore 0:
  9.4 73.3 all-gather.1

commit v2 on v1

--- a/solution.py
+++ b/solution.py
@@ -9,17 +9,16 @@
 GRP = ("yl", "x")
 EPA = ("yh", "zh", "zl", "c")
 CHIPS = ("yh", "zh", "zl")
-PLANE = ("yl", "x", "yh", "zh")
-SWAP = [(g * 8 + h, h * 8 + g) for g in range(8) for h in range(8)]
 CORES = [(0, 1), (1, 0)]
 D, FF, DH = 6144, 9216, 128
 EPS = 1e-6
 CHUNK, SLICE, SLOTS, MIG, UNITS = 96, 768, 32, 16, 288
 VMEM = pl.BlockSpec(memory_space=pltpu.VMEM)
+HBM = pl.BlockSpec(memory_space=pltpu.HBM)
 SMEM = pl.BlockSpec(memory_space=pltpu.SMEM)
 
 
-def call(kernel, outs, ins, name, smem=(), limit=48 << 20):
+def call(kernel, outs, ins, name, smem=(), limit=16 << 20):
     specs = [SMEM if i in smem else VMEM for i in range(len(ins))]
     return pl.pallas_call(
         kernel,
@@ -43,21 +42,37 @@
     return x * (1.0 / (1.0 + jnp.exp(-x)))
 
 
-def sort_kernel(tokens_ref, slot_row_ref, out_ref):
-    place = lax.broadcasted_iota(jnp.int32, (SLOTS, SLOTS), 0) == slot_row_ref[...]
-    out_ref[...] = jnp.dot(
-        place.astype(F32).astype(BF16), tokens_ref[...], preferred_element_type=F32
+def fetch(pairs, sems):
+    copies = [pltpu.make_async_copy(a, b, sems.at[i]) for i, (a, b) in enumerate(pairs)]
+    for copy in copies:
+        copy.start()
+    return copies
+
+
+def sort_kernel(tokens_ref, slot_ref, out_ref, held_ref, row_ref, sems):
+    for copy in fetch(((tokens_ref, held_ref), (slot_ref, row_ref)), sems):
+        copy.wait()
+    place = lax.broadcasted_iota(jnp.int32, (SLOTS, SLOTS), 0) == row_ref[...]
+    rows = jnp.dot(
+        place.astype(F32).astype(BF16), held_ref[...], preferred_element_type=F32
     ).astype(BF16)
-
-
-def features(own_ref, other_ref, gain_ref, where_ref):
-    group, core = where_ref[0], where_ref[1]
+    for i in range(32):
+        out_ref[i] = rows
+
+
+def slice_rows(own_ref, other_ref, gain_ref, where_ref):
+    group, first = where_ref[0], where_ref[1] == 0
+    pieces = []
     for pair in range(4):
-        for ref, side in ((own_ref, core), (other_ref, 1 - core)):
-            chunk = 2 * pair + side
-            x = ref[:, pair].reshape(8 * SLOTS, CHUNK).astype(F32)
-            scaled = (x * gain_ref[pl.ds(group * 8 + chunk, 1), :]).astype(BF16)
-            yield pl.multiple_of(chunk * CHUNK, 32), scaled, jnp.sum(x * x, axis=1, keepdims=True)
+        own = own_ref[:, pair].reshape(8 * SLOTS, CHUNK).astype(F32)
+        other = other_ref[:, pair].reshape(8 * SLOTS, CHUNK).astype(F32)
+        pieces += [jnp.where(first, own, other), jnp.where(first, other, own)]
+    rows = jnp.concatenate(pieces, axis=1)
+    scaled = [
+        (rows[:, 128 * j : 128 * j + 128] * gain_ref[pl.ds(6 * group + j, 1), :]).astype(BF16)
+        for j in range(6)
+    ]
+    return jnp.concatenate(scaled, axis=1), jnp.sum(rows * rows, axis=1, keepdims=True)
 
 
 def stats_lanes(total, lane):
@@ -66,17 +81,20 @@
     return jnp.where(at == lane, high, jnp.where(at == lane + 1, total - high, 0.0))
 
 
-def qkv_kernel(own_ref, other_ref, q_ref, k_ref, v_ref, gain_ref, target_ref, where_ref, out_ref):
-    q = k = v = total = 0.0
-    for at, scaled, squares in features(own_ref, other_ref, gain_ref, where_ref):
-        rows = pl.ds(at, CHUNK)
-        q += jnp.dot(scaled, q_ref[rows, :], preferred_element_type=F32)
-        k += jnp.dot(scaled, k_ref[rows, :], preferred_element_type=F32)
-        v += jnp.dot(scaled, v_ref[rows, :], preferred_element_type=F32)
-        total += squares
+def qkv_kernel(
+    own_ref, other_ref, q_ref, k_ref, v_ref, gain_ref, target_ref, where_ref, out_ref, scale_ref, held_ref, sems
+):
+    pairs = [(ref, held_ref.at[i]) for i, ref in enumerate((q_ref, k_ref, v_ref))]
+    gain, *copies = fetch([(gain_ref, scale_ref), *pairs], sems)
+    gain.wait()
+    rows, total = slice_rows(own_ref, other_ref, scale_ref, where_ref)
+    parts = []
+    for i, copy in enumerate(copies):
+        copy.wait()
+        parts.append(jnp.dot(rows, held_ref[i], preferred_element_type=F32))
     pick = lax.broadcasted_iota(jnp.int32, (MIG, SLOTS), 1) == target_ref[...]
     pick = pick.astype(F32).astype(BF16)
-    for i, part in enumerate((q, k, v, stats_lanes(total, 0))):
+    for i, part in enumerate((*parts, stats_lanes(total, 0))):
         part = part.astype(BF16)
         lanes = slice(128 * i, 128 * i + 128)
         out_ref[:, :SLOTS, lanes] = part.reshape(8, SLOTS, 128)
@@ -130,36 +148,42 @@
             ref[:, pair] = part.reshape(8, SLOTS, CHUNK).astype(ref.dtype)
 
 
-def resid_kernel(got_ref, tokens_ref, resid_ref, spread_ref):
+def resid_kernel(got_ref, tokens_ref, where_ref, spread_ref):
     total = got_ref[0].astype(F32)
     for i in range(1, 32):
         total += got_ref[i].astype(F32)
-    resid = (tokens_ref[...].astype(F32) + total).astype(BF16)
-    resid_ref[...] = resid
+    tokens = tokens_ref[where_ref[3], where_ref[4]]
+    resid = (tokens.astype(F32) + total).astype(BF16)
     for i in range(32):
         spread_ref[i] = resid
 
 
-def gate_kernel(own_ref, other_ref, gate_ref, up_ref, tail_ref, gain_ref, where_ref, out_ref):
-    gate = up = tail = total = 0.0
-    for at, scaled, squares in features(own_ref, other_ref, gain_ref, where_ref):
-        rows = pl.ds(at, CHUNK)
-        gate += jnp.dot(scaled, gate_ref[rows, :256], preferred_element_type=F32)
-        up += jnp.dot(scaled, up_ref[rows, :256], preferred_element_type=F32)
-        tail += jnp.dot(scaled, tail_ref[rows, :], preferred_element_type=F32)
-        total += squares
-    tail += stats_lanes(total, 96)
+def gate_kernel(own_ref, other_ref, gate_ref, up_ref, router_ref, gain_ref, where_ref, out_ref):
+    rows, total = slice_rows(own_ref, other_ref, gain_ref, where_ref)
+    gate = dot_nt(rows, gate_ref[:256])
+    up = dot_nt(rows, up_ref[:256])
+    at = pl.multiple_of(where_ref[0] * SLICE, SLICE)
+    router = router_ref[:, pl.ds(at, SLICE)]
+    rest = jnp.concatenate([gate_ref[256:], up_ref[256:], router, jnp.zeros_like(router)], axis=0)
+    tail = dot_nt(rows, rest) + stats_lanes(total, 96)
     out_ref[:, :, :256] = gate.astype(BF16).reshape(8, SLOTS, 256)
     out_ref[:, :, 256:512] = up.astype(BF16).reshape(8, SLOTS, 256)
-    out_ref[:, :, 512:] = tail.astype(BF16).reshape(8, SLOTS, 128)
-
-
-def expert_kernel(got_ref, down_ref, ids_ref, slot_row_ref, where_ref, keep_ref, send_ref):
+    out_ref[:, :, 512:640] = tail.astype(BF16).reshape(8, SLOTS, 128)
+    for d in range(8):
+        out_ref[d, :, 640:736] = own_ref[d, where_ref[4]]
+        out_ref[d, :, 736:] = jnp.zeros((SLOTS, 32), BF16)
+
+
+def expert_kernel(
+    got_ref, down_ref, ids_ref, slot_row_ref, where_ref, keep_ref, send_ref, resid_ref, held_ref, sems
+):
     core, expert = where_ref[1], where_ref[2]
+    copies = fetch([(down_ref.at[i], held_ref.at[i]) for i in range(8)], sems)
+    resid_ref[...] = got_ref[where_ref[3], :, 640:736]
     total = got_ref[0].astype(F32)
     for i in range(1, 8):
         total += got_ref[i].astype(F32)
-    tail = total[:, 512:]
+    tail = total[:, 512:640]
     scale = lax.rsqrt((tail[:, 96:97] + tail[:, 97:98]) * (1.0 / D) + EPS)
     main = (silu(scale * total[:, :256]) * (scale * total[:, 256:512])).astype(BF16)
     rest = (silu(scale * tail[:, :32]) * (scale * tail[:, 32:64])).astype(BF16)
@@ -178,11 +202,15 @@
     mine += jnp.where(ids[:, 1:2] == expert, lifted[1], 0.0)
     share = mine / (lifted[0] + lifted[1])
     hidden = jnp.concatenate([main, rest], axis=1)
-    for chip in range(32):
-        for ref, side in ((keep_ref, core), (send_ref, 1 - core)):
-            row = pl.multiple_of((2 * chip + side) * CHUNK, 32)
-            part = dot_nt(hidden, down_ref[pl.ds(row, CHUNK), :])
-            ref[chip] = (part * share).astype(ref.dtype)
+    first = core == 0
+    for i, copy in enumerate(copies):
+        copy.wait()
+        part = jnp.dot(hidden, held_ref[i], preferred_element_type=F32) * share
+        for j in range(4):
+            even = part[:, 192 * j : 192 * j + 96]
+            odd = part[:, 192 * j + 96 : 192 * j + 192]
+            keep_ref[4 * i + j] = jnp.where(first, even, odd)
+            send_ref[4 * i + j] = jnp.where(first, odd, even).astype(BF16)
 
 
 def final_kernel(got_ref, resid_ref, slot_ref, out_ref):
@@ -194,6 +222,10 @@
     out_ref[...] = jnp.dot(
         place.astype(F32).astype(BF16), out, preferred_element_type=F32
     ).astype(BF16)
+
+
+def in_hbm(x):
+    return pltpu.with_memory_space_constraint(x, pltpu.HBM)
 
 
 def exchange(x, axes):
@@ -221,46 +253,63 @@
     group = lax.axis_index(GRP).astype(jnp.int32)
     core = lax.axis_index("c").astype(jnp.int32)
     device = lax.axis_index(EPA).astype(jnp.int32)
-    where = jnp.stack([group, core, device * UNITS // FF])
+    expert = device * UNITS // FF
+    where = jnp.stack([group, core, expert, device // 8, device % 8 // 2])
     slot_row, slot_column = row_slot[None, :], row_slot[:, None]
 
-    down_full = lax.all_gather(down_weight, GRP, axis=0, tiled=True)
-
-    ordered = call(sort_kernel, shape((SLOTS, CHUNK), BF16), (tokens, slot_row), "sort_rows")
-    block = lax.ppermute(ordered, PLANE, SWAP)
-
-    router = lax.dynamic_slice_in_dim(router_weight, group * SLICE, SLICE, 0)
-    tail = jnp.concatenate(
-        [gate_weight[:, 256:], up_weight[:, 256:], router, jnp.zeros((SLICE, 32), BF16)], axis=1
-    )
-    attn_gain, expert_gain = attn_gain.reshape(64, CHUNK), expert_gain.reshape(64, CHUNK)
-
-    def gather(spread):
-        own = exchange(spread, CHIPS)
-        other = lax.ppermute(own, "c", CORES)
-        return own.reshape(8, 4, SLOTS, CHUNK), other.reshape(8, 4, SLOTS, CHUNK)
+    attn_gain, expert_gain = attn_gain.reshape(48, 128), expert_gain.reshape(48, 128)
 
     def scatter(keep, send):
         got = lax.ppermute(send, "c", CORES)
         both = (keep + got.astype(F32)).astype(BF16)
         return exchange(both.reshape(32, SLOTS, CHUNK), CHIPS)
 
-    own, other = gather(jnp.broadcast_to(block[None], (32, SLOTS, CHUNK)))
-    parts = call(
+    spread = pl.pallas_call(
+        sort_kernel,
+        out_shape=shape((32, SLOTS, CHUNK), BF16),
+        in_specs=[HBM, HBM],
+        out_specs=VMEM,
+        scratch_shapes=[
+            pltpu.VMEM((SLOTS, CHUNK), BF16),
+            pltpu.VMEM((1, SLOTS), jnp.int32),
+            pltpu.SemaphoreType.DMA((2,)),
+        ],
+        name="sorted_rows",
+    )(in_hbm(tokens), in_hbm(slot_row))
+    own = exchange(exchange(spread, CHIPS).reshape(8, 4, SLOTS, CHUNK), GRP)
+    rows_own, other = own, lax.ppermute(own, "c", CORES)
+    parts = pl.pallas_call(
         qkv_kernel,
-        shape((8, SLOTS + MIG, 512), BF16),
-        (own, other, query_weight, key_weight, value_weight, attn_gain, migration[:, 2:3], where),
-        "qkv_parts",
-        smem=(7,),
+        out_shape=shape((8, SLOTS + MIG, 512), BF16),
+        in_specs=[VMEM, VMEM, HBM, HBM, HBM, HBM, VMEM, SMEM],
+        out_specs=VMEM,
+        scratch_shapes=[
+            pltpu.VMEM((48, 128), F32),
+            pltpu.VMEM((3, SLICE, DH), BF16),
+            pltpu.SemaphoreType.DMA((4,)),
+        ],
+        compiler_params=pltpu.CompilerParams(vmem_limit_bytes=16 << 20),
+        name="qkv_parts",
+    )(
+        own,
+        other,
+        in_hbm(query_weight),
+        in_hbm(key_weight),
+        in_hbm(value_weight),
+        in_hbm(attn_gain),
+        migration[:, 2:3],
+        where,
     )
     parts = exchange(parts, GRP)
+    parts, down = lax.optimization_barrier((parts, down_weight.T))
+    down_full = lax.all_gather(down, GRP)
     heads = pl.pallas_call(
         attention_kernel,
         out_shape=shape((8, SLOTS + MIG, DH), BF16),
         in_specs=[VMEM, VMEM, VMEM, VMEM, SMEM, SMEM],
         out_specs=VMEM,
         scratch_shapes=[pltpu.VMEM((SLOTS + MIG, DH), F32)],
-        compiler_params=pltpu.CompilerParams(vmem_limit_bytes=48 << 20),
+        compiler_params=pltpu.CompilerParams(vmem_limit_bytes=16 << 20),
         name="attention",
     )(parts, states[:, 0], migration[:, 0:1], decay_rate[None], migration, where)
     heads = exchange(heads, GRP)
@@ -271,29 +320,36 @@
         "output_parts",
         smem=(3,),
     )
-    resid, spread = call(
+    spread = call(
         resid_kernel,
-        (shape((SLOTS, CHUNK), BF16), shape((32, SLOTS, CHUNK), BF16)),
-        (scatter(keep, send), block),
+        shape((32, SLOTS, CHUNK), BF16),
+        (scatter(keep, send), rows_own, where),
         "resid",
-    )
-    own, other = gather(spread)
-    resid = lax.ppermute(resid, PLANE, SWAP)
+        smem=(2,),
+    )
+    own = exchange(spread, CHIPS).reshape(8, 4, SLOTS, CHUNK)
+    other = lax.ppermute(own, "c", CORES)
     parts = call(
         gate_kernel,
-        shape((8, SLOTS, 640), BF16),
-        (own, other, gate_weight, up_weight, tail, expert_gain, where),
+        shape((8, SLOTS, 768), BF16),
+        (own, other, gate_weight.T, up_weight.T, router_weight.T, expert_gain, where),
         "gate_parts",
         smem=(6,),
     )
     parts = exchange(parts, GRP)
-    keep, send = call(
+    keep, send, resid = pl.pallas_call(
         expert_kernel,
-        (shape((32, SLOTS, CHUNK), F32), shape((32, SLOTS, CHUNK), BF16)),
-        (parts, down_full, expert_ids, slot_row, where),
-        "expert_parts",
-        smem=(4,),
-    )
+        out_shape=(
+            shape((32, SLOTS, CHUNK), F32),
+            shape((32, SLOTS, CHUNK), BF16),
+            shape((SLOTS, CHUNK), BF16),
+        ),
+        in_specs=[VMEM, HBM, VMEM, VMEM, SMEM],
+        out_specs=(VMEM, VMEM, VMEM),
+        scratch_shapes=[pltpu.VMEM((8, UNITS, SLICE), BF16), pltpu.SemaphoreType.DMA((8,))],
+        compiler_params=pltpu.CompilerParams(vmem_limit_bytes=24 << 20),
+        name="expert_parts",
+    )(parts, in_hbm(down_full), expert_ids, slot_row, where)
     return call(
         final_kernel,
         shape((SLOTS, CHUNK), BF16),

time: 192 us -> 189 us (0.984)
  the two profiles are of different devices: /device:TPU:10 before, /device:TPU:8 now
where the time goes in v2:
time: 189 us; the launch traced here: 188 us
  blocking collectives  101 us (53%)
  waiting for transfers between devices  33.2 us (18%)
  starting transfers between devices  21.9 us (12%)
  Pallas kernels  15.1 us (8%)
  between operations  14.3 us (8%)
    all_to_all x5, blocking collectives, exchange(): return lax.all_to_all(x, axes, 0, 0)  101 us
    all_to_all x3, waiting for transfers between devices, exchange(): return lax.all_to_all(x, axes, 0, 0)  27.3 us
    all_to_all x3, starting transfers between devices, exchange(): return lax.all_to_all(x, axes, 0, 0)  14.3 us
    pallas_call x1, Pallas kernels, shards(): pl.pallas_call(expert_kernel, out_shape=(shape((32, SLOTS, CHUNK), F32),...  4.55 us
    pallas_call x4, Pallas kernels, call(): pl.pallas_call(kernel, out_shape=outs, in_specs=specs, out_specs=jax.tree...  4.18 us
    ppermute x2, starting transfers between devices, scatter(): got = lax.ppermute(send, 'c', CORES)  3.84 us
  transfers between devices with their start and end apart: 8, of which 7 were waited for; matrix products, arithmetic and copies ran while one was open for 1% of the time, Pallas kernels for 3%

profile of v2, /device:TPU:8, one launch (start us, length us, event | category | flops | bytes accessed | tf_op | source)
XLA Modules:
  0.0 188.0 jit_solution(393777420002528279)
XLA Ops:
  6.5 1.7 sorted_rows.1
  8.3 29.2 %all_to_all.40 = bf16[32,32,96]{2,1,0:T(8,128)(2,1)} all-to-all(bf16[32,32,96]{2,1,0:T(8,128)(2,1)} %sorted_rows.1), channel_id=1, replica_groups=mesh['yl'=2,'x'=4,'yh'=4,'zh'=2,'zl'=4,'c'=2] {'yh','zh','zl'}, dimensions={0} | all-to-all | bytes 393216 | tf_op jit(solution)/shard_map/all_to_all | solution.py:232
  37.4 5.9 %all-to-all-start.1 = ((bf16[8,4,32,96]{3,2,1,0:T(8,128)(2,1)}), bf16[8,4,32,96]{3,2,1,0:T(8,128)(2,1)S(1)}, u32[]{:S(2)}, u32[]{:S(2)}) async-start(bf16[8,4,32,96]{3,2,1,0:T(8,128)(2,1)} %bitcast.1), calls=%async_computation.1 | async-start | bytes 524288 | tf_op jit(solution)/shard_map/all_to_all | solution.py:232
  44.2 5.0 %all-to-all-done.1.own_ref.tokens_ref = bf16[8,4,32,96]{3,2,1,0:T(8,128)(2,1)S(1)} async-done(((bf16[8,4,32,96]{3,2,1,0:T(8,128)(2,1)}), bf16[8,4,32,96]{3,2,1,0:T(8,128)(2,1)S(1)}, u32[]{:S(2)}, u32[]{:S(2)}) %all-to-all-start.1) | async-done | bytes 196640 | tf_op jit(solution)/shard_map/all_to_all | solution.py:232
  49.1 1.9 %collective-permute-start = (bf16[8,4,32,96]{3,2,1,0:T(8,128)(2,1)S(1)}, bf16[8,4,32,96]{3,2,1,0:T(8,128)(2,1)S(1)}, u32[]{:S(2)}, u32[]{:S(2)}) collective-permute-start(bf16[8,4,32,96]{3,2,1,0:T(8,128)(2,1)S(1)} %all-to-all-done.1.own_ref.tokens_ref), channel_id=1, source_target_pairs={{0,1},{1,0},{2,3},{3,2},{4,5},{5,4},{6,7},{7,6},{8,9},{9,8},{10,11... | collective-permute-start | bytes 589832 | tf_op jit(solution)/shard_map/ppermute | solution.py:280
  51.2 1.3 collective-permute-done.other_ref
  52.6 2.7 %qkv_parts.1 = bf16[8,48,512]{2,1,0:T(8,128)(2,1)S(1)} custom-call(bf16[8,4,32,96]{3,2,1,0:T(8,128)(2,1)S(1)} %all-to-all-done.1.own_ref.tokens_ref, bf16[8,4,32,96]{3,2,1,0:T(8,128)(2,1)S(1)} %collective-permute-done.other_ref, bf16[768,128]{1,0:T(8,128)(2,1)} %q_ref.1, bf16[768,128]{1,0:T(8,128)(2,1)} %k_ref.1, bf16[768,128]{1,0:T(8,128)(2,1)} %v_ref.1, ...), custom_call_target="tpu_custom_call" | custom-call | tf_op jit(solution)/shard_map/qkv_parts/pallas_call | solution.py:281
  55.3 11.8 %all_to_all.41.got_ref = bf16[8,48,512]{2,1,0:T(8,128)(2,1)S(1)} all-to-all(bf16[8,48,512]{2,1,0:T(8,128)(2,1)S(1)} %qkv_parts.1), channel_id=1, replica_groups=mesh['yl'=2,'x'=4,'yh'=4,'zh'=2,'zl'=4,'c'=2] {'yl','x'}, dimensions={0} | all-to-all | bytes 786432 | tf_op jit(solution)/shard_map/all_to_all | solution.py:232
  67.9 2.0 %attention.1 = bf16[8,48,128]{2,1,0:T(8,128)(2,1)S(1)} custom-call(bf16[8,48,512]{2,1,0:T(8,128)(2,1)S(1)} %all_to_all.41.got_ref, f32[32,128,128]{2,1,0:T(8,128)S(1)} %bitcast.21, s32[16,1]{1,0:T(8,128)S(1)} %get-tuple-element.20.source_ref, f32[1,1]{1,0:T(1,128)} %bitcast.20.decay_ref, s32[16,3]{1,0:T(8,128)S(1)} %copy.22.migration_ref, s32[5]{0:T(128)S(1)} %stack.23.where_ref), custom_call_target="tpu_custom_call" | custom-call | tf_op jit(solution)/shard_map/attention/pallas_call | solution.py:306
  69.9 20.7 %all_to_all.42.got_ref = bf16[8,48,128]{2,1,0:T(8,128)(2,1)S(1)} all-to-all(bf16[8,48,128]{2,1,0:T(8,128)(2,1)S(1)} %attention.1), channel_id=1, replica_groups=mesh['yl'=2,'x'=4,'yh'=4,'zh'=2,'zl'=4,'c'=2] {'yl','x'}, dimensions={0} | all-to-all | bytes 196608 | tf_op jit(solution)/shard_map/all_to_all | solution.py:232
  91.5 1.9 %collective-permute-start.1 = (bf16[8,4,32,96]{3,2,1,0:T(8,128)(2,1)S(1)}, bf16[8,4,32,96]{3,2,1,0:T(8,128)(2,1)S(1)}, u32[]{:S(2)}, u32[]{:S(2)}) collective-permute-start(bf16[8,4,32,96]{3,2,1,0:T(8,128)(2,1)S(1)} %get-tuple-element.14), channel_id=1, source_target_pairs={{0,1},{1,0},{2,3},{3,2},{4,5},{5,4},{6,7},{7,6},{8,9},{9,8},{10,11... | collective-permute-start | bytes 589832 | tf_op jit(solution)/shard_map/ppermute | solution.py:263
  93.4 1.5 collective-permute-done.1
  95.0 20.1 %all_to_all.43.got_ref = bf16[32,32,96]{2,1,0:T(8,128)(2,1)S(1)} all-to-all(bf16[32,32,96]{2,1,0:T(8,128)(2,1)S(1)} %bitcast.33), channel_id=1, replica_groups=mesh['yl'=2,'x'=4,'yh'=4,'zh'=2,'zl'=4,'c'=2] {'yh','zh','zl'}, dimensions={0} | all-to-all | bytes 393216 | tf_op jit(solution)/shard_map/all_to_all | solution.py:232
  115.7 19.7 %all_to_all.44 = bf16[32,32,96]{2,1,0:T(8,128)(2,1)S(1)} all-to-all(bf16[32,32,96]{2,1,0:T(8,128)(2,1)S(1)} %resid.1), channel_id=1, replica_groups=mesh['yl'=2,'x'=4,'yh'=4,'zh'=2,'zl'=4,'c'=2] {'yh','zh','zl'}, dimensions={0} | all-to-all | bytes 393216 | tf_op jit(solution)/shard_map/all_to_all | solution.py:232
  135.4 1.9 %collective-permute-start.2 = (bf16[8,4,32,96]{3,2,1,0:T(8,128)(2,1)S(1)}, bf16[8,4,32,96]{3,2,1,0:T(8,128)(2,1)S(1)}, u32[]{:S(2)}, u32[]{:S(2)}) collective-permute-start(bf16[8,4,32,96]{3,2,1,0:T(8,128)(2,1)S(1)} %bitcast.22), channel_id=1, source_target_pairs={{0,1},{1,0},{2,3},{3,2},{4,5},{5,4},{6,7},{7,6},{8,9},{9,8},{10,11... | collective-permute-start | bytes 589832 | tf_op jit(solution)/shard_map/ppermute | solution.py:331
  137.3 1.5 collective-permute-done.2.other_ref
  138.8 1.9 gate_parts.1
  140.7 4.2 %all-to-all-start.6 = ((bf16[8,32,768]{2,1,0:T(8,128)(2,1)}), bf16[8,32,768]{2,1,0:T(8,128)(2,1)S(1)}, u32[]{:S(2)}, u32[]{:S(2)}) async-start(bf16[8,32,768]{2,1,0:T(8,128)(2,1)} %gate_parts.1), calls=%async_computation.6 | async-start | bytes 786432 | tf_op jit(solution)/shard_map/all_to_all | solution.py:232
  145.0 7.7 %all-to-all-done.6.got_ref = bf16[8,32,768]{2,1,0:T(8,128)(2,1)S(1)} async-done(((bf16[8,32,768]{2,1,0:T(8,128)(2,1)}), bf16[8,32,768]{2,1,0:T(8,128)(2,1)S(1)}, u32[]{:S(2)}, u32[]{:S(2)}) %all-to-all-start.6) | async-done | bytes 393248 | tf_op jit(solution)/shard_map/all_to_all | solution.py:232
  152.8 4.6 %expert_parts.1 = (f32[32,32,96]{2,1,0:T(8,128)S(1)}, bf16[32,32,96]{2,1,0:T(8,128)(2,1)S(1)}, bf16[32,96]{1,0:T(8,128)(2,1)S(1)}) custom-call(bf16[8,32,768]{2,1,0:T(8,128)(2,1)S(1)} %all-to-all-done.6.got_ref, bf16[8,288,768]{2,1,0:T(8,128)(2,1)} %bitcast.32, s32[32,2]{1,0:T(8,128)S(1)} %copy.25.ids_ref, s32[1,32]{1,0:T(1,128)S(1)} %bitcast.29, ...), custom_call_target="tpu_custom_call" | custom-call | tf_op jit(solution)/shard_map/expert_parts/pallas_call | solution.py:340
  157.3 1.9 %collective-permute-start.3 = (bf16[32,32,96]{2,1,0:T(8,128)(2,1)S(1)}, bf16[32,32,96]{2,1,0:T(8,128)(2,1)S(1)}, u32[]{:S(2)}, u32[]{:S(2)}) collective-permute-start(bf16[32,32,96]{2,1,0:T(8,128)(2,1)S(1)} %get-tuple-element.17), channel_id=1, source_target_pairs={{0,1},{1,0},{2,3},{3,2},{4,5},{5,4},{6,7},{7,6},{8,9},{9,8},{10,11... | collective-permute-start | bytes 589832 | tf_op jit(solution)/shard_map/ppermute | solution.py:263
  159.3 1.5 collective-permute-done.3
  161.5 4.1 %all-to-all-start.7 = ((bf16[32,32,96]{2,1,0:T(8,128)(2,1)}), bf16[32,32,96]{2,1,0:T(8,128)(2,1)S(1)}, u32[]{:S(2)}, u32[]{:S(2)}) async-start(bf16[32,32,96]{2,1,0:T(8,128)(2,1)} %add_convert_fusion), calls=%async_computation.7 | async-start | bytes 524288 | tf_op jit(solution)/shard_map/all_to_all | solution.py:232
  165.7 14.6 %all-to-all-done.7.got_ref = bf16[32,32,96]{2,1,0:T(8,128)(2,1)S(1)} async-done(((bf16[32,32,96]{2,1,0:T(8,128)(2,1)}), bf16[32,32,96]{2,1,0:T(8,128)(2,1)S(1)}, u32[]{:S(2)}, u32[]{:S(2)}) %all-to-all-start.7) | async-done | bytes 196640 | tf_op jit(solution)/shard_map/all_to_all | solution.py:232
  (29 shorter events, 4.4 us)
Async XLA Ops:
  6.5 61.3 %copy-start = (f32[32,1,128,128]{3,2,1,0:T(8,128)S(1)}, f32[32,1,128,128]{3,2,1,0:T(8,128)}, u32[]{:S(2)}) copy-start(f32[32,1,128,128]{3,2,1,0:T(8,128)} %param.28) | copy-start | bytes 6291460
  6.5 84.1 %copy-start.4 = (bf16[768,128]{1,0:T(8,128)(2,1)S(1)}, bf16[768,128]{1,0:T(8,128)(2,1)}, u32[]{:S(2)}) copy-start(bf16[768,128]{1,0:T(8,128)(2,1)} %weight_ref.1) | copy-start | bytes 589828
  37.4 11.7 %all-to-all-start.1 = ((bf16[8,4,32,96]{3,2,1,0:T(8,128)(2,1)}), bf16[8,4,32,96]{3,2,1,0:T(8,128)(2,1)S(1)}, u32[]{:S(2)}, u32[]{:S(2)}) async-start(bf16[8,4,32,96]{3,2,1,0:T(8,128)(2,1)} %bitcast.1), calls=%async_computation.1 | async-start | bytes 524288 | tf_op jit(solution)/shard_map/all_to_all | solution.py:232
  43.3 109.4 %all-gather.3.cloned.1.call-start = ((), (), s32[]{:S(2)}) async-start(), calls=%async_computation.8 | async-start | bytes 3981312 | tf_op jit(solution)/shard_map/all_gather | solution.py:305
  49.1 3.4 %collective-permute-start = (bf16[8,4,32,96]{3,2,1,0:T(8,128)(2,1)S(1)}, bf16[8,4,32,96]{3,2,1,0:T(8,128)(2,1)S(1)}, u32[]{:S(2)}, u32[]{:S(2)}) collective-permute-start(bf16[8,4,32,96]{3,2,1,0:T(8,128)(2,1)S(1)} %all-to-all-done.1.own_ref.tokens_ref), channel_id=1, source_target_pairs={{0,1},{1,0},{2,3},{3,2},{4,5},{5,4},{6,7},{7,6},{8,9},{9,8},{10,11... | collective-permute-start | bytes 589832 | tf_op jit(solution)/shard_map/ppermute | solution.py:280
  55.2 83.6 %copy-start.1 = (bf16[768,288]{0,1:T(8,128)(2,1)S(1)}, bf16[768,288]{0,1:T(8,128)(2,1)}, u32[]{:S(2)}) copy-start(bf16[768,288]{0,1:T(8,128)(2,1)} %param.21) | copy-start | bytes 1327108
  55.2 83.6 %copy-start.5 = (f32[6144]{0:T(1024)S(1)}, f32[6144]{0:T(1024)}, u32[]{:S(2)}) copy-start(f32[6144]{0:T(1024)} %param.26) | copy-start | bytes 73732
  67.1 71.7 %copy-start.2 = (bf16[768,288]{0,1:T(8,128)(2,1)S(1)}, bf16[768,288]{0,1:T(8,128)(2,1)}, u32[]{:S(2)}) copy-start(bf16[768,288]{0,1:T(8,128)(2,1)} %param.22) | copy-start | bytes 1327108
  67.1 71.7 %copy-start.3 = (bf16[6144,32]{0,1:T(8,128)(2,1)S(1)}, bf16[6144,32]{0,1:T(8,128)(2,1)}, u32[]{:S(2)}) copy-start(bf16[6144,32]{0,1:T(8,128)(2,1)} %param.24) | copy-start | bytes 1179652
  69.9 75.1 %copy-start.7 = (s32[32,2]{0,1:T(2,128)S(1)}, s32[32,2]{0,1:T(2,128)}, u32[]{:S(2)}) copy-start(s32[32,2]{0,1:T(2,128)} %param.29) | copy-start | bytes 772
  69.9 82.9 %copy-start.6 = (s32[32]{0:T(128)S(1)}, s32[32]{0:T(128)}, u32[]{:S(2)}) copy-start(s32[32]{0:T(128)} %param.30) | copy-start | bytes 388
  91.5 3.4 %collective-permute-start.1 = (bf16[8,4,32,96]{3,2,1,0:T(8,128)(2,1)S(1)}, bf16[8,4,32,96]{3,2,1,0:T(8,128)(2,1)S(1)}, u32[]{:S(2)}, u32[]{:S(2)}) collective-permute-start(bf16[8,4,32,96]{3,2,1,0:T(8,128)(2,1)S(1)} %get-tuple-element.14), channel_id=1, source_target_pairs={{0,1},{1,0},{2,3},{3,2},{4,5},{5,4},{6,7},{7,6},{8,9},{9,8},{10,11... | collective-permute-start | bytes 589832 | tf_op jit(solution)/shard_map/ppermute | solution.py:263
  135.4 3.4 %collective-permute-start.2 = (bf16[8,4,32,96]{3,2,1,0:T(8,128)(2,1)S(1)}, bf16[8,4,32,96]{3,2,1,0:T(8,128)(2,1)S(1)}, u32[]{:S(2)}, u32[]{:S(2)}) collective-permute-start(bf16[8,4,32,96]{3,2,1,0:T(8,128)(2,1)S(1)} %bitcast.22), channel_id=1, source_target_pairs={{0,1},{1,0},{2,3},{3,2},{4,5},{5,4},{6,7},{7,6},{8,9},{9,8},{10,11... | collective-permute-start | bytes 589832 | tf_op jit(solution)/shard_map/ppermute | solution.py:331
  140.7 12.0 %all-to-all-start.6 = ((bf16[8,32,768]{2,1,0:T(8,128)(2,1)}), bf16[8,32,768]{2,1,0:T(8,128)(2,1)S(1)}, u32[]{:S(2)}, u32[]{:S(2)}) async-start(bf16[8,32,768]{2,1,0:T(8,128)(2,1)} %gate_parts.1), calls=%async_computation.6 | async-start | bytes 786432 | tf_op jit(solution)/shard_map/all_to_all | solution.py:232
  157.3 3.4 %collective-permute-start.3 = (bf16[32,32,96]{2,1,0:T(8,128)(2,1)S(1)}, bf16[32,32,96]{2,1,0:T(8,128)(2,1)S(1)}, u32[]{:S(2)}, u32[]{:S(2)}) collective-permute-start(bf16[32,32,96]{2,1,0:T(8,128)(2,1)S(1)} %get-tuple-element.17), channel_id=1, source_target_pairs={{0,1},{1,0},{2,3},{3,2},{4,5},{5,4},{6,7},{7,6},{8,9},{9,8},{10,11... | collective-permute-start | bytes 589832 | tf_op jit(solution)/shard_map/ppermute | solution.py:263
  161.5 18.8 %all-to-all-start.7 = ((bf16[32,32,96]{2,1,0:T(8,128)(2,1)}), bf16[32,32,96]{2,1,0:T(8,128)(2,1)S(1)}, u32[]{:S(2)}, u32[]{:S(2)}) async-start(bf16[32,32,96]{2,1,0:T(8,128)(2,1)} %add_convert_fusion), calls=%async_computation.7 | async-start | bytes 524288 | tf_op jit(solution)/shard_map/all_to_all | solution.py:232
Sparse Core Ops, SparseCore 0:
  67.2 57.2 all-gather.2

commit v3 on v2

--- a/solution.py
+++ b/solution.py
@@ -174,19 +174,16 @@
         out_ref[d, :, 736:] = jnp.zeros((SLOTS, 32), BF16)
 
 
-def expert_kernel(
-    got_ref, down_ref, ids_ref, slot_row_ref, where_ref, keep_ref, send_ref, resid_ref, held_ref, sems
-):
-    core, expert = where_ref[1], where_ref[2]
-    copies = fetch([(down_ref.at[i], held_ref.at[i]) for i in range(8)], sems)
+def hidden_kernel(got_ref, ids_ref, slot_row_ref, where_ref, out_ref, resid_ref):
+    expert = where_ref[2]
     resid_ref[...] = got_ref[where_ref[3], :, 640:736]
     total = got_ref[0].astype(F32)
     for i in range(1, 8):
         total += got_ref[i].astype(F32)
     tail = total[:, 512:640]
     scale = lax.rsqrt((tail[:, 96:97] + tail[:, 97:98]) * (1.0 / D) + EPS)
-    main = (silu(scale * total[:, :256]) * (scale * total[:, 256:512])).astype(BF16)
-    rest = (silu(scale * tail[:, :32]) * (scale * tail[:, 32:64])).astype(BF16)
+    main = silu(scale * total[:, :256]) * (scale * total[:, 256:512])
+    rest = silu(scale * tail[:, :32]) * (scale * tail[:, 32:64])
     logits = scale * tail[:, 64:96]
     place = lax.broadcasted_iota(jnp.int32, (SLOTS, SLOTS), 0) == slot_row_ref[...]
     ids = jnp.dot(
@@ -201,16 +198,22 @@
     mine = jnp.where(ids[:, 0:1] == expert, lifted[0], 0.0)
     mine += jnp.where(ids[:, 1:2] == expert, lifted[1], 0.0)
     share = mine / (lifted[0] + lifted[1])
-    hidden = jnp.concatenate([main, rest], axis=1)
-    first = core == 0
-    for i, copy in enumerate(copies):
-        copy.wait()
-        part = jnp.dot(hidden, held_ref[i], preferred_element_type=F32) * share
-        for j in range(4):
-            even = part[:, 192 * j : 192 * j + 96]
-            odd = part[:, 192 * j + 96 : 192 * j + 192]
-            keep_ref[4 * i + j] = jnp.where(first, even, odd)
-            send_ref[4 * i + j] = jnp.where(first, odd, even).astype(BF16)
+    main, rest = (main * share).astype(BF16), (rest * share).astype(BF16)
+    for d in range(8):
+        out_ref[d, :, :256] = main
+        out_ref[d, :, 256:] = rest
+
+
+def down_kernel(got_ref, down_ref, where_ref, keep_ref, send_ref):
+    first = where_ref[1] == 0
+    part = jnp.dot(
+        got_ref[...].reshape(8 * SLOTS, UNITS), down_ref[...], preferred_element_type=F32
+    )
+    for pair in range(4):
+        even = part[:, 192 * pair : 192 * pair + 96]
+        odd = part[:, 192 * pair + 96 : 192 * pair + 192]
+        keep_ref[:, pair] = jnp.where(first, even, odd).reshape(8, SLOTS, CHUNK)
+        send_ref[:, pair] = jnp.where(first, odd, even).astype(BF16).reshape(8, SLOTS, CHUNK)
 
 
 def final_kernel(got_ref, resid_ref, slot_ref, out_ref):
@@ -259,10 +262,8 @@
 
     attn_gain, expert_gain = attn_gain.reshape(48, 128), expert_gain.reshape(48, 128)
 
-    def scatter(keep, send):
-        got = lax.ppermute(send, "c", CORES)
-        both = (keep + got.astype(F32)).astype(BF16)
-        return exchange(both.reshape(32, SLOTS, CHUNK), CHIPS)
+    def merge(keep, send):
+        return (keep + lax.ppermute(send, "c", CORES).astype(F32)).astype(BF16)
 
     spread = pl.pallas_call(
         sort_kernel,
@@ -301,8 +302,6 @@
         where,
     )
     parts = exchange(parts, GRP)
-    parts, down = lax.optimization_barrier((parts, down_weight.T))
-    down_full = lax.all_gather(down, GRP)
     heads = pl.pallas_call(
         attention_kernel,
         out_shape=shape((8, SLOTS + MIG, DH), BF16),
@@ -323,7 +322,11 @@
     spread = call(
         resid_kernel,
         shape((32, SLOTS, CHUNK), BF16),
-        (scatter(keep, send), rows_own, where),
+        (
+            exchange(merge(keep, send).reshape(32, SLOTS, CHUNK), CHIPS),
+            rows_own,
+            where,
+        ),
         "resid",
         smem=(2,),
     )
@@ -337,23 +340,27 @@
         smem=(6,),
     )
     parts = exchange(parts, GRP)
-    keep, send, resid = pl.pallas_call(
-        expert_kernel,
-        out_shape=(
-            shape((32, SLOTS, CHUNK), F32),
-            shape((32, SLOTS, CHUNK), BF16),
-            shape((SLOTS, CHUNK), BF16),
-        ),
-        in_specs=[VMEM, HBM, VMEM, VMEM, SMEM],
-        out_specs=(VMEM, VMEM, VMEM),
-        scratch_shapes=[pltpu.VMEM((8, UNITS, SLICE), BF16), pltpu.SemaphoreType.DMA((8,))],
-        compiler_params=pltpu.CompilerParams(vmem_limit_bytes=24 << 20),
-        name="expert_parts",
-    )(parts, in_hbm(down_full), expert_ids, slot_row, where)
+    hidden, resid = call(
+        hidden_kernel,
+        (shape((8, SLOTS, UNITS), BF16), shape((SLOTS, CHUNK), BF16)),
+        (parts, expert_ids, slot_row, where),
+        "hidden",
+        smem=(3,),
+    )
+    hidden = exchange(hidden, GRP)
+    keep, send = call(
+        down_kernel,
+        (shape((8, 4, SLOTS, CHUNK), F32), shape((8, 4, SLOTS, CHUNK), BF16)),
+        (hidden, down_weight.T, where),
+        "down_parts",
+        smem=(2,),
+    )
+    parts = exchange(merge(keep, send), GRP)
+    parts = exchange(parts.reshape(32, SLOTS, CHUNK), CHIPS)
     return call(
         final_kernel,
         shape((SLOTS, CHUNK), BF16),
-        (scatter(keep, send), resid, slot_column),
+        (parts, resid, slot_column),
         "layer_out",
     )
 

time: 189 us -> 181 us (0.958)
  the two profiles are of different devices: /device:TPU:8 before, /device:TPU:10 now
where the time goes in v3:
time: 181 us; the launch traced here: 180 us
  blocking collectives  96.4 us (53%)
  waiting for transfers between devices  38.4 us (21%)
  starting transfers between devices  29.5 us (16%)
  Pallas kernels  13.7 us (8%)
    all_to_all x6, blocking collectives, exchange(): return lax.all_to_all(x, axes, 0, 0)  96.4 us
    all_to_all x4, waiting for transfers between devices, exchange(): return lax.all_to_all(x, axes, 0, 0)  32.6 us
    all_to_all x4, starting transfers between devices, exchange(): return lax.all_to_all(x, axes, 0, 0)  21.9 us
    pallas_call x6, Pallas kernels, call(): pl.pallas_call(kernel, out_shape=outs, in_specs=specs, out_specs=jax.tree...  6.62 us
    ppermute x2, starting transfers between devices, merge(): return (keep + lax.ppermute(send, 'c', CORES).astype(F32)).astype(BF16)  3.84 us
  transfers between devices with their start and end apart: 8, of which 8 were waited for; matrix products, arithmetic and copies ran while one was open for 1% of the time, Pallas kernels for 0%

profile of v3, /device:TPU:10, one launch (start us, length us, event | category | flops | bytes accessed | tf_op | source)
XLA Modules:
  0.0 180.2 jit_solution(4337409161227454471)
XLA Ops:
  0.0 1.7 sorted_rows.1
  1.7 29.2 %all_to_all.50 = bf16[32,32,96]{2,1,0:T(8,128)(2,1)} all-to-all(bf16[32,32,96]{2,1,0:T(8,128)(2,1)} %sorted_rows.1), channel_id=1, replica_groups=mesh['yl'=2,'x'=4,'yh'=4,'zh'=2,'zl'=4,'c'=2] {'yh','zh','zl'}, dimensions={0} | all-to-all | bytes 393216 | tf_op jit(solution)/shard_map/all_to_all | solution.py:235
  30.9 5.9 %all-to-all-start.1 = ((bf16[8,4,32,96]{3,2,1,0:T(8,128)(2,1)}), bf16[8,4,32,96]{3,2,1,0:T(8,128)(2,1)S(1)}, u32[]{:S(2)}, u32[]{:S(2)}) async-start(bf16[8,4,32,96]{3,2,1,0:T(8,128)(2,1)} %bitcast.1), calls=%async_computation.1 | async-start | bytes 524288 | tf_op jit(solution)/shard_map/all_to_all | solution.py:235
  37.6 4.4 %all-to-all-done.1.own_ref.tokens_ref = bf16[8,4,32,96]{3,2,1,0:T(8,128)(2,1)S(1)} async-done(((bf16[8,4,32,96]{3,2,1,0:T(8,128)(2,1)}), bf16[8,4,32,96]{3,2,1,0:T(8,128)(2,1)S(1)}, u32[]{:S(2)}, u32[]{:S(2)}) %all-to-all-start.1) | async-done | bytes 196640 | tf_op jit(solution)/shard_map/all_to_all | solution.py:235
  42.0 1.9 %collective-permute-start = (bf16[8,4,32,96]{3,2,1,0:T(8,128)(2,1)S(1)}, bf16[8,4,32,96]{3,2,1,0:T(8,128)(2,1)S(1)}, u32[]{:S(2)}, u32[]{:S(2)}) collective-permute-start(bf16[8,4,32,96]{3,2,1,0:T(8,128)(2,1)S(1)} %all-to-all-done.1.own_ref.tokens_ref), channel_id=1, source_target_pairs={{0,1},{1,0},{2,3},{3,2},{4,5},{5,4},{6,7},{7,6},{8,9},{9,8},{10,11... | collective-permute-start | bytes 589832 | tf_op jit(solution)/shard_map/ppermute | solution.py:281
  45.4 3.4 %qkv_parts.1 = bf16[8,48,512]{2,1,0:T(8,128)(2,1)} custom-call(bf16[8,4,32,96]{3,2,1,0:T(8,128)(2,1)S(1)} %all-to-all-done.1.own_ref.tokens_ref, bf16[8,4,32,96]{3,2,1,0:T(8,128)(2,1)S(1)} %collective-permute-done.other_ref, bf16[768,128]{1,0:T(8,128)(2,1)} %q_ref.1, bf16[768,128]{1,0:T(8,128)(2,1)} %k_ref.1, bf16[768,128]{1,0:T(8,128)(2,1)} %v_ref.1, ...), custom_call_target="tpu_custom_call" | custom-call | tf_op jit(solution)/shard_map/qkv_parts/pallas_call | solution.py:282
  48.8 5.5 %all-to-all-start.2 = ((bf16[8,48,512]{2,1,0:T(8,128)(2,1)}), bf16[8,48,512]{2,1,0:T(8,128)(2,1)S(1)}, u32[]{:S(2)}, u32[]{:S(2)}) async-start(bf16[8,48,512]{2,1,0:T(8,128)(2,1)} %qkv_parts.1), calls=%async_computation.2 | async-start | bytes 786432 | tf_op jit(solution)/shard_map/all_to_all | solution.py:235
  55.0 6.5 %all-to-all-done.2.got_ref = bf16[8,48,512]{2,1,0:T(8,128)(2,1)S(1)} async-done(((bf16[8,48,512]{2,1,0:T(8,128)(2,1)}), bf16[8,48,512]{2,1,0:T(8,128)(2,1)S(1)}, u32[]{:S(2)}, u32[]{:S(2)}) %all-to-all-start.2) | async-done | bytes 393248 | tf_op jit(solution)/shard_map/all_to_all | solution.py:235
  61.5 2.0 %attention.1 = bf16[8,48,128]{2,1,0:T(8,128)(2,1)S(1)} custom-call(bf16[8,48,512]{2,1,0:T(8,128)(2,1)S(1)} %all-to-all-done.2.got_ref, f32[32,128,128]{2,1,0:T(8,128)S(1)} %bitcast.21, s32[16,1]{1,0:T(8,128)S(1)} %get-tuple-element.18.source_ref, f32[1,1]{1,0:T(1,128)} %bitcast.20.decay_ref, s32[16,3]{1,0:T(8,128)S(1)} %copy.22.migration_ref, ...), custom_call_target="tpu_custom_call" | custom-call | tf_op jit(solution)/shard_map/attention/pallas_call | solution.py:305
  63.6 9.1 %all_to_all.51.got_ref = bf16[8,48,128]{2,1,0:T(8,128)(2,1)S(1)} all-to-all(bf16[8,48,128]{2,1,0:T(8,128)(2,1)S(1)} %attention.1), channel_id=1, replica_groups=mesh['yl'=2,'x'=4,'yh'=4,'zh'=2,'zl'=4,'c'=2] {'yl','x'}, dimensions={0} | all-to-all | bytes 196608 | tf_op jit(solution)/shard_map/all_to_all | solution.py:235
  73.6 1.9 %collective-permute-start.1 = (bf16[8,4,32,96]{3,2,1,0:T(8,128)(2,1)S(1)}, bf16[8,4,32,96]{3,2,1,0:T(8,128)(2,1)S(1)}, u32[]{:S(2)}, u32[]{:S(2)}) collective-permute-start(bf16[8,4,32,96]{3,2,1,0:T(8,128)(2,1)S(1)} %get-tuple-element.12), channel_id=1, source_target_pairs={{0,1},{1,0},{2,3},{3,2},{4,5},{5,4},{6,7},{7,6},{8,9},{9,8},{10,11... | collective-permute-start | bytes 589832 | tf_op jit(solution)/shard_map/ppermute | solution.py:266
  75.5 1.5 collective-permute-done.1
  77.1 18.9 %all_to_all.52.got_ref = bf16[32,32,96]{2,1,0:T(8,128)(2,1)S(1)} all-to-all(bf16[32,32,96]{2,1,0:T(8,128)(2,1)S(1)} %bitcast.33), channel_id=1, replica_groups=mesh['yl'=2,'x'=4,'yh'=4,'zh'=2,'zl'=4,'c'=2] {'yh','zh','zl'}, dimensions={0} | all-to-all | bytes 393216 | tf_op jit(solution)/shard_map/all_to_all | solution.py:235
  96.7 18.8 %all_to_all.53 = bf16[32,32,96]{2,1,0:T(8,128)(2,1)S(1)} all-to-all(bf16[32,32,96]{2,1,0:T(8,128)(2,1)S(1)} %resid.1), channel_id=1, replica_groups=mesh['yl'=2,'x'=4,'yh'=4,'zh'=2,'zl'=4,'c'=2] {'yh','zh','zl'}, dimensions={0} | all-to-all | bytes 393216 | tf_op jit(solution)/shard_map/all_to_all | solution.py:235
  115.5 1.9 %collective-permute-start.2 = (bf16[8,4,32,96]{3,2,1,0:T(8,128)(2,1)S(1)}, bf16[8,4,32,96]{3,2,1,0:T(8,128)(2,1)S(1)}, u32[]{:S(2)}, u32[]{:S(2)}) collective-permute-start(bf16[8,4,32,96]{3,2,1,0:T(8,128)(2,1)S(1)} %bitcast.22), channel_id=1, source_target_pairs={{0,1},{1,0},{2,3},{3,2},{4,5},{5,4},{6,7},{7,6},{8,9},{9,8},{10,11... | collective-permute-start | bytes 589832 | tf_op jit(solution)/shard_map/ppermute | solution.py:334
  117.4 1.5 collective-permute-done.2.other_ref
  118.9 1.9 %gate_parts.1 = bf16[8,32,768]{2,1,0:T(8,128)(2,1)} custom-call(bf16[8,4,32,96]{3,2,1,0:T(8,128)(2,1)S(1)} %bitcast.23, bf16[8,4,32,96]{3,2,1,0:T(8,128)(2,1)S(1)} %collective-permute-done.2.other_ref, bf16[288,768]{1,0:T(8,128)(2,1)S(1)} %bitcast.24, bf16[288,768]{1,0:T(8,128)(2,1)S(1)} %bitcast.25, bf16[32,6144]{1,0:T(8,128)(2,1)S(1)} %bitcast.27, ...), custom_call_target="tpu_custom_call" | custom-call | tf_op jit(solution)/shard_map/gate_parts/pallas_call | solution.py:23
  120.8 5.7 %all-to-all-start.6 = ((bf16[8,32,768]{2,1,0:T(8,128)(2,1)}), bf16[8,32,768]{2,1,0:T(8,128)(2,1)S(1)}, u32[]{:S(2)}, u32[]{:S(2)}) async-start(bf16[8,32,768]{2,1,0:T(8,128)(2,1)} %gate_parts.1), calls=%async_computation.6 | async-start | bytes 786432 | tf_op jit(solution)/shard_map/all_to_all | solution.py:235
  126.6 7.1 %all-to-all-done.6.got_ref = bf16[8,32,768]{2,1,0:T(8,128)(2,1)S(1)} async-done(((bf16[8,32,768]{2,1,0:T(8,128)(2,1)}), bf16[8,32,768]{2,1,0:T(8,128)(2,1)S(1)}, u32[]{:S(2)}, u32[]{:S(2)}) %all-to-all-start.6) | async-done | bytes 393248 | tf_op jit(solution)/shard_map/all_to_all | solution.py:235
  134.7 9.5 %all_to_all.54.got_ref = bf16[8,32,288]{2,1,0:T(8,128)(2,1)S(1)} all-to-all(bf16[8,32,288]{2,1,0:T(8,128)(2,1)S(1)} %get-tuple-element.13), channel_id=1, replica_groups=mesh['yl'=2,'x'=4,'yh'=4,'zh'=2,'zl'=4,'c'=2] {'yl','x'}, dimensions={0} | all-to-all | bytes 294912 | tf_op jit(solution)/shard_map/all_to_all | solution.py:235
  145.6 1.9 %collective-permute-start.3 = (bf16[8,4,32,96]{3,2,1,0:T(8,128)(2,1)S(1)}, bf16[8,4,32,96]{3,2,1,0:T(8,128)(2,1)S(1)}, u32[]{:S(2)}, u32[]{:S(2)}) collective-permute-start(bf16[8,4,32,96]{3,2,1,0:T(8,128)(2,1)S(1)} %get-tuple-element.15), channel_id=1, source_target_pairs={{0,1},{1,0},{2,3},{3,2},{4,5},{5,4},{6,7},{7,6},{8,9},{9,8},{10,11... | collective-permute-start | bytes 589832 | tf_op jit(solution)/shard_map/ppermute | solution.py:266
  149.1 10.9 %all_to_all.55 = bf16[8,4,32,96]{3,2,1,0:T(8,128)(2,1)} all-to-all(bf16[8,4,32,96]{3,2,1,0:T(8,128)(2,1)S(1)} %add_convert_fusion), channel_id=1, replica_groups=mesh['yl'=2,'x'=4,'yh'=4,'zh'=2,'zl'=4,'c'=2] {'yl','x'}, dimensions={0} | all-to-all | bytes 393216 | tf_op jit(solution)/shard_map/all_to_all | solution.py:235
  160.0 4.7 %all-to-all-start.9 = ((bf16[32,32,96]{2,1,0:T(8,128)(2,1)}), bf16[32,32,96]{2,1,0:T(8,128)(2,1)S(1)}, u32[]{:S(2)}, u32[]{:S(2)}) async-start(bf16[32,32,96]{2,1,0:T(8,128)(2,1)} %bitcast.17), calls=%async_computation.9 | async-start | bytes 524288 | tf_op jit(solution)/shard_map/all_to_all | solution.py:235
  164.8 14.6 %all-to-all-done.9.got_ref = bf16[32,32,96]{2,1,0:T(8,128)(2,1)S(1)} async-done(((bf16[32,32,96]{2,1,0:T(8,128)(2,1)}), bf16[32,32,96]{2,1,0:T(8,128)(2,1)S(1)}, u32[]{:S(2)}, u32[]{:S(2)}) %all-to-all-start.9) | async-done | bytes 196640 | tf_op jit(solution)/shard_map/all_to_all | solution.py:235
  (32 shorter events, 8.9 us)
Async XLA Ops:
  0.0 61.5 %copy-start = (f32[32,1,128,128]{3,2,1,0:T(8,128)S(1)}, f32[32,1,128,128]{3,2,1,0:T(8,128)}, u32[]{:S(2)}) copy-start(f32[32,1,128,128]{3,2,1,0:T(8,128)} %param.28) | copy-start | bytes 6291460
  30.9 11.1 %all-to-all-start.1 = ((bf16[8,4,32,96]{3,2,1,0:T(8,128)(2,1)}), bf16[8,4,32,96]{3,2,1,0:T(8,128)(2,1)S(1)}, u32[]{:S(2)}, u32[]{:S(2)}) async-start(bf16[8,4,32,96]{3,2,1,0:T(8,128)(2,1)} %bitcast.1), calls=%async_computation.1 | async-start | bytes 524288 | tf_op jit(solution)/shard_map/all_to_all | solution.py:235
  42.0 3.4 %collective-permute-start = (bf16[8,4,32,96]{3,2,1,0:T(8,128)(2,1)S(1)}, bf16[8,4,32,96]{3,2,1,0:T(8,128)(2,1)S(1)}, u32[]{:S(2)}, u32[]{:S(2)}) collective-permute-start(bf16[8,4,32,96]{3,2,1,0:T(8,128)(2,1)S(1)} %all-to-all-done.1.own_ref.tokens_ref), channel_id=1, source_target_pairs={{0,1},{1,0},{2,3},{3,2},{4,5},{5,4},{6,7},{7,6},{8,9},{9,8},{10,11... | collective-permute-start | bytes 589832 | tf_op jit(solution)/shard_map/ppermute | solution.py:281
  48.8 23.8 %copy-start.5 = (bf16[768,128]{1,0:T(8,128)(2,1)S(1)}, bf16[768,128]{1,0:T(8,128)(2,1)}, u32[]{:S(2)}) copy-start(bf16[768,128]{1,0:T(8,128)(2,1)} %weight_ref.1) | copy-start | bytes 589828
  48.8 12.7 %all-to-all-start.2 = ((bf16[8,48,512]{2,1,0:T(8,128)(2,1)}), bf16[8,48,512]{2,1,0:T(8,128)(2,1)S(1)}, u32[]{:S(2)}, u32[]{:S(2)}) async-start(bf16[8,48,512]{2,1,0:T(8,128)(2,1)} %qkv_parts.1), calls=%async_computation.2 | async-start | bytes 786432 | tf_op jit(solution)/shard_map/all_to_all | solution.py:235
  63.5 55.4 %copy-start.1 = (bf16[768,288]{0,1:T(8,128)(2,1)S(1)}, bf16[768,288]{0,1:T(8,128)(2,1)}, u32[]{:S(2)}) copy-start(bf16[768,288]{0,1:T(8,128)(2,1)} %param.21) | copy-start | bytes 1327108
  63.6 55.4 %copy-start.2 = (bf16[768,288]{0,1:T(8,128)(2,1)S(1)}, bf16[768,288]{0,1:T(8,128)(2,1)}, u32[]{:S(2)}) copy-start(bf16[768,288]{0,1:T(8,128)(2,1)} %param.22) | copy-start | bytes 1327108
  63.6 55.3 %copy-start.4 = (bf16[6144,32]{0,1:T(8,128)(2,1)S(1)}, bf16[6144,32]{0,1:T(8,128)(2,1)}, u32[]{:S(2)}) copy-start(bf16[6144,32]{0,1:T(8,128)(2,1)} %param.24) | copy-start | bytes 1179652
  63.6 55.3 %copy-start.6 = (f32[6144]{0:T(1024)S(1)}, f32[6144]{0:T(1024)}, u32[]{:S(2)}) copy-start(f32[6144]{0:T(1024)} %param.26) | copy-start | bytes 73732
  73.6 3.4 %collective-permute-start.1 = (bf16[8,4,32,96]{3,2,1,0:T(8,128)(2,1)S(1)}, bf16[8,4,32,96]{3,2,1,0:T(8,128)(2,1)S(1)}, u32[]{:S(2)}, u32[]{:S(2)}) collective-permute-start(bf16[8,4,32,96]{3,2,1,0:T(8,128)(2,1)S(1)} %get-tuple-element.12), channel_id=1, source_target_pairs={{0,1},{1,0},{2,3},{3,2},{4,5},{5,4},{6,7},{7,6},{8,9},{9,8},{10,11... | collective-permute-start | bytes 589832 | tf_op jit(solution)/shard_map/ppermute | solution.py:266
  96.0 30.5 %copy-start.8 = (s32[32,2]{0,1:T(2,128)S(1)}, s32[32,2]{0,1:T(2,128)}, u32[]{:S(2)}) copy-start(s32[32,2]{0,1:T(2,128)} %param.29) | copy-start | bytes 772
  96.0 37.7 %copy-start.7 = (s32[32]{0:T(128)S(1)}, s32[32]{0:T(128)}, u32[]{:S(2)}) copy-start(s32[32]{0:T(128)} %param.30) | copy-start | bytes 388
  96.6 47.5 %copy-start.3 = (bf16[768,288]{0,1:T(8,128)(2,1)S(1)}, bf16[768,288]{0,1:T(8,128)(2,1)}, u32[]{:S(2)}) copy-start(bf16[768,288]{0,1:T(8,128)(2,1)} %param.23) | copy-start | bytes 1327108
  115.5 3.4 %collective-permute-start.2 = (bf16[8,4,32,96]{3,2,1,0:T(8,128)(2,1)S(1)}, bf16[8,4,32,96]{3,2,1,0:T(8,128)(2,1)S(1)}, u32[]{:S(2)}, u32[]{:S(2)}) collective-permute-start(bf16[8,4,32,96]{3,2,1,0:T(8,128)(2,1)S(1)} %bitcast.22), channel_id=1, source_target_pairs={{0,1},{1,0},{2,3},{3,2},{4,5},{5,4},{6,7},{7,6},{8,9},{9,8},{10,11... | collective-permute-start | bytes 589832 | tf_op jit(solution)/shard_map/ppermute | solution.py:334
  120.8 12.9 %all-to-all-start.6 = ((bf16[8,32,768]{2,1,0:T(8,128)(2,1)}), bf16[8,32,768]{2,1,0:T(8,128)(2,1)S(1)}, u32[]{:S(2)}, u32[]{:S(2)}) async-start(bf16[8,32,768]{2,1,0:T(8,128)(2,1)} %gate_parts.1), calls=%async_computation.6 | async-start | bytes 786432 | tf_op jit(solution)/shard_map/all_to_all | solution.py:235
  145.6 3.4 %collective-permute-start.3 = (bf16[8,4,32,96]{3,2,1,0:T(8,128)(2,1)S(1)}, bf16[8,4,32,96]{3,2,1,0:T(8,128)(2,1)S(1)}, u32[]{:S(2)}, u32[]{:S(2)}) collective-permute-start(bf16[8,4,32,96]{3,2,1,0:T(8,128)(2,1)S(1)} %get-tuple-element.15), channel_id=1, source_target_pairs={{0,1},{1,0},{2,3},{3,2},{4,5},{5,4},{6,7},{7,6},{8,9},{9,8},{10,11... | collective-permute-start | bytes 589832 | tf_op jit(solution)/shard_map/ppermute | solution.py:266
  160.0 19.4 %all-to-all-start.9 = ((bf16[32,32,96]{2,1,0:T(8,128)(2,1)}), bf16[32,32,96]{2,1,0:T(8,128)(2,1)S(1)}, u32[]{:S(2)}, u32[]{:S(2)}) async-start(bf16[32,32,96]{2,1,0:T(8,128)(2,1)} %bitcast.17), calls=%async_computation.9 | async-start | bytes 524288 | tf_op jit(solution)/shard_map/all_to_all | solution.py:235

commit v4 on v3

--- a/solution.py
+++ b/solution.py
@@ -12,7 +12,8 @@
 CORES = [(0, 1), (1, 0)]
 D, FF, DH = 6144, 9216, 128
 EPS = 1e-6
-CHUNK, SLICE, SLOTS, MIG, UNITS = 96, 768, 32, 16, 288
+PACK = (24, 128)
+CHUNK, HALF, SLICE, SLOTS, MIG, UNITS = 96, 384, 768, 32, 16, 288
 VMEM = pl.BlockSpec(memory_space=pltpu.VMEM)
 HBM = pl.BlockSpec(memory_space=pltpu.HBM)
 SMEM = pl.BlockSpec(memory_space=pltpu.SMEM)
@@ -42,6 +43,18 @@
     return x * (1.0 / (1.0 + jnp.exp(-x)))
 
 
+def packed(rows):
+    last = rows[..., 24:, :]
+    beside = jnp.concatenate([last[..., 32 * i : 32 * i + 32] for i in range(3)], axis=-2)
+    return jnp.concatenate([rows[..., :24, :], beside], axis=-1)
+
+
+def unpacked(rows):
+    beside = rows[..., CHUNK:]
+    last = jnp.concatenate([beside[..., 8 * i : 8 * i + 8, :] for i in range(3)], axis=-1)
+    return jnp.concatenate([rows[..., :CHUNK], last], axis=-2)
+
+
 def fetch(pairs, sems):
     copies = [pltpu.make_async_copy(a, b, sems.at[i]) for i, (a, b) in enumerate(pairs)]
     for copy in copies:
@@ -53,21 +66,23 @@
     for copy in fetch(((tokens_ref, held_ref), (slot_ref, row_ref)), sems):
         copy.wait()
     place = lax.broadcasted_iota(jnp.int32, (SLOTS, SLOTS), 0) == row_ref[...]
-    rows = jnp.dot(
-        place.astype(F32).astype(BF16), held_ref[...], preferred_element_type=F32
+    rows = packed(
+        jnp.dot(place.astype(F32).astype(BF16), held_ref[...], preferred_element_type=F32)
     ).astype(BF16)
     for i in range(32):
         out_ref[i] = rows
 
 
-def slice_rows(own_ref, other_ref, gain_ref, where_ref):
-    group, first = where_ref[0], where_ref[1] == 0
+def chunk_rows(own_ref, other_ref, first):
     pieces = []
     for pair in range(4):
-        own = own_ref[:, pair].reshape(8 * SLOTS, CHUNK).astype(F32)
-        other = other_ref[:, pair].reshape(8 * SLOTS, CHUNK).astype(F32)
+        own = unpacked(own_ref[:, pair].astype(F32)).reshape(8 * SLOTS, CHUNK)
+        other = unpacked(other_ref[:, pair].astype(F32)).reshape(8 * SLOTS, CHUNK)
         pieces += [jnp.where(first, own, other), jnp.where(first, other, own)]
-    rows = jnp.concatenate(pieces, axis=1)
+    return jnp.concatenate(pieces, axis=1)
+
+
+def scaled_rows(rows, gain_ref, group):
     scaled = [
         (rows[:, 128 * j : 128 * j + 128] * gain_ref[pl.ds(6 * group + j, 1), :]).astype(BF16)
         for j in range(6)
@@ -82,25 +97,26 @@
 
 
 def qkv_kernel(
-    own_ref, other_ref, q_ref, k_ref, v_ref, gain_ref, target_ref, where_ref, out_ref, scale_ref, held_ref, sems
+    own_ref, other_ref, q_ref, k_ref, v_ref, gain_ref, target_ref, where_ref, out_ref, tokens_ref, scale_ref, held_ref, half_ref, sems
 ):
-    pairs = [(ref, held_ref.at[i]) for i, ref in enumerate((q_ref, k_ref, v_ref))]
+    pairs = [(ref, held_ref.at[:, pl.ds(128 * i, 128)]) for i, ref in enumerate((q_ref, k_ref, v_ref))]
     gain, *copies = fetch([(gain_ref, scale_ref), *pairs], sems)
+    first = where_ref[1] == 0
+    rows = chunk_rows(own_ref, other_ref, first)
+    half_ref[...] = jnp.where(first, rows[:, :HALF], rows[:, HALF:])
+    tokens_ref[...] = half_ref[pl.ds(pl.multiple_of(8 * where_ref[4], 8), 8), :]
     gain.wait()
-    rows, total = slice_rows(own_ref, other_ref, scale_ref, where_ref)
-    parts = []
-    for i, copy in enumerate(copies):
+    rows, total = scaled_rows(rows, scale_ref, where_ref[0])
+    for copy in copies:
         copy.wait()
-        parts.append(jnp.dot(rows, held_ref[i], preferred_element_type=F32))
+    parts = jnp.dot(rows, held_ref[...], preferred_element_type=F32)
+    parts = jnp.concatenate([parts, stats_lanes(total, 0)], axis=1).astype(BF16)
     pick = lax.broadcasted_iota(jnp.int32, (MIG, SLOTS), 1) == target_ref[...]
     pick = pick.astype(F32).astype(BF16)
-    for i, part in enumerate((*parts, stats_lanes(total, 0))):
-        part = part.astype(BF16)
-        lanes = slice(128 * i, 128 * i + 128)
-        out_ref[:, :SLOTS, lanes] = part.reshape(8, SLOTS, 128)
-        moved = jnp.dot(pick, part[7 * SLOTS :], preferred_element_type=F32).astype(BF16)
-        for d in range(8):
-            out_ref[d, SLOTS:, lanes] = moved
+    moved = jnp.dot(pick, parts[7 * SLOTS :], preferred_element_type=F32).astype(BF16)
+    out_ref[:, :SLOTS] = parts.reshape(8, SLOTS, 512)
+    for d in range(8):
+        out_ref[d, SLOTS:] = moved
 
 
 def attention_kernel(got_ref, states_ref, source_ref, decay_ref, migration_ref, where_ref, out_ref, o_ref):
@@ -131,7 +147,7 @@
 
 
 def output_kernel(got_ref, weight_ref, target_ref, where_ref, keep_ref, send_ref):
-    core = where_ref[1]
+    first = where_ref[1] == 0
     moved = got_ref[0, SLOTS:].astype(F32)
     for i in range(1, 8):
         moved += got_ref[i, SLOTS:].astype(F32)
@@ -141,25 +157,33 @@
     taken = jnp.sum(place, axis=1, keepdims=True) > 0.0
     last = jnp.where(taken, landed, got_ref[7, :SLOTS].astype(F32)).astype(BF16)
     rows = jnp.concatenate([got_ref[:7, :SLOTS].reshape(7 * SLOTS, DH), last], axis=0)
-    for pair in range(4):
-        for ref, side in ((keep_ref, core), (send_ref, 1 - core)):
-            at = pl.multiple_of((2 * pair + side) * CHUNK, 32)
-            part = dot_nt(rows, weight_ref[pl.ds(at, CHUNK), :])
-            ref[:, pair] = part.reshape(8, SLOTS, CHUNK).astype(ref.dtype)
-
-
-def resid_kernel(got_ref, tokens_ref, where_ref, spread_ref):
+    part = dot_nt(rows, weight_ref[...])
+    low, high = part[:, :HALF], part[:, HALF:]
+    keep_ref[...] = jnp.where(first, low, high).reshape(32, 8, HALF)
+    send_ref[...] = jnp.where(first, high, low).reshape(32, 8, HALF).astype(BF16)
+
+
+def resid_kernel(got_ref, tokens_ref, spread_ref):
     total = got_ref[0].astype(F32)
     for i in range(1, 32):
         total += got_ref[i].astype(F32)
-    tokens = tokens_ref[where_ref[3], where_ref[4]]
-    resid = (tokens.astype(F32) + total).astype(BF16)
+    resid = (tokens_ref[...] + total).astype(BF16)
     for i in range(32):
         spread_ref[i] = resid
 
 
-def gate_kernel(own_ref, other_ref, gate_ref, up_ref, router_ref, gain_ref, where_ref, out_ref):
-    rows, total = slice_rows(own_ref, other_ref, gain_ref, where_ref)
+def gate_kernel(
+    own_ref, other_ref, gate_ref, up_ref, router_ref, gain_ref, where_ref, out_ref, blocks_ref
+):
+    first = where_ref[1] == 0
+    own = own_ref[...].astype(F32).reshape(8 * SLOTS, HALF)
+    other = other_ref[...].astype(F32).reshape(8 * SLOTS, HALF)
+    rows = jnp.concatenate([jnp.where(first, own, other), jnp.where(first, other, own)], axis=1)
+    start = lax.broadcasted_iota(jnp.int32, (SLICE, CHUNK), 0) - CHUNK * where_ref[5]
+    pick = (start == lax.broadcasted_iota(jnp.int32, (SLICE, CHUNK), 1)).astype(F32).astype(BF16)
+    blocks = jnp.dot(rows.astype(BF16), pick, preferred_element_type=F32)
+    blocks_ref[...] = blocks.astype(BF16).reshape(8, SLOTS, CHUNK)
+    rows, total = scaled_rows(rows, gain_ref, where_ref[0])
     gate = dot_nt(rows, gate_ref[:256])
     up = dot_nt(rows, up_ref[:256])
     at = pl.multiple_of(where_ref[0] * SLICE, SLICE)
@@ -169,14 +193,10 @@
     out_ref[:, :, :256] = gate.astype(BF16).reshape(8, SLOTS, 256)
     out_ref[:, :, 256:512] = up.astype(BF16).reshape(8, SLOTS, 256)
     out_ref[:, :, 512:640] = tail.astype(BF16).reshape(8, SLOTS, 128)
-    for d in range(8):
-        out_ref[d, :, 640:736] = own_ref[d, where_ref[4]]
-        out_ref[d, :, 736:] = jnp.zeros((SLOTS, 32), BF16)
-
-
-def hidden_kernel(got_ref, ids_ref, slot_row_ref, where_ref, out_ref, resid_ref):
+
+
+def hidden_kernel(got_ref, blocks_ref, ids_ref, slot_row_ref, where_ref, out_ref):
     expert = where_ref[2]
-    resid_ref[...] = got_ref[where_ref[3], :, 640:736]
     total = got_ref[0].astype(F32)
     for i in range(1, 8):
         total += got_ref[i].astype(F32)
@@ -198,29 +218,31 @@
     mine = jnp.where(ids[:, 0:1] == expert, lifted[0], 0.0)
     mine += jnp.where(ids[:, 1:2] == expert, lifted[1], 0.0)
     share = mine / (lifted[0] + lifted[1])
-    main, rest = (main * share).astype(BF16), (rest * share).astype(BF16)
+    main, rest = (main * share).astype(BF16), rest * share
     for d in range(8):
         out_ref[d, :, :256] = main
-        out_ref[d, :, 256:] = rest
-
-
-def down_kernel(got_ref, down_ref, where_ref, keep_ref, send_ref):
+        out_ref[d, :, 256:] = jnp.concatenate([rest, blocks_ref[d].astype(F32)], axis=1).astype(BF16)
+
+
+def down_kernel(got_ref, down_ref, where_ref, keep_ref, send_ref, resid_ref):
     first = where_ref[1] == 0
     part = jnp.dot(
-        got_ref[...].reshape(8 * SLOTS, UNITS), down_ref[...], preferred_element_type=F32
-    )
+        got_ref[:, :, :UNITS].reshape(8 * SLOTS, UNITS), down_ref[...], preferred_element_type=F32
+    )
+    resid_ref[...] = got_ref[where_ref[3], :, UNITS:]
     for pair in range(4):
         even = part[:, 192 * pair : 192 * pair + 96]
         odd = part[:, 192 * pair + 96 : 192 * pair + 192]
-        keep_ref[:, pair] = jnp.where(first, even, odd).reshape(8, SLOTS, CHUNK)
-        send_ref[:, pair] = jnp.where(first, odd, even).astype(BF16).reshape(8, SLOTS, CHUNK)
+        keep_ref[:, pair] = packed(jnp.where(first, even, odd).reshape(8, SLOTS, CHUNK))
+        sent = packed(jnp.where(first, odd, even).reshape(8, SLOTS, CHUNK))
+        send_ref[:, pair] = sent.astype(BF16)
 
 
 def final_kernel(got_ref, resid_ref, slot_ref, out_ref):
     total = got_ref[0].astype(F32)
     for i in range(1, 32):
         total += got_ref[i].astype(F32)
-    out = (resid_ref[...].astype(F32) + total).astype(BF16)
+    out = (resid_ref[...].astype(F32) + unpacked(total)).astype(BF16)
     place = lax.broadcasted_iota(jnp.int32, (SLOTS, SLOTS), 1) == slot_ref[...]
     out_ref[...] = jnp.dot(
         place.astype(F32).astype(BF16), out, preferred_element_type=F32
@@ -257,7 +279,7 @@
     core = lax.axis_index("c").astype(jnp.int32)
     device = lax.axis_index(EPA).astype(jnp.int32)
     expert = device * UNITS // FF
-    where = jnp.stack([group, core, expert, device // 8, device % 8 // 2])
+    where = jnp.stack([group, core, expert, device // 8, device // 2, device % 8])
     slot_row, slot_column = row_slot[None, :], row_slot[:, None]
 
     attn_gain, expert_gain = attn_gain.reshape(48, 128), expert_gain.reshape(48, 128)
@@ -267,7 +289,7 @@
 
     spread = pl.pallas_call(
         sort_kernel,
-        out_shape=shape((32, SLOTS, CHUNK), BF16),
+        out_shape=shape((32, *PACK), BF16),
         in_specs=[HBM, HBM],
         out_specs=VMEM,
         scratch_shapes=[
@@ -277,16 +299,17 @@
         ],
         name="sorted_rows",
     )(in_hbm(tokens), in_hbm(slot_row))
-    own = exchange(exchange(spread, CHIPS).reshape(8, 4, SLOTS, CHUNK), GRP)
-    rows_own, other = own, lax.ppermute(own, "c", CORES)
-    parts = pl.pallas_call(
+    own = exchange(exchange(spread, CHIPS).reshape(8, 4, *PACK), GRP)
+    other = lax.ppermute(own, "c", CORES)
+    parts, block = pl.pallas_call(
         qkv_kernel,
-        out_shape=shape((8, SLOTS + MIG, 512), BF16),
+        out_shape=(shape((8, SLOTS + MIG, 512), BF16), shape((8, HALF), F32)),
         in_specs=[VMEM, VMEM, HBM, HBM, HBM, HBM, VMEM, SMEM],
-        out_specs=VMEM,
+        out_specs=(VMEM, VMEM),
         scratch_shapes=[
             pltpu.VMEM((48, 128), F32),
-            pltpu.VMEM((3, SLICE, DH), BF16),
+            pltpu.VMEM((SLICE, 3 * DH), BF16),
+            pltpu.VMEM((8 * SLOTS, HALF), F32),
             pltpu.SemaphoreType.DMA((4,)),
         ],
         compiler_params=pltpu.CompilerParams(vmem_limit_bytes=16 << 20),
@@ -314,49 +337,48 @@
     heads = exchange(heads, GRP)
     keep, send = call(
         output_kernel,
-        (shape((8, 4, SLOTS, CHUNK), F32), shape((8, 4, SLOTS, CHUNK), BF16)),
+        (shape((32, 8, HALF), F32), shape((32, 8, HALF), BF16)),
         (heads, output_weight, migration[:, 2][None, :], where),
         "output_parts",
         smem=(3,),
     )
     spread = call(
         resid_kernel,
-        shape((32, SLOTS, CHUNK), BF16),
-        (
-            exchange(merge(keep, send).reshape(32, SLOTS, CHUNK), CHIPS),
-            rows_own,
-            where,
-        ),
+        shape((32, 8, HALF), BF16),
+        (exchange(merge(keep, send), CHIPS), block),
         "resid",
-        smem=(2,),
-    )
-    own = exchange(spread, CHIPS).reshape(8, 4, SLOTS, CHUNK)
+    )
+    own = exchange(spread, CHIPS)
     other = lax.ppermute(own, "c", CORES)
-    parts = call(
+    parts, blocks = call(
         gate_kernel,
-        shape((8, SLOTS, 768), BF16),
+        (shape((8, SLOTS, 640), BF16), shape((8, SLOTS, CHUNK), BF16)),
         (own, other, gate_weight.T, up_weight.T, router_weight.T, expert_gain, where),
         "gate_parts",
         smem=(6,),
     )
     parts = exchange(parts, GRP)
-    hidden, resid = call(
+    hidden = call(
         hidden_kernel,
-        (shape((8, SLOTS, UNITS), BF16), shape((SLOTS, CHUNK), BF16)),
-        (parts, expert_ids, slot_row, where),
+        shape((8, SLOTS, UNITS + CHUNK), BF16),
+        (parts, blocks, expert_ids, slot_row, where),
         "hidden",
-        smem=(3,),
+        smem=(4,),
     )
     hidden = exchange(hidden, GRP)
-    keep, send = call(
+    keep, send, resid = call(
         down_kernel,
-        (shape((8, 4, SLOTS, CHUNK), F32), shape((8, 4, SLOTS, CHUNK), BF16)),
+        (
+            shape((8, 4, *PACK), F32),
+            shape((8, 4, *PACK), BF16),
+            shape((SLOTS, CHUNK), BF16),
+        ),
         (hidden, down_weight.T, where),
         "down_parts",
         smem=(2,),
     )
     parts = exchange(merge(keep, send), GRP)
-    parts = exchange(parts.reshape(32, SLOTS, CHUNK), CHIPS)
+    parts = exchange(parts.reshape(32, *PACK), CHIPS)
     return call(
         final_kernel,
         shape((SLOTS, CHUNK), BF16),

time: 181 us -> 173 us (0.956)
  the two profiles are of different devices: /device:TPU:10 before, /device:TPU:8 now
where the time goes in v4:
time: 173 us; the launch traced here: 172 us
  blocking collectives  91.7 us (53%)
  waiting for transfers between devices  37.5 us (22%)
  starting transfers between devices  27.2 us (16%)
  Pallas kernels  13.3 us (8%)
    all_to_all x6, blocking collectives, exchange(): return lax.all_to_all(x, axes, 0, 0)  91.7 us
    all_to_all x4, waiting for transfers between devices, exchange(): return lax.all_to_all(x, axes, 0, 0)  32 us
    all_to_all x4, starting transfers between devices, exchange(): return lax.all_to_all(x, axes, 0, 0)  19.5 us
    pallas_call x6, Pallas kernels, call(): pl.pallas_call(kernel, out_shape=outs, in_specs=specs, out_specs=jax.tree...  6.29 us
    ppermute x2, starting transfers between devices, merge(): return (keep + lax.ppermute(send, 'c', CORES).astype(F32)).astype(BF16)  3.84 us
    ppermute x2, starting transfers between devices, shards(): other = lax.ppermute(own, 'c', CORES)  3.82 us
  transfers between devices with their start and end apart: 8, of which 8 were waited for; matrix products, arithmetic and copies ran while one was open for 1% of the time, Pallas kernels for 0%

profile of v4, /device:TPU:8, one launch (start us, length us, event | category | flops | bytes accessed | tf_op | source)
XLA Modules:
  0.0 171.7 jit_solution(7580014380632476971)
XLA Ops:
  0.0 1.8 %sorted_rows.1 = bf16[32,24,128]{2,1,0:T(8,128)(2,1)} custom-call(bf16[32,96]{1,0:T(8,128)(2,1)} %tokens_ref.1, s32[1,32]{1,0:T(1,128)} %bitcast.26), custom_call_target="tpu_custom_call" | custom-call | tf_op jit(solution)/shard_map/sorted_rows/pallas_call | solution.py:290
  1.8 28.7 %all_to_all.50 = bf16[32,24,128]{2,1,0:T(8,128)(2,1)} all-to-all(bf16[32,24,128]{2,1,0:T(8,128)(2,1)} %sorted_rows.1), channel_id=1, replica_groups=mesh['yl'=2,'x'=4,'yh'=4,'zh'=2,'zl'=4,'c'=2] {'yh','zh','zl'}, dimensions={0} | all-to-all | bytes 393216 | tf_op jit(solution)/shard_map/all_to_all | solution.py:257
  30.5 5.8 %all-to-all-start.1 = ((bf16[8,4,24,128]{3,2,1,0:T(8,128)(2,1)}), bf16[8,4,24,128]{3,2,1,0:T(8,128)(2,1)S(1)}, u32[]{:S(2)}, u32[]{:S(2)}) async-start(bf16[8,4,24,128]{3,2,1,0:T(8,128)(2,1)} %bitcast.1), calls=%async_computation.1 | async-start | bytes 393216 | tf_op jit(solution)/shard_map/all_to_all | solution.py:257
  37.1 4.7 %all-to-all-done.1.own_ref = bf16[8,4,24,128]{3,2,1,0:T(8,128)(2,1)S(1)} async-done(((bf16[8,4,24,128]{3,2,1,0:T(8,128)(2,1)}), bf16[8,4,24,128]{3,2,1,0:T(8,128)(2,1)S(1)}, u32[]{:S(2)}, u32[]{:S(2)}) %all-to-all-start.1) | async-done | bytes 196640 | tf_op jit(solution)/shard_map/all_to_all | solution.py:257
  41.7 1.9 %collective-permute-start = (bf16[8,4,24,128]{3,2,1,0:T(8,128)(2,1)S(1)}, bf16[8,4,24,128]{3,2,1,0:T(8,128)(2,1)S(1)}, u32[]{:S(2)}, u32[]{:S(2)}) collective-permute-start(bf16[8,4,24,128]{3,2,1,0:T(8,128)(2,1)S(1)} %all-to-all-done.1.own_ref), channel_id=1, source_target_pairs={{0,1},{1,0},{2,3},{3,2},{4,5},{5,4},{6,7},{7,6},{8,9},{9,8},{10,11... | collective-permute-start | bytes 589832 | tf_op jit(solution)/shard_map/ppermute | solution.py:303
  45.1 3.1 %qkv_parts.1 = (bf16[8,48,512]{2,1,0:T(8,128)(2,1)}, f32[8,384]{1,0:T(8,128)S(1)}) custom-call(bf16[8,4,24,128]{3,2,1,0:T(8,128)(2,1)S(1)} %all-to-all-done.1.own_ref, bf16[8,4,24,128]{3,2,1,0:T(8,128)(2,1)S(1)} %collective-permute-done.other_ref, bf16[768,128]{1,0:T(8,128)(2,1)} %q_ref.1, bf16[768,128]{1,0:T(8,128)(2,1)} %k_ref.1, bf16[768,128]{1,0:T(8,128)(2,1)} %v_ref.1, ...), custom_call_target="tpu_custom_call" | custom-call | tf_op jit(solution)/shard_map/qkv_parts/pallas_call | solution.py:304
  48.2 4.8 %all-to-all-start.2 = ((bf16[8,48,512]{2,1,0:T(8,128)(2,1)}), bf16[8,48,512]{2,1,0:T(8,128)(2,1)S(1)}, u32[]{:S(2)}, u32[]{:S(2)}) async-start(bf16[8,48,512]{2,1,0:T(8,128)(2,1)} %get-tuple-element.14), calls=%async_computation.2 | async-start | bytes 786432 | tf_op jit(solution)/shard_map/all_to_all | solution.py:257
  53.7 7.2 %all-to-all-done.2.got_ref = bf16[8,48,512]{2,1,0:T(8,128)(2,1)S(1)} async-done(((bf16[8,48,512]{2,1,0:T(8,128)(2,1)}), bf16[8,48,512]{2,1,0:T(8,128)(2,1)S(1)}, u32[]{:S(2)}, u32[]{:S(2)}) %all-to-all-start.2) | async-done | bytes 393248 | tf_op jit(solution)/shard_map/all_to_all | solution.py:257
  60.9 2.0 %attention.1 = bf16[8,48,128]{2,1,0:T(8,128)(2,1)S(1)} custom-call(bf16[8,48,512]{2,1,0:T(8,128)(2,1)S(1)} %all-to-all-done.2.got_ref, f32[32,128,128]{2,1,0:T(8,128)S(1)} %bitcast.20, s32[16,1]{1,0:T(8,128)S(1)} %get-tuple-element.24.source_ref, f32[1,1]{1,0:T(1,128)} %bitcast.19.decay_ref, s32[16,3]{1,0:T(8,128)S(1)} %copy.22.migration_ref, ...), custom_call_target="tpu_custom_call" | custom-call | tf_op jit(solution)/shard_map/attention/pallas_call | solution.py:328
  62.9 9.0 %all_to_all.51.got_ref = bf16[8,48,128]{2,1,0:T(8,128)(2,1)S(1)} all-to-all(bf16[8,48,128]{2,1,0:T(8,128)(2,1)S(1)} %attention.1), channel_id=1, replica_groups=mesh['yl'=2,'x'=4,'yh'=4,'zh'=2,'zl'=4,'c'=2] {'yl','x'}, dimensions={0} | all-to-all | bytes 196608 | tf_op jit(solution)/shard_map/all_to_all | solution.py:257
  72.8 1.9 %collective-permute-start.1 = (bf16[32,8,384]{2,1,0:T(8,128)(2,1)S(1)}, bf16[32,8,384]{2,1,0:T(8,128)(2,1)S(1)}, u32[]{:S(2)}, u32[]{:S(2)}) collective-permute-start(bf16[32,8,384]{2,1,0:T(8,128)(2,1)S(1)} %get-tuple-element.16), channel_id=1, source_target_pairs={{0,1},{1,0},{2,3},{3,2},{4,5},{5,4},{6,7},{7,6},{8,9},{9,8},{10,11... | collective-permute-start | bytes 589832 | tf_op jit(solution)/shard_map/ppermute | solution.py:288
  74.7 1.4 collective-permute-done.1
  76.2 17.0 %all_to_all.52.got_ref = bf16[32,8,384]{2,1,0:T(8,128)(2,1)S(1)} all-to-all(bf16[32,8,384]{2,1,0:T(8,128)(2,1)S(1)} %add_convert_fusion.1), channel_id=1, replica_groups=mesh['yl'=2,'x'=4,'yh'=4,'zh'=2,'zl'=4,'c'=2] {'yh','zh','zl'}, dimensions={0} | all-to-all | bytes 393216 | tf_op jit(solution)/shard_map/all_to_all | solution.py:257
  93.3 17.4 %all_to_all.53.own_ref = bf16[32,8,384]{2,1,0:T(8,128)(2,1)S(1)} all-to-all(bf16[32,8,384]{2,1,0:T(8,128)(2,1)S(1)} %resid.1), channel_id=1, replica_groups=mesh['yl'=2,'x'=4,'yh'=4,'zh'=2,'zl'=4,'c'=2] {'yh','zh','zl'}, dimensions={0} | all-to-all | bytes 393216 | tf_op jit(solution)/shard_map/all_to_all | solution.py:257
  110.6 1.9 %collective-permute-start.2 = (bf16[32,8,384]{2,1,0:T(8,128)(2,1)S(1)}, bf16[32,8,384]{2,1,0:T(8,128)(2,1)S(1)}, u32[]{:S(2)}, u32[]{:S(2)}) collective-permute-start(bf16[32,8,384]{2,1,0:T(8,128)(2,1)S(1)} %all_to_all.53.own_ref), channel_id=1, source_target_pairs={{0,1},{1,0},{2,3},{3,2},{4,5},{5,4},{6,7},{7,6},{8,9},{9,8},{10,11... | collective-permute-start | bytes 589832 | tf_op jit(solution)/shard_map/ppermute | solution.py:352
  114.0 1.9 %gate_parts.1 = (bf16[8,32,640]{2,1,0:T(8,128)(2,1)}, bf16[8,32,96]{2,1,0:T(8,128)(2,1)S(1)}) custom-call(bf16[32,8,384]{2,1,0:T(8,128)(2,1)S(1)} %all_to_all.53.own_ref, bf16[32,8,384]{2,1,0:T(8,128)(2,1)S(1)} %collective-permute-done.2.other_ref, bf16[288,768]{1,0:T(8,128)(2,1)S(1)} %bitcast.21, bf16[288,768]{1,0:T(8,128)(2,1)S(1)} %bitcast.22, ...), custom_call_target="tpu_custom_call" | custom-call | tf_op jit(solution)/shard_map/gate_parts/pallas_call | solution.py:24
  115.8 5.0 %all-to-all-start.6 = ((bf16[8,32,640]{2,1,0:T(8,128)(2,1)}), bf16[8,32,640]{2,1,0:T(8,128)(2,1)S(1)}, u32[]{:S(2)}, u32[]{:S(2)}) async-start(bf16[8,32,640]{2,1,0:T(8,128)(2,1)} %get-tuple-element.18), calls=%async_computation.6 | async-start | bytes 655360 | tf_op jit(solution)/shard_map/all_to_all | solution.py:257
  120.9 7.0 %all-to-all-done.6.got_ref = bf16[8,32,640]{2,1,0:T(8,128)(2,1)S(1)} async-done(((bf16[8,32,640]{2,1,0:T(8,128)(2,1)}), bf16[8,32,640]{2,1,0:T(8,128)(2,1)S(1)}, u32[]{:S(2)}, u32[]{:S(2)}) %all-to-all-start.6) | async-done | bytes 327712 | tf_op jit(solution)/shard_map/all_to_all | solution.py:257
  128.9 9.5 %all_to_all.54.got_ref = bf16[8,32,384]{2,1,0:T(8,128)(2,1)S(1)} all-to-all(bf16[8,32,384]{2,1,0:T(8,128)(2,1)S(1)} %hidden.1), channel_id=1, replica_groups=mesh['yl'=2,'x'=4,'yh'=4,'zh'=2,'zl'=4,'c'=2] {'yl','x'}, dimensions={0} | all-to-all | bytes 393216 | tf_op jit(solution)/shard_map/all_to_all | solution.py:257
  138.4 1.7 down_parts.1
  140.1 1.9 %collective-permute-start.3 = (bf16[8,4,24,128]{3,2,1,0:T(8,128)(2,1)S(1)}, bf16[8,4,24,128]{3,2,1,0:T(8,128)(2,1)S(1)}, u32[]{:S(2)}, u32[]{:S(2)}) collective-permute-start(bf16[8,4,24,128]{3,2,1,0:T(8,128)(2,1)S(1)} %get-tuple-element.21), channel_id=1, source_target_pairs={{0,1},{1,0},{2,3},{3,2},{4,5},{5,4},{6,7},{7,6},{8,9},{9,8},{10,11... | collective-permute-start | bytes 589832 | tf_op jit(solution)/shard_map/ppermute | solution.py:288
  143.4 10.2 %all_to_all.55 = bf16[8,4,24,128]{3,2,1,0:T(8,128)(2,1)} all-to-all(bf16[8,4,24,128]{3,2,1,0:T(8,128)(2,1)S(1)} %add_convert_fusion), channel_id=1, replica_groups=mesh['yl'=2,'x'=4,'yh'=4,'zh'=2,'zl'=4,'c'=2] {'yl','x'}, dimensions={0} | all-to-all | bytes 393216 | tf_op jit(solution)/shard_map/all_to_all | solution.py:257
  153.7 4.0 %all-to-all-start.9 = ((bf16[32,24,128]{2,1,0:T(8,128)(2,1)}), bf16[32,24,128]{2,1,0:T(8,128)(2,1)S(1)}, u32[]{:S(2)}, u32[]{:S(2)}) async-start(bf16[32,24,128]{2,1,0:T(8,128)(2,1)} %bitcast.16), calls=%async_computation.9 | async-start | bytes 393216 | tf_op jit(solution)/shard_map/all_to_all | solution.py:257
  157.7 13.2 %all-to-all-done.9.got_ref = bf16[32,24,128]{2,1,0:T(8,128)(2,1)S(1)} async-done(((bf16[32,24,128]{2,1,0:T(8,128)(2,1)}), bf16[32,24,128]{2,1,0:T(8,128)(2,1)S(1)}, u32[]{:S(2)}, u32[]{:S(2)}) %all-to-all-start.9) | async-done | bytes 196640 | tf_op jit(solution)/shard_map/all_to_all | solution.py:257
  (32 shorter events, 8.1 us)
Async XLA Ops:
  0.0 60.9 %copy-start = (f32[32,1,128,128]{3,2,1,0:T(8,128)S(1)}, f32[32,1,128,128]{3,2,1,0:T(8,128)}, u32[]{:S(2)}) copy-start(f32[32,1,128,128]{3,2,1,0:T(8,128)} %param.28) | copy-start | bytes 6291460
  30.5 11.3 %all-to-all-start.1 = ((bf16[8,4,24,128]{3,2,1,0:T(8,128)(2,1)}), bf16[8,4,24,128]{3,2,1,0:T(8,128)(2,1)S(1)}, u32[]{:S(2)}, u32[]{:S(2)}) async-start(bf16[8,4,24,128]{3,2,1,0:T(8,128)(2,1)} %bitcast.1), calls=%async_computation.1 | async-start | bytes 393216 | tf_op jit(solution)/shard_map/all_to_all | solution.py:257
  41.7 3.3 %collective-permute-start = (bf16[8,4,24,128]{3,2,1,0:T(8,128)(2,1)S(1)}, bf16[8,4,24,128]{3,2,1,0:T(8,128)(2,1)S(1)}, u32[]{:S(2)}, u32[]{:S(2)}) collective-permute-start(bf16[8,4,24,128]{3,2,1,0:T(8,128)(2,1)S(1)} %all-to-all-done.1.own_ref), channel_id=1, source_target_pairs={{0,1},{1,0},{2,3},{3,2},{4,5},{5,4},{6,7},{7,6},{8,9},{9,8},{10,11... | collective-permute-start | bytes 589832 | tf_op jit(solution)/shard_map/ppermute | solution.py:303
  45.1 26.9 %copy-start.5 = (bf16[768,128]{1,0:T(8,128)(2,1)S(1)}, bf16[768,128]{1,0:T(8,128)(2,1)}, u32[]{:S(2)}) copy-start(bf16[768,128]{1,0:T(8,128)(2,1)} %weight_ref.1) | copy-start | bytes 589828
  48.2 12.6 %all-to-all-start.2 = ((bf16[8,48,512]{2,1,0:T(8,128)(2,1)}), bf16[8,48,512]{2,1,0:T(8,128)(2,1)S(1)}, u32[]{:S(2)}, u32[]{:S(2)}) async-start(bf16[8,48,512]{2,1,0:T(8,128)(2,1)} %get-tuple-element.14), calls=%async_computation.2 | async-start | bytes 786432 | tf_op jit(solution)/shard_map/all_to_all | solution.py:257
  60.9 53.1 %copy-start.1 = (bf16[768,288]{0,1:T(8,128)(2,1)S(1)}, bf16[768,288]{0,1:T(8,128)(2,1)}, u32[]{:S(2)}) copy-start(bf16[768,288]{0,1:T(8,128)(2,1)} %param.21) | copy-start | bytes 1327108
  60.9 53.1 %copy-start.2 = (bf16[768,288]{0,1:T(8,128)(2,1)S(1)}, bf16[768,288]{0,1:T(8,128)(2,1)}, u32[]{:S(2)}) copy-start(bf16[768,288]{0,1:T(8,128)(2,1)} %param.22) | copy-start | bytes 1327108
  60.9 53.1 %copy-start.4 = (bf16[6144,32]{0,1:T(8,128)(2,1)S(1)}, bf16[6144,32]{0,1:T(8,128)(2,1)}, u32[]{:S(2)}) copy-start(bf16[6144,32]{0,1:T(8,128)(2,1)} %param.24) | copy-start | bytes 1179652
  60.9 53.1 %copy-start.6 = (f32[6144]{0:T(1024)S(1)}, f32[6144]{0:T(1024)}, u32[]{:S(2)}) copy-start(f32[6144]{0:T(1024)} %param.26) | copy-start | bytes 73732
  72.8 3.3 %collective-permute-start.1 = (bf16[32,8,384]{2,1,0:T(8,128)(2,1)S(1)}, bf16[32,8,384]{2,1,0:T(8,128)(2,1)S(1)}, u32[]{:S(2)}, u32[]{:S(2)}) collective-permute-start(bf16[32,8,384]{2,1,0:T(8,128)(2,1)S(1)} %get-tuple-element.16), channel_id=1, source_target_pairs={{0,1},{1,0},{2,3},{3,2},{4,5},{5,4},{6,7},{7,6},{8,9},{9,8},{10,11... | collective-permute-start | bytes 589832 | tf_op jit(solution)/shard_map/ppermute | solution.py:288
  76.1 44.6 %copy-start.8 = (s32[32,2]{0,1:T(2,128)S(1)}, s32[32,2]{0,1:T(2,128)}, u32[]{:S(2)}) copy-start(s32[32,2]{0,1:T(2,128)} %param.29) | copy-start | bytes 772
  76.1 51.8 %copy-start.7 = (s32[32]{0:T(128)S(1)}, s32[32]{0:T(128)}, u32[]{:S(2)}) copy-start(s32[32]{0:T(128)} %param.30) | copy-start | bytes 388
  93.2 45.2 %copy-start.3 = (bf16[768,288]{0,1:T(8,128)(2,1)S(1)}, bf16[768,288]{0,1:T(8,128)(2,1)}, u32[]{:S(2)}) copy-start(bf16[768,288]{0,1:T(8,128)(2,1)} %param.23) | copy-start | bytes 1327108
  110.6 3.3 %collective-permute-start.2 = (bf16[32,8,384]{2,1,0:T(8,128)(2,1)S(1)}, bf16[32,8,384]{2,1,0:T(8,128)(2,1)S(1)}, u32[]{:S(2)}, u32[]{:S(2)}) collective-permute-start(bf16[32,8,384]{2,1,0:T(8,128)(2,1)S(1)} %all_to_all.53.own_ref), channel_id=1, source_target_pairs={{0,1},{1,0},{2,3},{3,2},{4,5},{5,4},{6,7},{7,6},{8,9},{9,8},{10,11... | collective-permute-start | bytes 589832 | tf_op jit(solution)/shard_map/ppermute | solution.py:352
  115.8 12.1 %all-to-all-start.6 = ((bf16[8,32,640]{2,1,0:T(8,128)(2,1)}), bf16[8,32,640]{2,1,0:T(8,128)(2,1)S(1)}, u32[]{:S(2)}, u32[]{:S(2)}) async-start(bf16[8,32,640]{2,1,0:T(8,128)(2,1)} %get-tuple-element.18), calls=%async_computation.6 | async-start | bytes 655360 | tf_op jit(solution)/shard_map/all_to_all | solution.py:257
  140.1 3.3 %collective-permute-start.3 = (bf16[8,4,24,128]{3,2,1,0:T(8,128)(2,1)S(1)}, bf16[8,4,24,128]{3,2,1,0:T(8,128)(2,1)S(1)}, u32[]{:S(2)}, u32[]{:S(2)}) collective-permute-start(bf16[8,4,24,128]{3,2,1,0:T(8,128)(2,1)S(1)} %get-tuple-element.21), channel_id=1, source_target_pairs={{0,1},{1,0},{2,3},{3,2},{4,5},{5,4},{6,7},{7,6},{8,9},{9,8},{10,11... | collective-permute-start | bytes 589832 | tf_op jit(solution)/shard_map/ppermute | solution.py:288
  153.7 17.2 %all-to-all-start.9 = ((bf16[32,24,128]{2,1,0:T(8,128)(2,1)}), bf16[32,24,128]{2,1,0:T(8,128)(2,1)S(1)}, u32[]{:S(2)}, u32[]{:S(2)}) async-start(bf16[32,24,128]{2,1,0:T(8,128)(2,1)} %bitcast.16), calls=%async_computation.9 | async-start | bytes 393216 | tf_op jit(solution)/shard_map/all_to_all | solution.py:257

commit v5 on v4

--- a/solution.py
+++ b/solution.py
@@ -31,6 +31,10 @@
     )(*ins)
 
 
+def index_of(axes):
+    return lax.axis_index(axes).astype(jnp.int32)
+
+
 def shape(dims, dtype):
     return jax.ShapeDtypeStruct(dims, dtype)
 
@@ -96,30 +100,42 @@
     return jnp.where(at == lane, high, jnp.where(at == lane + 1, total - high, 0.0))
 
 
+def targets(migration_ref):
+    row = lax.broadcasted_iota(jnp.int32, (MIG, SLOTS), 0)
+    slot = lax.broadcasted_iota(jnp.int32, (MIG, SLOTS), 1)
+    found = jnp.zeros((MIG, SLOTS), F32)
+    for m in range(MIG):
+        found = jnp.where((row == m) & (slot == migration_ref[2, m]), 1.0, found)
+    return found
+
+
 def qkv_kernel(
-    own_ref, other_ref, q_ref, k_ref, v_ref, gain_ref, target_ref, where_ref, out_ref, tokens_ref, scale_ref, held_ref, half_ref, sems
+    own_ref, other_ref, q_ref, k_ref, v_ref, gain_ref, listed_ref, out_ref, tokens_ref,
+    scale_ref, held_ref, half_ref, migration_ref, sems
 ):
     pairs = [(ref, held_ref.at[:, pl.ds(128 * i, 128)]) for i, ref in enumerate((q_ref, k_ref, v_ref))]
-    gain, *copies = fetch([(gain_ref, scale_ref), *pairs], sems)
-    first = where_ref[1] == 0
+    gain, *copies = fetch([(gain_ref, scale_ref), *pairs, (listed_ref, migration_ref)], sems)
+    first = index_of("c") == 0
     rows = chunk_rows(own_ref, other_ref, first)
     half_ref[...] = jnp.where(first, rows[:, :HALF], rows[:, HALF:])
-    tokens_ref[...] = half_ref[pl.ds(pl.multiple_of(8 * where_ref[4], 8), 8), :]
+    tokens_ref[...] = half_ref[pl.ds(pl.multiple_of(8 * index_of(CHIPS), 8), 8), :]
     gain.wait()
-    rows, total = scaled_rows(rows, scale_ref, where_ref[0])
+    rows, total = scaled_rows(rows, scale_ref, index_of(GRP))
     for copy in copies:
         copy.wait()
     parts = jnp.dot(rows, held_ref[...], preferred_element_type=F32)
     parts = jnp.concatenate([parts, stats_lanes(total, 0)], axis=1).astype(BF16)
-    pick = lax.broadcasted_iota(jnp.int32, (MIG, SLOTS), 1) == target_ref[...]
-    pick = pick.astype(F32).astype(BF16)
+    pick = targets(migration_ref).astype(BF16)
     moved = jnp.dot(pick, parts[7 * SLOTS :], preferred_element_type=F32).astype(BF16)
     out_ref[:, :SLOTS] = parts.reshape(8, SLOTS, 512)
     for d in range(8):
         out_ref[d, SLOTS:] = moved
 
 
-def attention_kernel(got_ref, states_ref, source_ref, decay_ref, migration_ref, where_ref, out_ref, o_ref):
+def attention_kernel(
+    got_ref, states_ref, decay_ref, listed_ref, out_ref, place_ref, o_ref, migration_ref, sems
+):
+    (copy,) = fetch([(listed_ref, migration_ref)], sems)
     total = got_ref[0].astype(F32)
     for i in range(1, 8):
         total += got_ref[i].astype(F32)
@@ -130,29 +146,32 @@
     turned = jnp.concatenate([q, jnp.zeros((128 - rows, 128), F32)], axis=0).T
     for s in range(SLOTS):
         o_ref[s : s + 1, :] = jnp.sum(turned[:, s : s + 1] * states_ref[s], axis=0, keepdims=True)
+    copy.wait()
+    place_ref[...] = targets(migration_ref).T
     for m in range(MIG):
         s = SLOTS + m
         o_ref[s : s + 1, :] = jnp.sum(
-            turned[:, s : s + 1] * states_ref[migration_ref[m, 1]], axis=0, keepdims=True
+            turned[:, s : s + 1] * states_ref[migration_ref[1, m]], axis=0, keepdims=True
         )
-    retain = jnp.exp(-decay_ref[...])
+    retain = jnp.exp(jnp.full((1, DH), -decay_ref[0], F32))
     mixed = retain * o_ref[...] + jnp.sum(q * k, axis=1, keepdims=True) * v
     heads = mixed * lax.rsqrt(jnp.mean(mixed * mixed, axis=1, keepdims=True) + EPS)
-    here = source_ref[...] == where_ref[0]
-    own = heads[:SLOTS].astype(BF16)
-    moved = jnp.where(here, heads[SLOTS:], 0.0).astype(BF16)
+    own, moved = heads[:SLOTS].astype(BF16), heads[SLOTS:]
+    row, group = lax.broadcasted_iota(jnp.int32, (MIG, DH), 0), index_of(GRP)
+    for m in range(MIG):
+        moved = jnp.where((row == m) & (migration_ref[0, m] != group), 0.0, moved)
+    moved = moved.astype(BF16)
     for d in range(8):
         out_ref[d, :SLOTS] = own
         out_ref[d, SLOTS:] = moved
 
 
-def output_kernel(got_ref, weight_ref, target_ref, where_ref, keep_ref, send_ref):
-    first = where_ref[1] == 0
+def output_kernel(got_ref, weight_ref, place_ref, keep_ref, send_ref):
+    first = index_of("c") == 0
     moved = got_ref[0, SLOTS:].astype(F32)
     for i in range(1, 8):
         moved += got_ref[i, SLOTS:].astype(F32)
-    place = lax.broadcasted_iota(jnp.int32, (SLOTS, MIG), 0) == target_ref[...]
-    place = place.astype(F32)
+    place = place_ref[...]
     landed = jnp.dot(place.astype(BF16), moved.astype(BF16), preferred_element_type=F32)
     taken = jnp.sum(place, axis=1, keepdims=True) > 0.0
     last = jnp.where(taken, landed, got_ref[7, :SLOTS].astype(F32)).astype(BF16)
@@ -173,20 +192,20 @@
 
 
 def gate_kernel(
-    own_ref, other_ref, gate_ref, up_ref, router_ref, gain_ref, where_ref, out_ref, blocks_ref
+    own_ref, other_ref, gate_ref, up_ref, router_ref, gain_ref, out_ref, blocks_ref
 ):
-    first = where_ref[1] == 0
+    first = index_of("c") == 0
     own = own_ref[...].astype(F32).reshape(8 * SLOTS, HALF)
     other = other_ref[...].astype(F32).reshape(8 * SLOTS, HALF)
     rows = jnp.concatenate([jnp.where(first, own, other), jnp.where(first, other, own)], axis=1)
-    start = lax.broadcasted_iota(jnp.int32, (SLICE, CHUNK), 0) - CHUNK * where_ref[5]
+    start = lax.broadcasted_iota(jnp.int32, (SLICE, CHUNK), 0) - CHUNK * index_of(("zl", "c"))
     pick = (start == lax.broadcasted_iota(jnp.int32, (SLICE, CHUNK), 1)).astype(F32).astype(BF16)
     blocks = jnp.dot(rows.astype(BF16), pick, preferred_element_type=F32)
     blocks_ref[...] = blocks.astype(BF16).reshape(8, SLOTS, CHUNK)
-    rows, total = scaled_rows(rows, gain_ref, where_ref[0])
+    rows, total = scaled_rows(rows, gain_ref, index_of(GRP))
     gate = dot_nt(rows, gate_ref[:256])
     up = dot_nt(rows, up_ref[:256])
-    at = pl.multiple_of(where_ref[0] * SLICE, SLICE)
+    at = pl.multiple_of(index_of(GRP) * SLICE, SLICE)
     router = router_ref[:, pl.ds(at, SLICE)]
     rest = jnp.concatenate([gate_ref[256:], up_ref[256:], router, jnp.zeros_like(router)], axis=0)
     tail = dot_nt(rows, rest) + stats_lanes(total, 96)
@@ -195,8 +214,8 @@
     out_ref[:, :, 512:640] = tail.astype(BF16).reshape(8, SLOTS, 128)
 
 
-def hidden_kernel(got_ref, blocks_ref, ids_ref, slot_row_ref, where_ref, out_ref):
-    expert = where_ref[2]
+def hidden_kernel(got_ref, blocks_ref, ids_ref, slot_row_ref, out_ref):
+    expert = index_of(EPA) * UNITS // FF
     total = got_ref[0].astype(F32)
     for i in range(1, 8):
         total += got_ref[i].astype(F32)
@@ -206,9 +225,7 @@
     rest = silu(scale * tail[:, :32]) * (scale * tail[:, 32:64])
     logits = scale * tail[:, 64:96]
     place = lax.broadcasted_iota(jnp.int32, (SLOTS, SLOTS), 0) == slot_row_ref[...]
-    ids = jnp.dot(
-        place.astype(F32).astype(BF16), ids_ref[...].astype(F32).astype(BF16), preferred_element_type=F32
-    )
+    ids = dot_nt(place.astype(F32).astype(BF16), ids_ref[...].astype(F32).astype(BF16))
     ids = (ids + 0.5).astype(jnp.int32)
     at = lax.broadcasted_iota(jnp.int32, (SLOTS, 32), 1)
     lifted = []
@@ -224,12 +241,12 @@
         out_ref[d, :, 256:] = jnp.concatenate([rest, blocks_ref[d].astype(F32)], axis=1).astype(BF16)
 
 
-def down_kernel(got_ref, down_ref, where_ref, keep_ref, send_ref, resid_ref):
-    first = where_ref[1] == 0
+def down_kernel(got_ref, down_ref, keep_ref, send_ref, resid_ref):
+    first = index_of("c") == 0
     part = jnp.dot(
         got_ref[:, :, :UNITS].reshape(8 * SLOTS, UNITS), down_ref[...], preferred_element_type=F32
     )
-    resid_ref[...] = got_ref[where_ref[3], :, UNITS:]
+    resid_ref[...] = got_ref[index_of(("yh", "zh")), :, UNITS:]
     for pair in range(4):
         even = part[:, 192 * pair : 192 * pair + 96]
         odd = part[:, 192 * pair + 96 : 192 * pair + 192]
@@ -243,9 +260,9 @@
     for i in range(1, 32):
         total += got_ref[i].astype(F32)
     out = (resid_ref[...].astype(F32) + unpacked(total)).astype(BF16)
-    place = lax.broadcasted_iota(jnp.int32, (SLOTS, SLOTS), 1) == slot_ref[...]
-    out_ref[...] = jnp.dot(
-        place.astype(F32).astype(BF16), out, preferred_element_type=F32
+    place = lax.broadcasted_iota(jnp.int32, (SLOTS, SLOTS), 0) == slot_ref[...]
+    out_ref[...] = lax.dot_general(
+        place.astype(F32).astype(BF16), out, (((0,), (0,)), ((), ())), preferred_element_type=F32
     ).astype(BF16)
 
 
@@ -275,13 +292,7 @@
     row_slot,
     migration,
 ):
-    group = lax.axis_index(GRP).astype(jnp.int32)
-    core = lax.axis_index("c").astype(jnp.int32)
-    device = lax.axis_index(EPA).astype(jnp.int32)
-    expert = device * UNITS // FF
-    where = jnp.stack([group, core, expert, device // 8, device // 2, device % 8])
-    slot_row, slot_column = row_slot[None, :], row_slot[:, None]
-
+    slot_row, migration, expert_ids = row_slot[None, :], migration.T, expert_ids.T
     attn_gain, expert_gain = attn_gain.reshape(48, 128), expert_gain.reshape(48, 128)
 
     def merge(keep, send):
@@ -289,7 +300,7 @@
 
     spread = pl.pallas_call(
         sort_kernel,
-        out_shape=shape((32, *PACK), BF16),
+        out_shape=pltpu.VMEM((32, *PACK), BF16),
         in_specs=[HBM, HBM],
         out_specs=VMEM,
         scratch_shapes=[
@@ -304,13 +315,14 @@
     parts, block = pl.pallas_call(
         qkv_kernel,
         out_shape=(shape((8, SLOTS + MIG, 512), BF16), shape((8, HALF), F32)),
-        in_specs=[VMEM, VMEM, HBM, HBM, HBM, HBM, VMEM, SMEM],
+        in_specs=[VMEM, VMEM, HBM, HBM, HBM, HBM, HBM],
         out_specs=(VMEM, VMEM),
         scratch_shapes=[
             pltpu.VMEM((48, 128), F32),
             pltpu.VMEM((SLICE, 3 * DH), BF16),
             pltpu.VMEM((8 * SLOTS, HALF), F32),
-            pltpu.SemaphoreType.DMA((4,)),
+            pltpu.SMEM((3, MIG), jnp.int32),
+            pltpu.SemaphoreType.DMA((5,)),
         ],
         compiler_params=pltpu.CompilerParams(vmem_limit_bytes=16 << 20),
         name="qkv_parts",
@@ -321,26 +333,28 @@
         in_hbm(key_weight),
         in_hbm(value_weight),
         in_hbm(attn_gain),
-        migration[:, 2:3],
-        where,
+        in_hbm(migration),
     )
     parts = exchange(parts, GRP)
-    heads = pl.pallas_call(
+    heads, place = pl.pallas_call(
         attention_kernel,
-        out_shape=shape((8, SLOTS + MIG, DH), BF16),
-        in_specs=[VMEM, VMEM, VMEM, VMEM, SMEM, SMEM],
-        out_specs=VMEM,
-        scratch_shapes=[pltpu.VMEM((SLOTS + MIG, DH), F32)],
+        out_shape=(shape((8, SLOTS + MIG, DH), BF16), shape((SLOTS, MIG), F32)),
+        in_specs=[VMEM, VMEM, SMEM, HBM],
+        out_specs=(VMEM, VMEM),
+        scratch_shapes=[
+            pltpu.VMEM((SLOTS + MIG, DH), F32),
+            pltpu.SMEM((3, MIG), jnp.int32),
+            pltpu.SemaphoreType.DMA((1,)),
+        ],
         compiler_params=pltpu.CompilerParams(vmem_limit_bytes=16 << 20),
         name="attention",
-    )(parts, states[:, 0], migration[:, 0:1], decay_rate[None], migration, where)
+    )(parts, states[:, 0], decay_rate, in_hbm(migration))
     heads = exchange(heads, GRP)
     keep, send = call(
         output_kernel,
         (shape((32, 8, HALF), F32), shape((32, 8, HALF), BF16)),
-        (heads, output_weight, migration[:, 2][None, :], where),
+        (heads, output_weight, place),
         "output_parts",
-        smem=(3,),
     )
     spread = call(
         resid_kernel,
@@ -353,17 +367,15 @@
     parts, blocks = call(
         gate_kernel,
         (shape((8, SLOTS, 640), BF16), shape((8, SLOTS, CHUNK), BF16)),
-        (own, other, gate_weight.T, up_weight.T, router_weight.T, expert_gain, where),
+        (own, other, gate_weight.T, up_weight.T, router_weight.T, expert_gain),
         "gate_parts",
-        smem=(6,),
     )
     parts = exchange(parts, GRP)
     hidden = call(
         hidden_kernel,
         shape((8, SLOTS, UNITS + CHUNK), BF16),
-        (parts, blocks, expert_ids, slot_row, where),
+        (parts, blocks, expert_ids, slot_row),
         "hidden",
-        smem=(4,),
     )
     hidden = exchange(hidden, GRP)
     keep, send, resid = call(
@@ -373,16 +385,15 @@
             shape((8, 4, *PACK), BF16),
             shape((SLOTS, CHUNK), BF16),
         ),
-        (hidden, down_weight.T, where),
+        (hidden, down_weight.T),
         "down_parts",
-        smem=(2,),
     )
     parts = exchange(merge(keep, send), GRP)
     parts = exchange(parts.reshape(32, *PACK), CHIPS)
     return call(
         final_kernel,
         shape((SLOTS, CHUNK), BF16),
-        (parts, resid, slot_column),
+        (parts, resid, slot_row),
         "layer_out",
     )
 

time: 173 us -> 165 us (0.954)
  blocking collectives: 91.7 us -> 130 us
  waiting for transfers between devices: 37.5 us -> 12.8 us
  starting transfers between devices: 27.2 us -> 12.5 us
  Pallas kernels: 13.3 us -> 8.66 us
    all_to_all x6 -> x9, blocking collectives: 91.7 us -> 130 us  [exchange(): return lax.all_to_all(x, axes, 0, 0)]
    all_to_all x4 -> x1, waiting for transfers between devices: 32 us -> 7.17 us  [exchange(): return lax.all_to_all(x, axes, 0, 0)]
    all_to_all x4 -> x1, starting transfers between devices: 19.5 us -> 4.82 us  [exchange(): return lax.all_to_all(x, axes, 0, 0)]
    pallas_call x6, Pallas kernels: 6.29 us -> 3.42 us  [call(): pl.pallas_call(kernel, out_shape=outs, in_specs=specs, out_specs=jax.tree...]
  transfers between devices with their start and end apart: 8 -> 5, of which waited for: 8 -> 5; matrix products, arithmetic and copies ran while one was open for 1% -> 0% of each run, Pallas kernels for 0% -> 0%
where the time goes in v5:
time: 165 us
  blocking collectives  130 us (79%)
  waiting for transfers between devices  12.8 us (8%)
  starting transfers between devices  12.5 us (8%)
  Pallas kernels  8.66 us (5%)
    all_to_all x9, blocking collectives, exchange(): return lax.all_to_all(x, axes, 0, 0)  130 us
    all_to_all x1, waiting for transfers between devices, exchange(): return lax.all_to_all(x, axes, 0, 0)  7.17 us
    all_to_all x1, starting transfers between devices, exchange(): return lax.all_to_all(x, axes, 0, 0)  4.82 us
    ppermute x2, starting transfers between devices, merge(): return (keep + lax.ppermute(send, 'c', CORES).astype(F32)).astype(BF16)  3.83 us
    ppermute x2, starting transfers between devices, shards(): other = lax.ppermute(own, 'c', CORES)  3.82 us
    pallas_call x6, Pallas kernels, call(): pl.pallas_call(kernel, out_shape=outs, in_specs=specs, out_specs=jax.tree...  3.42 us
  transfers between devices with their start and end apart: 5, of which 5 were waited for; matrix products, arithmetic and copies ran while one was open for 0% of the time, Pallas kernels for 0%

profile of v5, /device:TPU:8, one launch (start us, length us, event | category | flops | bytes accessed | tf_op | source)
XLA Modules:
  0.0 164.8 jit_solution(1037341459586043842)
XLA Ops:
  0.0 1.1 sorted_rows.1
  1.1 28.3 %all_to_all.50 = bf16[32,24,128]{2,1,0:T(8,128)(2,1)S(1)} all-to-all(bf16[32,24,128]{2,1,0:T(8,128)(2,1)S(1)} %sorted_rows.1), channel_id=1, replica_groups=mesh['yl'=2,'x'=4,'yh'=4,'zh'=2,'zl'=4,'c'=2] {'yh','zh','zl'}, dimensions={0} | all-to-all | bytes 393216 | tf_op jit(solution)/shard_map/all_to_all | solution.py:274
  29.5 11.0 %all_to_all.51.own_ref = bf16[8,4,24,128]{3,2,1,0:T(8,128)(2,1)S(1)} all-to-all(bf16[8,4,24,128]{3,2,1,0:T(8,128)(2,1)S(1)} %bitcast.22), channel_id=1, replica_groups=mesh['yl'=2,'x'=4,'yh'=4,'zh'=2,'zl'=4,'c'=2] {'yl','x'}, dimensions={0} | all-to-all | bytes 393216 | tf_op jit(solution)/shard_map/all_to_all | solution.py:274
  40.5 1.9 %collective-permute-start = (bf16[8,4,24,128]{3,2,1,0:T(8,128)(2,1)S(1)}, bf16[8,4,24,128]{3,2,1,0:T(8,128)(2,1)S(1)}, u32[]{:S(2)}, u32[]{:S(2)}) collective-permute-start(bf16[8,4,24,128]{3,2,1,0:T(8,128)(2,1)S(1)} %all_to_all.51.own_ref), channel_id=1, source_target_pairs={{0,1},{1,0},{2,3},{3,2},{4,5},{5,4},{6,7},{7,6},{8,9},{9,8},{10,11... | collective-permute-start | bytes 589832 | tf_op jit(solution)/shard_map/ppermute | solution.py:314
  42.4 1.4 collective-permute-done.other_ref
  43.9 2.6 %qkv_parts.1 = (bf16[8,48,512]{2,1,0:T(8,128)(2,1)}, f32[8,384]{1,0:T(8,128)S(1)}) custom-call(bf16[8,4,24,128]{3,2,1,0:T(8,128)(2,1)S(1)} %all_to_all.51.own_ref, bf16[8,4,24,128]{3,2,1,0:T(8,128)(2,1)S(1)} %collective-permute-done.other_ref, bf16[768,128]{1,0:T(8,128)(2,1)} %q_ref.1, bf16[768,128]{1,0:T(8,128)(2,1)} %k_ref.1, bf16[768,128]{1,0:T(8,128)(2,1)} %v_ref.1, ...), custom_call_target="tpu_custom_call" | custom-call | tf_op jit(solution)/shard_map/qkv_parts/pallas_call | solution.py:315
  46.5 4.8 %all-to-all-start.2 = ((bf16[8,48,512]{2,1,0:T(8,128)(2,1)}), bf16[8,48,512]{2,1,0:T(8,128)(2,1)S(1)}, u32[]{:S(2)}, u32[]{:S(2)}) async-start(bf16[8,48,512]{2,1,0:T(8,128)(2,1)} %get-tuple-element.16), calls=%async_computation.2 | async-start | bytes 786432 | tf_op jit(solution)/shard_map/all_to_all | solution.py:274
  52.0 7.2 %all-to-all-done.2.got_ref = bf16[8,48,512]{2,1,0:T(8,128)(2,1)S(1)} async-done(((bf16[8,48,512]{2,1,0:T(8,128)(2,1)}), bf16[8,48,512]{2,1,0:T(8,128)(2,1)S(1)}, u32[]{:S(2)}, u32[]{:S(2)}) %all-to-all-start.2) | async-done | bytes 393248 | tf_op jit(solution)/shard_map/all_to_all | solution.py:274
  59.2 1.5 attention.1
  60.6 9.0 %all_to_all.52.got_ref = bf16[8,48,128]{2,1,0:T(8,128)(2,1)S(1)} all-to-all(bf16[8,48,128]{2,1,0:T(8,128)(2,1)S(1)} %get-tuple-element.17), channel_id=1, replica_groups=mesh['yl'=2,'x'=4,'yh'=4,'zh'=2,'zl'=4,'c'=2] {'yl','x'}, dimensions={0} | all-to-all | bytes 196608 | tf_op jit(solution)/shard_map/all_to_all | solution.py:274
  70.0 1.9 %collective-permute-start.1 = (bf16[32,8,384]{2,1,0:T(8,128)(2,1)S(1)}, bf16[32,8,384]{2,1,0:T(8,128)(2,1)S(1)}, u32[]{:S(2)}, u32[]{:S(2)}) collective-permute-start(bf16[32,8,384]{2,1,0:T(8,128)(2,1)S(1)} %get-tuple-element.20), channel_id=1, source_target_pairs={{0,1},{1,0},{2,3},{3,2},{4,5},{5,4},{6,7},{7,6},{8,9},{9,8},{10,11... | collective-permute-start | bytes 589832 | tf_op jit(solution)/shard_map/ppermute | solution.py:299
  71.9 1.4 collective-permute-done.1
  73.4 17.0 %all_to_all.53.got_ref = bf16[32,8,384]{2,1,0:T(8,128)(2,1)S(1)} all-to-all(bf16[32,8,384]{2,1,0:T(8,128)(2,1)S(1)} %add_convert_fusion.1), channel_id=1, replica_groups=mesh['yl'=2,'x'=4,'yh'=4,'zh'=2,'zl'=4,'c'=2] {'yh','zh','zl'}, dimensions={0} | all-to-all | bytes 393216 | tf_op jit(solution)/shard_map/all_to_all | solution.py:274
  90.5 17.4 %all_to_all.54.own_ref = bf16[32,8,384]{2,1,0:T(8,128)(2,1)S(1)} all-to-all(bf16[32,8,384]{2,1,0:T(8,128)(2,1)S(1)} %resid.1), channel_id=1, replica_groups=mesh['yl'=2,'x'=4,'yh'=4,'zh'=2,'zl'=4,'c'=2] {'yh','zh','zl'}, dimensions={0} | all-to-all | bytes 393216 | tf_op jit(solution)/shard_map/all_to_all | solution.py:274
  107.8 1.9 %collective-permute-start.2 = (bf16[32,8,384]{2,1,0:T(8,128)(2,1)S(1)}, bf16[32,8,384]{2,1,0:T(8,128)(2,1)S(1)}, u32[]{:S(2)}, u32[]{:S(2)}) collective-permute-start(bf16[32,8,384]{2,1,0:T(8,128)(2,1)S(1)} %all_to_all.54.own_ref), channel_id=1, source_target_pairs={{0,1},{1,0},{2,3},{3,2},{4,5},{5,4},{6,7},{7,6},{8,9},{9,8},{10,11... | collective-permute-start | bytes 589832 | tf_op jit(solution)/shard_map/ppermute | solution.py:366
  109.7 1.4 collective-permute-done.2.other_ref
  111.8 11.3 %all_to_all.55.got_ref = bf16[8,32,640]{2,1,0:T(8,128)(2,1)S(1)} all-to-all(bf16[8,32,640]{2,1,0:T(8,128)(2,1)S(1)} %get-tuple-element.22), channel_id=1, replica_groups=mesh['yl'=2,'x'=4,'yh'=4,'zh'=2,'zl'=4,'c'=2] {'yl','x'}, dimensions={0} | all-to-all | bytes 655360 | tf_op jit(solution)/shard_map/all_to_all | solution.py:274
  123.5 9.3 %all_to_all.56.got_ref = bf16[8,32,384]{2,1,0:T(8,128)(2,1)S(1)} all-to-all(bf16[8,32,384]{2,1,0:T(8,128)(2,1)S(1)} %hidden.1), channel_id=1, replica_groups=mesh['yl'=2,'x'=4,'yh'=4,'zh'=2,'zl'=4,'c'=2] {'yl','x'}, dimensions={0} | all-to-all | bytes 393216 | tf_op jit(solution)/shard_map/all_to_all | solution.py:274
  132.8 1.1 down_parts.1
  134.0 1.9 %collective-permute-start.3 = (bf16[8,4,24,128]{3,2,1,0:T(8,128)(2,1)S(1)}, bf16[8,4,24,128]{3,2,1,0:T(8,128)(2,1)S(1)}, u32[]{:S(2)}, u32[]{:S(2)}) collective-permute-start(bf16[8,4,24,128]{3,2,1,0:T(8,128)(2,1)S(1)} %get-tuple-element.25), channel_id=1, source_target_pairs={{0,1},{1,0},{2,3},{3,2},{4,5},{5,4},{6,7},{7,6},{8,9},{9,8},{10,11... | collective-permute-start | bytes 589832 | tf_op jit(solution)/shard_map/ppermute | solution.py:299
  135.9 1.4 collective-permute-done.3
  137.3 9.6 %all_to_all.57 = bf16[8,4,24,128]{3,2,1,0:T(8,128)(2,1)S(1)} all-to-all(bf16[8,4,24,128]{3,2,1,0:T(8,128)(2,1)S(1)} %add_convert_fusion), channel_id=1, replica_groups=mesh['yl'=2,'x'=4,'yh'=4,'zh'=2,'zl'=4,'c'=2] {'yl','x'}, dimensions={0} | all-to-all | bytes 393216 | tf_op jit(solution)/shard_map/all_to_all | solution.py:274
  146.9 17.0 %all_to_all.58.got_ref = bf16[32,24,128]{2,1,0:T(8,128)(2,1)S(1)} all-to-all(bf16[32,24,128]{2,1,0:T(8,128)(2,1)S(1)} %bitcast.23), channel_id=1, replica_groups=mesh['yl'=2,'x'=4,'yh'=4,'zh'=2,'zl'=4,'c'=2] {'yh','zh','zl'}, dimensions={0} | all-to-all | bytes 393216 | tf_op jit(solution)/shard_map/all_to_all | solution.py:274
  163.9 0.8 layer_out.1
  (24 shorter events, 1.6 us)
Async XLA Ops:
  0.0 59.1 %copy-start = (f32[32,1,128,128]{3,2,1,0:T(8,128)S(1)}, f32[32,1,128,128]{3,2,1,0:T(8,128)}, u32[]{:S(2)}) copy-start(f32[32,1,128,128]{3,2,1,0:T(8,128)} %param.28) | copy-start | bytes 6291460
  40.5 3.3 %collective-permute-start = (bf16[8,4,24,128]{3,2,1,0:T(8,128)(2,1)S(1)}, bf16[8,4,24,128]{3,2,1,0:T(8,128)(2,1)S(1)}, u32[]{:S(2)}, u32[]{:S(2)}) collective-permute-start(bf16[8,4,24,128]{3,2,1,0:T(8,128)(2,1)S(1)} %all_to_all.51.own_ref), channel_id=1, source_target_pairs={{0,1},{1,0},{2,3},{3,2},{4,5},{5,4},{6,7},{7,6},{8,9},{9,8},{10,11... | collective-permute-start | bytes 589832 | tf_op jit(solution)/shard_map/ppermute | solution.py:314
  43.9 25.8 %copy-start.5 = (bf16[768,128]{1,0:T(8,128)(2,1)S(1)}, bf16[768,128]{1,0:T(8,128)(2,1)}, u32[]{:S(2)}) copy-start(bf16[768,128]{1,0:T(8,128)(2,1)} %weight_ref.1) | copy-start | bytes 589828
  46.5 12.6 %all-to-all-start.2 = ((bf16[8,48,512]{2,1,0:T(8,128)(2,1)}), bf16[8,48,512]{2,1,0:T(8,128)(2,1)S(1)}, u32[]{:S(2)}, u32[]{:S(2)}) async-start(bf16[8,48,512]{2,1,0:T(8,128)(2,1)} %get-tuple-element.16), calls=%async_computation.2 | async-start | bytes 786432 | tf_op jit(solution)/shard_map/all_to_all | solution.py:274
  59.1 52.0 %copy-start.1 = (bf16[768,288]{0,1:T(8,128)(2,1)S(1)}, bf16[768,288]{0,1:T(8,128)(2,1)}, u32[]{:S(2)}) copy-start(bf16[768,288]{0,1:T(8,128)(2,1)} %param.21) | copy-start | bytes 1327108
  59.1 52.0 %copy-start.2 = (bf16[768,288]{0,1:T(8,128)(2,1)S(1)}, bf16[768,288]{0,1:T(8,128)(2,1)}, u32[]{:S(2)}) copy-start(bf16[768,288]{0,1:T(8,128)(2,1)} %param.22) | copy-start | bytes 1327108
  59.1 52.0 %copy-start.4 = (bf16[6144,32]{0,1:T(8,128)(2,1)S(1)}, bf16[6144,32]{0,1:T(8,128)(2,1)}, u32[]{:S(2)}) copy-start(bf16[6144,32]{0,1:T(8,128)(2,1)} %param.24) | copy-start | bytes 1179652
  59.1 52.0 %copy-start.6 = (f32[6144]{0:T(1024)S(1)}, f32[6144]{0:T(1024)}, u32[]{:S(2)}) copy-start(f32[6144]{0:T(1024)} %param.26) | copy-start | bytes 73732
  70.0 3.3 %collective-permute-start.1 = (bf16[32,8,384]{2,1,0:T(8,128)(2,1)S(1)}, bf16[32,8,384]{2,1,0:T(8,128)(2,1)S(1)}, u32[]{:S(2)}, u32[]{:S(2)}) collective-permute-start(bf16[32,8,384]{2,1,0:T(8,128)(2,1)S(1)} %get-tuple-element.20), channel_id=1, source_target_pairs={{0,1},{1,0},{2,3},{3,2},{4,5},{5,4},{6,7},{7,6},{8,9},{9,8},{10,11... | collective-permute-start | bytes 589832 | tf_op jit(solution)/shard_map/ppermute | solution.py:299
  73.3 49.7 %copy-start.7 = (s32[32]{0:T(128)S(1)}, s32[32]{0:T(128)}, u32[]{:S(2)}) copy-start(s32[32]{0:T(128)} %param.30) | copy-start | bytes 388
  73.3 49.7 %copy-start.8 = (s32[32,2]{0,1:T(2,128)S(1)}, s32[32,2]{0,1:T(2,128)}, u32[]{:S(2)}) copy-start(s32[32,2]{0,1:T(2,128)} %param.29) | copy-start | bytes 772
  90.4 42.4 %copy-start.3 = (bf16[768,288]{0,1:T(8,128)(2,1)S(1)}, bf16[768,288]{0,1:T(8,128)(2,1)}, u32[]{:S(2)}) copy-start(bf16[768,288]{0,1:T(8,128)(2,1)} %param.23) | copy-start | bytes 1327108
  107.8 3.3 %collective-permute-start.2 = (bf16[32,8,384]{2,1,0:T(8,128)(2,1)S(1)}, bf16[32,8,384]{2,1,0:T(8,128)(2,1)S(1)}, u32[]{:S(2)}, u32[]{:S(2)}) collective-permute-start(bf16[32,8,384]{2,1,0:T(8,128)(2,1)S(1)} %all_to_all.54.own_ref), channel_id=1, source_target_pairs={{0,1},{1,0},{2,3},{3,2},{4,5},{5,4},{6,7},{7,6},{8,9},{9,8},{10,11... | collective-permute-start | bytes 589832 | tf_op jit(solution)/shard_map/ppermute | solution.py:366
  134.0 3.3 %collective-permute-start.3 = (bf16[8,4,24,128]{3,2,1,0:T(8,128)(2,1)S(1)}, bf16[8,4,24,128]{3,2,1,0:T(8,128)(2,1)S(1)}, u32[]{:S(2)}, u32[]{:S(2)}) collective-permute-start(bf16[8,4,24,128]{3,2,1,0:T(8,128)(2,1)S(1)} %get-tuple-element.25), channel_id=1, source_target_pairs={{0,1},{1,0},{2,3},{3,2},{4,5},{5,4},{6,7},{7,6},{8,9},{9,8},{10,11... | collective-permute-start | bytes 589832 | tf_op jit(solution)/shard_map/ppermute | solution.py:299

commit v6 on v5

--- a/solution.py
+++ b/solution.py
@@ -66,24 +66,36 @@
     return copies
 
 
-def sort_kernel(tokens_ref, slot_ref, out_ref, held_ref, row_ref, sems):
-    for copy in fetch(((tokens_ref, held_ref), (slot_ref, row_ref)), sems):
-        copy.wait()
+def sort_kernel(
+    tokens_ref, slot_ref, q_ref, k_ref, v_ref, gain_ref, decay_ref,
+    out_ref, weight_ref, scale_ref, retain_ref, held_ref, row_ref, sems,
+):
+    pairs = [(ref, weight_ref.at[:, pl.ds(128 * i, 128)]) for i, ref in enumerate((q_ref, k_ref, v_ref))]
+    tokens, slots, *copies = fetch(
+        [(tokens_ref, held_ref), (slot_ref, row_ref), *pairs, (gain_ref, scale_ref)], sems
+    )
+    retain_ref[...] = jnp.broadcast_to(jnp.exp(-decay_ref[...]), retain_ref.shape)
+    tokens.wait()
+    slots.wait()
     place = lax.broadcasted_iota(jnp.int32, (SLOTS, SLOTS), 0) == row_ref[...]
     rows = packed(
         jnp.dot(place.astype(F32).astype(BF16), held_ref[...], preferred_element_type=F32)
     ).astype(BF16)
     for i in range(32):
         out_ref[i] = rows
-
-
-def chunk_rows(own_ref, other_ref, first):
-    pieces = []
-    for pair in range(4):
-        own = unpacked(own_ref[:, pair].astype(F32)).reshape(8 * SLOTS, CHUNK)
-        other = unpacked(other_ref[:, pair].astype(F32)).reshape(8 * SLOTS, CHUNK)
-        pieces += [jnp.where(first, own, other), jnp.where(first, other, own)]
-    return jnp.concatenate(pieces, axis=1)
+    for copy in copies:
+        copy.wait()
+
+
+def chunk_rows(got_ref):
+    return jnp.concatenate(
+        [
+            unpacked(got_ref[:, core, pair].astype(F32)).reshape(8 * SLOTS, CHUNK)
+            for pair in range(4)
+            for core in range(2)
+        ],
+        axis=1,
+    )
 
 
 def scaled_rows(rows, gain_ref, group):
@@ -110,21 +122,17 @@
 
 
 def qkv_kernel(
-    own_ref, other_ref, q_ref, k_ref, v_ref, gain_ref, listed_ref, out_ref, tokens_ref,
-    scale_ref, held_ref, half_ref, migration_ref, sems
+    got_ref, weight_ref, scale_ref, listed_ref, out_ref, tokens_ref, half_ref, migration_ref, sems
 ):
-    pairs = [(ref, held_ref.at[:, pl.ds(128 * i, 128)]) for i, ref in enumerate((q_ref, k_ref, v_ref))]
-    gain, *copies = fetch([(gain_ref, scale_ref), *pairs, (listed_ref, migration_ref)], sems)
+    (copy,) = fetch([(listed_ref, migration_ref)], sems)
     first = index_of("c") == 0
-    rows = chunk_rows(own_ref, other_ref, first)
+    rows = chunk_rows(got_ref)
     half_ref[...] = jnp.where(first, rows[:, :HALF], rows[:, HALF:])
     tokens_ref[...] = half_ref[pl.ds(pl.multiple_of(8 * index_of(CHIPS), 8), 8), :]
-    gain.wait()
     rows, total = scaled_rows(rows, scale_ref, index_of(GRP))
-    for copy in copies:
-        copy.wait()
-    parts = jnp.dot(rows, held_ref[...], preferred_element_type=F32)
+    parts = jnp.dot(rows, weight_ref[...], preferred_element_type=F32)
     parts = jnp.concatenate([parts, stats_lanes(total, 0)], axis=1).astype(BF16)
+    copy.wait()
     pick = targets(migration_ref).astype(BF16)
     moved = jnp.dot(pick, parts[7 * SLOTS :], preferred_element_type=F32).astype(BF16)
     out_ref[:, :SLOTS] = parts.reshape(8, SLOTS, 512)
@@ -133,7 +141,7 @@
 
 
 def attention_kernel(
-    got_ref, states_ref, decay_ref, listed_ref, out_ref, place_ref, o_ref, migration_ref, sems
+    got_ref, states_ref, retain_ref, listed_ref, out_ref, place_ref, o_ref, migration_ref, sems
 ):
     (copy,) = fetch([(listed_ref, migration_ref)], sems)
     total = got_ref[0].astype(F32)
@@ -153,8 +161,7 @@
         o_ref[s : s + 1, :] = jnp.sum(
             turned[:, s : s + 1] * states_ref[migration_ref[1, m]], axis=0, keepdims=True
         )
-    retain = jnp.exp(jnp.full((1, DH), -decay_ref[0], F32))
-    mixed = retain * o_ref[...] + jnp.sum(q * k, axis=1, keepdims=True) * v
+    mixed = retain_ref[:1] * o_ref[...] + jnp.sum(q * k, axis=1, keepdims=True) * v
     heads = mixed * lax.rsqrt(jnp.mean(mixed * mixed, axis=1, keepdims=True) + EPS)
     own, moved = heads[:SLOTS].astype(BF16), heads[SLOTS:]
     row, group = lax.broadcasted_iota(jnp.int32, (MIG, DH), 0), index_of(GRP)
@@ -241,18 +248,18 @@
         out_ref[d, :, 256:] = jnp.concatenate([rest, blocks_ref[d].astype(F32)], axis=1).astype(BF16)
 
 
-def down_kernel(got_ref, down_ref, keep_ref, send_ref, resid_ref):
-    first = index_of("c") == 0
+def down_kernel(got_ref, down_ref, out_ref, resid_ref):
     part = jnp.dot(
         got_ref[:, :, :UNITS].reshape(8 * SLOTS, UNITS), down_ref[...], preferred_element_type=F32
     )
     resid_ref[...] = got_ref[index_of(("yh", "zh")), :, UNITS:]
-    for pair in range(4):
-        even = part[:, 192 * pair : 192 * pair + 96]
-        odd = part[:, 192 * pair + 96 : 192 * pair + 192]
-        keep_ref[:, pair] = packed(jnp.where(first, even, odd).reshape(8, SLOTS, CHUNK))
-        sent = packed(jnp.where(first, odd, even).reshape(8, SLOTS, CHUNK))
-        send_ref[:, pair] = sent.astype(BF16)
+    for chunk in range(8):
+        rows = part[:, CHUNK * chunk : CHUNK * chunk + CHUNK].reshape(8, SLOTS, CHUNK)
+        out_ref[:, chunk % 2, chunk // 2] = packed(rows).astype(BF16)
+
+
+def pair_kernel(got_ref, out_ref):
+    out_ref[...] = (got_ref[:, 0].astype(F32) + got_ref[:, 1].astype(F32)).astype(BF16)
 
 
 def final_kernel(got_ref, resid_ref, slot_ref, out_ref):
@@ -298,48 +305,44 @@
     def merge(keep, send):
         return (keep + lax.ppermute(send, "c", CORES).astype(F32)).astype(BF16)
 
-    spread = pl.pallas_call(
+    spread, weight, scale, retain = pl.pallas_call(
         sort_kernel,
-        out_shape=pltpu.VMEM((32, *PACK), BF16),
-        in_specs=[HBM, HBM],
-        out_specs=VMEM,
+        out_shape=(
+            pltpu.VMEM((32, *PACK), BF16),
+            pltpu.VMEM((SLICE, 3 * DH), BF16),
+            pltpu.VMEM((48, 128), F32),
+            pltpu.VMEM((8, DH), F32),
+        ),
+        in_specs=[HBM] * 6 + [VMEM],
+        out_specs=(VMEM,) * 4,
         scratch_shapes=[
             pltpu.VMEM((SLOTS, CHUNK), BF16),
             pltpu.VMEM((1, SLOTS), jnp.int32),
-            pltpu.SemaphoreType.DMA((2,)),
+            pltpu.SemaphoreType.DMA((6,)),
         ],
         name="sorted_rows",
-    )(in_hbm(tokens), in_hbm(slot_row))
-    own = exchange(exchange(spread, CHIPS).reshape(8, 4, *PACK), GRP)
-    other = lax.ppermute(own, "c", CORES)
+    )(*map(in_hbm, (tokens, slot_row, query_weight, key_weight, value_weight, attn_gain)), decay_rate[None])
+    got = exchange(spread, CHIPS).reshape(8, 1, 4, *PACK)
+    got = jnp.broadcast_to(got, (8, 2, 4, *PACK)).reshape(16, 4, *PACK)
+    got = exchange(got, GRP + ("c",)).reshape(8, 2, 4, *PACK)
     parts, block = pl.pallas_call(
         qkv_kernel,
         out_shape=(shape((8, SLOTS + MIG, 512), BF16), shape((8, HALF), F32)),
-        in_specs=[VMEM, VMEM, HBM, HBM, HBM, HBM, HBM],
+        in_specs=[VMEM, VMEM, VMEM, HBM],
         out_specs=(VMEM, VMEM),
         scratch_shapes=[
-            pltpu.VMEM((48, 128), F32),
-            pltpu.VMEM((SLICE, 3 * DH), BF16),
             pltpu.VMEM((8 * SLOTS, HALF), F32),
             pltpu.SMEM((3, MIG), jnp.int32),
-            pltpu.SemaphoreType.DMA((5,)),
+            pltpu.SemaphoreType.DMA((1,)),
         ],
         compiler_params=pltpu.CompilerParams(vmem_limit_bytes=16 << 20),
         name="qkv_parts",
-    )(
-        own,
-        other,
-        in_hbm(query_weight),
-        in_hbm(key_weight),
-        in_hbm(value_weight),
-        in_hbm(attn_gain),
-        in_hbm(migration),
-    )
+    )(got, weight, scale, in_hbm(migration))
     parts = exchange(parts, GRP)
     heads, place = pl.pallas_call(
         attention_kernel,
         out_shape=(shape((8, SLOTS + MIG, DH), BF16), shape((SLOTS, MIG), F32)),
-        in_specs=[VMEM, VMEM, SMEM, HBM],
+        in_specs=[VMEM, VMEM, VMEM, HBM],
         out_specs=(VMEM, VMEM),
         scratch_shapes=[
             pltpu.VMEM((SLOTS + MIG, DH), F32),
@@ -348,7 +351,7 @@
         ],
         compiler_params=pltpu.CompilerParams(vmem_limit_bytes=16 << 20),
         name="attention",
-    )(parts, states[:, 0], decay_rate, in_hbm(migration))
+    )(parts, states[:, 0], retain, in_hbm(migration))
     heads = exchange(heads, GRP)
     keep, send = call(
         output_kernel,
@@ -378,17 +381,14 @@
         "hidden",
     )
     hidden = exchange(hidden, GRP)
-    keep, send, resid = call(
+    parts, resid = call(
         down_kernel,
-        (
-            shape((8, 4, *PACK), F32),
-            shape((8, 4, *PACK), BF16),
-            shape((SLOTS, CHUNK), BF16),
-        ),
+        (shape((8, 2, 4, *PACK), BF16), shape((SLOTS, CHUNK), BF16)),
         (hidden, down_weight.T),
         "down_parts",
     )
-    parts = exchange(merge(keep, send), GRP)
+    parts = exchange(parts.reshape(16, 4, *PACK), GRP + ("c",)).reshape(8, 2, 4, *PACK)
+    parts = call(pair_kernel, shape((8, 4, *PACK), BF16), (parts,), "pair_sum")
     parts = exchange(parts.reshape(32, *PACK), CHIPS)
     return call(
         final_kernel,

time: 165 us -> 162 us (0.982)
  blocking collectives: 130 us -> 147 us
  waiting for transfers between devices: 12.8 us -> 2.81 us
  starting transfers between devices: 12.5 us -> 3.83 us
    all_to_all x9 -> x10, blocking collectives: 130 us -> 147 us  [exchange(): return lax.all_to_all(x, axes, 0, 0)]
    all_to_all x1 -> x0, waiting for transfers between devices: 7.17 us -> none  [exchange(): return lax.all_to_all(x, axes, 0, 0)]
    all_to_all x1 -> x0, starting transfers between devices: 4.82 us -> none  [exchange(): return lax.all_to_all(x, axes, 0, 0)]
    ppermute x2 -> x1, starting transfers between devices: 3.83 us -> 1.92 us  [merge(): return (keep + lax.ppermute(send, 'c', CORES).astype(F32)).astype(BF16)]
    ppermute x2 -> x1, starting transfers between devices: 3.82 us -> 1.91 us  [shards(): other = lax.ppermute(own, 'c', CORES)]
    pallas_call x6 -> x7, Pallas kernels: 3.42 us -> 2.9 us  [call(): pl.pallas_call(kernel, out_shape=outs, in_specs=specs, out_specs=jax.tree...]
  transfers between devices with their start and end apart: 5 -> 2, of which waited for: 5 -> 2; matrix products, arithmetic and copies ran while one was open for 0% -> 0% of each run, Pallas kernels for 0% -> 0%
where the time goes in v6:
time: 162 us; the launch traced here: 161 us
  blocking collectives  147 us (91%)
  Pallas kernels  7.17 us (4%)
  starting transfers between devices  3.83 us (2%)
  waiting for transfers between devices  2.81 us (2%)
    all_to_all x10, blocking collectives, exchange(): return lax.all_to_all(x, axes, 0, 0)  147 us
  transfers between devices with their start and end apart: 2, of which 2 were waited for; matrix products, arithmetic and copies ran while one was open for 0% of the time, Pallas kernels for 0%

profile of v6, /device:TPU:8, one launch (start us, length us, event | category | flops | bytes accessed | tf_op | source)
XLA Modules:
  0.0 161.5 jit_solution(9257633245172704797)
XLA Ops:
  0.7 1.4 sorted_rows.1
  2.0 28.3 %all_to_all.50 = bf16[32,24,128]{2,1,0:T(8,128)(2,1)S(1)} all-to-all(bf16[32,24,128]{2,1,0:T(8,128)(2,1)S(1)} %get-tuple-element.19), channel_id=1, replica_groups=mesh['yl'=2,'x'=4,'yh'=4,'zh'=2,'zl'=4,'c'=2] {'yh','zh','zl'}, dimensions={0} | all-to-all | bytes 393216 | tf_op jit(solution)/shard_map/all_to_all | solution.py:281
  30.4 0.1 broadcast_in_dim.16
  30.4 13.7 %all_to_all.51 = bf16[16,4,24,128]{3,2,1,0:T(8,128)(2,1)S(1)} all-to-all(bf16[16,4,24,128]{3,2,1,0:T(8,128)(2,1)S(1)} %bitcast.32), channel_id=1, replica_groups=mesh['yl'=2,'x'=4,'yh'=4,'zh'=2,'zl'=4,'c'=2] {'yl','x','c'}, dimensions={0} | all-to-all | bytes 786432 | tf_op jit(solution)/shard_map/all_to_all | solution.py:281
  44.1 1.4 qkv_parts.1
  45.5 11.5 %all_to_all.52.got_ref = bf16[8,48,512]{2,1,0:T(8,128)(2,1)S(1)} all-to-all(bf16[8,48,512]{2,1,0:T(8,128)(2,1)S(1)} %get-tuple-element.22), channel_id=1, replica_groups=mesh['yl'=2,'x'=4,'yh'=4,'zh'=2,'zl'=4,'c'=2] {'yl','x'}, dimensions={0} | all-to-all | bytes 786432 | tf_op jit(solution)/shard_map/all_to_all | solution.py:281
  57.1 1.5 attention.1
  58.6 8.9 %all_to_all.53.got_ref = bf16[8,48,128]{2,1,0:T(8,128)(2,1)S(1)} all-to-all(bf16[8,48,128]{2,1,0:T(8,128)(2,1)S(1)} %get-tuple-element.24), channel_id=1, replica_groups=mesh['yl'=2,'x'=4,'yh'=4,'zh'=2,'zl'=4,'c'=2] {'yl','x'}, dimensions={0} | all-to-all | bytes 196608 | tf_op jit(solution)/shard_map/all_to_all | solution.py:281
  67.5 0.3 output_parts.1
  67.9 1.9 %collective-permute-start = (bf16[32,8,384]{2,1,0:T(8,128)(2,1)S(1)}, bf16[32,8,384]{2,1,0:T(8,128)(2,1)S(1)}, u32[]{:S(2)}, u32[]{:S(2)}) collective-permute-start(bf16[32,8,384]{2,1,0:T(8,128)(2,1)S(1)} %get-tuple-element.27), channel_id=1, source_target_pairs={{0,1},{1,0},{2,3},{3,2},{4,5},{5,4},{6,7},{7,6},{8,9},{9,8},{10,11... | collective-permute-start | bytes 589832 | tf_op jit(solution)/shard_map/ppermute | solution.py:306
  69.8 1.4 collective-permute-done
  71.3 17.0 %all_to_all.54.got_ref = bf16[32,8,384]{2,1,0:T(8,128)(2,1)S(1)} all-to-all(bf16[32,8,384]{2,1,0:T(8,128)(2,1)S(1)} %add_convert_fusion), channel_id=1, replica_groups=mesh['yl'=2,'x'=4,'yh'=4,'zh'=2,'zl'=4,'c'=2] {'yh','zh','zl'}, dimensions={0} | all-to-all | bytes 393216 | tf_op jit(solution)/shard_map/all_to_all | solution.py:281
  88.3 0.1 resid.1
  88.3 17.3 %all_to_all.55.own_ref = bf16[32,8,384]{2,1,0:T(8,128)(2,1)S(1)} all-to-all(bf16[32,8,384]{2,1,0:T(8,128)(2,1)S(1)} %resid.1), channel_id=1, replica_groups=mesh['yl'=2,'x'=4,'yh'=4,'zh'=2,'zl'=4,'c'=2] {'yh','zh','zl'}, dimensions={0} | all-to-all | bytes 393216 | tf_op jit(solution)/shard_map/all_to_all | solution.py:281
  105.7 1.9 %collective-permute-start.1 = (bf16[32,8,384]{2,1,0:T(8,128)(2,1)S(1)}, bf16[32,8,384]{2,1,0:T(8,128)(2,1)S(1)}, u32[]{:S(2)}, u32[]{:S(2)}) collective-permute-start(bf16[32,8,384]{2,1,0:T(8,128)(2,1)S(1)} %all_to_all.55.own_ref), channel_id=1, source_target_pairs={{0,1},{1,0},{2,3},{3,2},{4,5},{5,4},{6,7},{7,6},{8,9},{9,8},{10,11... | collective-permute-start | bytes 589832 | tf_op jit(solution)/shard_map/ppermute | solution.py:369
  107.6 1.4 collective-permute-done.1.other_ref
  109.0 0.6 gate_parts.1
  109.6 11.3 %all_to_all.56.got_ref = bf16[8,32,640]{2,1,0:T(8,128)(2,1)S(1)} all-to-all(bf16[8,32,640]{2,1,0:T(8,128)(2,1)S(1)} %get-tuple-element.29), channel_id=1, replica_groups=mesh['yl'=2,'x'=4,'yh'=4,'zh'=2,'zl'=4,'c'=2] {'yl','x'}, dimensions={0} | all-to-all | bytes 655360 | tf_op jit(solution)/shard_map/all_to_all | solution.py:281
  121.0 0.5 hidden.1
  121.4 9.3 %all_to_all.57.got_ref = bf16[8,32,384]{2,1,0:T(8,128)(2,1)S(1)} all-to-all(bf16[8,32,384]{2,1,0:T(8,128)(2,1)S(1)} %hidden.1), channel_id=1, replica_groups=mesh['yl'=2,'x'=4,'yh'=4,'zh'=2,'zl'=4,'c'=2] {'yl','x'}, dimensions={0} | all-to-all | bytes 393216 | tf_op jit(solution)/shard_map/all_to_all | solution.py:281
  130.7 0.6 down_parts.1
  131.3 12.1 %all_to_all.58 = bf16[16,4,24,128]{3,2,1,0:T(8,128)(2,1)S(1)} all-to-all(bf16[16,4,24,128]{3,2,1,0:T(8,128)(2,1)S(1)} %bitcast.25), channel_id=1, replica_groups=mesh['yl'=2,'x'=4,'yh'=4,'zh'=2,'zl'=4,'c'=2] {'yl','x','c'}, dimensions={0} | all-to-all | bytes 786432 | tf_op jit(solution)/shard_map/all_to_all | solution.py:281
  143.4 17.2 %all_to_all.59.got_ref = bf16[32,24,128]{2,1,0:T(8,128)(2,1)S(1)} all-to-all(bf16[32,24,128]{2,1,0:T(8,128)(2,1)S(1)} %bitcast.21), channel_id=1, replica_groups=mesh['yl'=2,'x'=4,'yh'=4,'zh'=2,'zl'=4,'c'=2] {'yh','zh','zl'}, dimensions={0} | all-to-all | bytes 393216 | tf_op jit(solution)/shard_map/all_to_all | solution.py:281
  160.6 0.8 layer_out.1
  (20 shorter events, 0.1 us)
Async XLA Ops:
  0.7 56.4 %copy-start = (f32[32,1,128,128]{3,2,1,0:T(8,128)S(1)}, f32[32,1,128,128]{3,2,1,0:T(8,128)}, u32[]{:S(2)}) copy-start(f32[32,1,128,128]{3,2,1,0:T(8,128)} %param.28) | copy-start | bytes 6291460
  44.1 23.5 %copy-start.5 = (bf16[768,128]{1,0:T(8,128)(2,1)S(1)}, bf16[768,128]{1,0:T(8,128)(2,1)}, u32[]{:S(2)}) copy-start(bf16[768,128]{1,0:T(8,128)(2,1)} %weight_ref.1) | copy-start | bytes 589828
  57.1 51.9 %copy-start.1 = (bf16[768,288]{0,1:T(8,128)(2,1)S(1)}, bf16[768,288]{0,1:T(8,128)(2,1)}, u32[]{:S(2)}) copy-start(bf16[768,288]{0,1:T(8,128)(2,1)} %param.21) | copy-start | bytes 1327108
  57.1 51.9 %copy-start.2 = (bf16[768,288]{0,1:T(8,128)(2,1)S(1)}, bf16[768,288]{0,1:T(8,128)(2,1)}, u32[]{:S(2)}) copy-start(bf16[768,288]{0,1:T(8,128)(2,1)} %param.22) | copy-start | bytes 1327108
  57.1 51.9 %copy-start.4 = (bf16[6144,32]{0,1:T(8,128)(2,1)S(1)}, bf16[6144,32]{0,1:T(8,128)(2,1)}, u32[]{:S(2)}) copy-start(bf16[6144,32]{0,1:T(8,128)(2,1)} %param.24) | copy-start | bytes 1179652
  57.1 51.9 %copy-start.6 = (f32[6144]{0:T(1024)S(1)}, f32[6144]{0:T(1024)}, u32[]{:S(2)}) copy-start(f32[6144]{0:T(1024)} %param.26) | copy-start | bytes 73732
  67.9 3.3 %collective-permute-start = (bf16[32,8,384]{2,1,0:T(8,128)(2,1)S(1)}, bf16[32,8,384]{2,1,0:T(8,128)(2,1)S(1)}, u32[]{:S(2)}, u32[]{:S(2)}) collective-permute-start(bf16[32,8,384]{2,1,0:T(8,128)(2,1)S(1)} %get-tuple-element.27), channel_id=1, source_target_pairs={{0,1},{1,0},{2,3},{3,2},{4,5},{5,4},{6,7},{7,6},{8,9},{9,8},{10,11... | collective-permute-start | bytes 589832 | tf_op jit(solution)/shard_map/ppermute | solution.py:306
  71.2 49.7 %copy-start.7 = (s32[32]{0:T(128)S(1)}, s32[32]{0:T(128)}, u32[]{:S(2)}) copy-start(s32[32]{0:T(128)} %param.30) | copy-start | bytes 388
  71.2 49.7 %copy-start.8 = (s32[32,2]{0,1:T(2,128)S(1)}, s32[32,2]{0,1:T(2,128)}, u32[]{:S(2)}) copy-start(s32[32,2]{0,1:T(2,128)} %param.29) | copy-start | bytes 772
  88.3 42.4 %copy-start.3 = (bf16[768,288]{0,1:T(8,128)(2,1)S(1)}, bf16[768,288]{0,1:T(8,128)(2,1)}, u32[]{:S(2)}) copy-start(bf16[768,288]{0,1:T(8,128)(2,1)} %param.23) | copy-start | bytes 1327108
  105.7 3.3 %collective-permute-start.1 = (bf16[32,8,384]{2,1,0:T(8,128)(2,1)S(1)}, bf16[32,8,384]{2,1,0:T(8,128)(2,1)S(1)}, u32[]{:S(2)}, u32[]{:S(2)}) collective-permute-start(bf16[32,8,384]{2,1,0:T(8,128)(2,1)S(1)} %all_to_all.55.own_ref), channel_id=1, source_target_pairs={{0,1},{1,0},{2,3},{3,2},{4,5},{5,4},{6,7},{7,6},{8,9},{9,8},{10,11... | collective-permute-start | bytes 589832 | tf_op jit(solution)/shard_map/ppermute | solution.py:369

commit v7 on v6

--- a/solution.py
+++ b/solution.py
@@ -67,14 +67,13 @@
 
 
 def sort_kernel(
-    tokens_ref, slot_ref, q_ref, k_ref, v_ref, gain_ref, decay_ref,
-    out_ref, weight_ref, scale_ref, retain_ref, held_ref, row_ref, sems,
+    tokens_ref, slot_ref, q_ref, k_ref, v_ref, gain_ref,
+    out_ref, weight_ref, scale_ref, held_ref, row_ref, sems,
 ):
     pairs = [(ref, weight_ref.at[:, pl.ds(128 * i, 128)]) for i, ref in enumerate((q_ref, k_ref, v_ref))]
     tokens, slots, *copies = fetch(
         [(tokens_ref, held_ref), (slot_ref, row_ref), *pairs, (gain_ref, scale_ref)], sems
     )
-    retain_ref[...] = jnp.broadcast_to(jnp.exp(-decay_ref[...]), retain_ref.shape)
     tokens.wait()
     slots.wait()
     place = lax.broadcasted_iota(jnp.int32, (SLOTS, SLOTS), 0) == row_ref[...]
@@ -122,7 +121,7 @@
 
 
 def qkv_kernel(
-    got_ref, weight_ref, scale_ref, listed_ref, out_ref, tokens_ref, half_ref, migration_ref, sems
+    got_ref, weight_ref, scale_ref, listed_ref, decay_ref, out_ref, tokens_ref, retain_ref, half_ref, migration_ref, sems
 ):
     (copy,) = fetch([(listed_ref, migration_ref)], sems)
     first = index_of("c") == 0
@@ -130,6 +129,7 @@
     half_ref[...] = jnp.where(first, rows[:, :HALF], rows[:, HALF:])
     tokens_ref[...] = half_ref[pl.ds(pl.multiple_of(8 * index_of(CHIPS), 8), 8), :]
     rows, total = scaled_rows(rows, scale_ref, index_of(GRP))
+    retain_ref[...] = jnp.broadcast_to(jnp.exp(-decay_ref[...]), retain_ref.shape)
     parts = jnp.dot(rows, weight_ref[...], preferred_element_type=F32)
     parts = jnp.concatenate([parts, stats_lanes(total, 0)], axis=1).astype(BF16)
     copy.wait()
@@ -305,31 +305,30 @@
     def merge(keep, send):
         return (keep + lax.ppermute(send, "c", CORES).astype(F32)).astype(BF16)
 
-    spread, weight, scale, retain = pl.pallas_call(
+    spread, weight, scale = pl.pallas_call(
         sort_kernel,
         out_shape=(
             pltpu.VMEM((32, *PACK), BF16),
             pltpu.VMEM((SLICE, 3 * DH), BF16),
             pltpu.VMEM((48, 128), F32),
-            pltpu.VMEM((8, DH), F32),
         ),
-        in_specs=[HBM] * 6 + [VMEM],
-        out_specs=(VMEM,) * 4,
+        in_specs=[HBM] * 6,
+        out_specs=(VMEM,) * 3,
         scratch_shapes=[
             pltpu.VMEM((SLOTS, CHUNK), BF16),
             pltpu.VMEM((1, SLOTS), jnp.int32),
             pltpu.SemaphoreType.DMA((6,)),
         ],
         name="sorted_rows",
-    )(*map(in_hbm, (tokens, slot_row, query_weight, key_weight, value_weight, attn_gain)), decay_rate[None])
+    )(*map(in_hbm, (tokens, slot_row, query_weight, key_weight, value_weight, attn_gain)))
     got = exchange(spread, CHIPS).reshape(8, 1, 4, *PACK)
     got = jnp.broadcast_to(got, (8, 2, 4, *PACK)).reshape(16, 4, *PACK)
     got = exchange(got, GRP + ("c",)).reshape(8, 2, 4, *PACK)
-    parts, block = pl.pallas_call(
+    parts, block, retain = pl.pallas_call(
         qkv_kernel,
-        out_shape=(shape((8, SLOTS + MIG, 512), BF16), shape((8, HALF), F32)),
-        in_specs=[VMEM, VMEM, VMEM, HBM],
-        out_specs=(VMEM, VMEM),
+        out_shape=(shape((8, SLOTS + MIG, 512), BF16), shape((8, HALF), F32), shape((8, DH), F32)),
+        in_specs=[VMEM, VMEM, VMEM, HBM, VMEM],
+        out_specs=(VMEM,) * 3,
         scratch_shapes=[
             pltpu.VMEM((8 * SLOTS, HALF), F32),
             pltpu.SMEM((3, MIG), jnp.int32),
@@ -337,7 +336,7 @@
         ],
         compiler_params=pltpu.CompilerParams(vmem_limit_bytes=16 << 20),
         name="qkv_parts",
-    )(got, weight, scale, in_hbm(migration))
+    )(got, weight, scale, in_hbm(migration), decay_rate[None])
     parts = exchange(parts, GRP)
     heads, place = pl.pallas_call(
         attention_kernel,

time: 162 us -> 162 us (level)
  blocking collectives: 147 us -> 133 us
  waiting for transfers between devices: 2.81 us -> 10.3 us
  starting transfers between devices: 3.83 us -> 9.61 us
    all_to_all x10 -> x9, blocking collectives: 147 us -> 133 us  [exchange(): return lax.all_to_all(x, axes, 0, 0)]
    all_to_all x0 -> x1, waiting for transfers between devices: none -> 7.44 us  [exchange(): return lax.all_to_all(x, axes, 0, 0)]
    all_to_all x0 -> x1, starting transfers between devices: none -> 5.78 us  [exchange(): return lax.all_to_all(x, axes, 0, 0)]
  transfers between devices with their start and end apart: 2 -> 3, of which waited for: 2 -> 3; matrix products, arithmetic and copies ran while one was open for 0% -> 0% of each run, Pallas kernels for 0% -> 0%
where the time goes in v7:
time: 162 us
  blocking collectives  133 us (82%)
  waiting for transfers between devices  10.3 us (6%)
  starting transfers between devices  9.61 us (6%)
  Pallas kernels  7.2 us (4%)
    all_to_all x9, blocking collectives, exchange(): return lax.all_to_all(x, axes, 0, 0)  133 us
    all_to_all x1, waiting for transfers between devices, exchange(): return lax.all_to_all(x, axes, 0, 0)  7.44 us
    all_to_all x1, starting transfers between devices, exchange(): return lax.all_to_all(x, axes, 0, 0)  5.78 us
  transfers between devices with their start and end apart: 3, of which 3 were waited for; matrix products, arithmetic and copies ran while one was open for 0% of the time, Pallas kernels for 0%

profile of v7, /device:TPU:8, one launch (start us, length us, event | category | flops | bytes accessed | tf_op | source)
XLA Modules:
  0.0 161.8 jit_solution(15459858052779282022)
XLA Ops:
  0.0 1.3 sorted_rows.1
  1.4 28.3 %all_to_all.50 = bf16[32,24,128]{2,1,0:T(8,128)(2,1)S(1)} all-to-all(bf16[32,24,128]{2,1,0:T(8,128)(2,1)S(1)} %get-tuple-element.19), channel_id=1, replica_groups=mesh['yl'=2,'x'=4,'yh'=4,'zh'=2,'zl'=4,'c'=2] {'yh','zh','zl'}, dimensions={0} | all-to-all | bytes 393216 | tf_op jit(solution)/shard_map/all_to_all | solution.py:281
  29.7 0.8 broadcast_in_dim.15
  30.5 5.8 %all-to-all-start.1 = ((bf16[16,4,24,128]{3,2,1,0:T(8,128)(2,1)}), bf16[16,4,24,128]{3,2,1,0:T(8,128)(2,1)S(1)}, u32[]{:S(2)}, u32[]{:S(2)}) async-start(bf16[16,4,24,128]{3,2,1,0:T(8,128)(2,1)} %bitcast.3), calls=%async_computation.1 | async-start | bytes 786432 | tf_op jit(solution)/shard_map/all_to_all | solution.py:281
  36.9 7.4 %all-to-all-done.1 = bf16[16,4,24,128]{3,2,1,0:T(8,128)(2,1)S(1)} async-done(((bf16[16,4,24,128]{3,2,1,0:T(8,128)(2,1)}), bf16[16,4,24,128]{3,2,1,0:T(8,128)(2,1)S(1)}, u32[]{:S(2)}, u32[]{:S(2)}) %all-to-all-start.1) | async-done | bytes 393248 | tf_op jit(solution)/shard_map/all_to_all | solution.py:281
  44.4 1.4 qkv_parts.1
  45.8 11.6 %all_to_all.51.got_ref = bf16[8,48,512]{2,1,0:T(8,128)(2,1)S(1)} all-to-all(bf16[8,48,512]{2,1,0:T(8,128)(2,1)S(1)} %get-tuple-element.22), channel_id=1, replica_groups=mesh['yl'=2,'x'=4,'yh'=4,'zh'=2,'zl'=4,'c'=2] {'yl','x'}, dimensions={0} | all-to-all | bytes 786432 | tf_op jit(solution)/shard_map/all_to_all | solution.py:281
  57.4 1.5 attention.1
  58.9 8.9 %all_to_all.52.got_ref = bf16[8,48,128]{2,1,0:T(8,128)(2,1)S(1)} all-to-all(bf16[8,48,128]{2,1,0:T(8,128)(2,1)S(1)} %get-tuple-element.24), channel_id=1, replica_groups=mesh['yl'=2,'x'=4,'yh'=4,'zh'=2,'zl'=4,'c'=2] {'yl','x'}, dimensions={0} | all-to-all | bytes 196608 | tf_op jit(solution)/shard_map/all_to_all | solution.py:281
  67.9 0.3 output_parts.1
  68.2 1.9 %collective-permute-start = (bf16[32,8,384]{2,1,0:T(8,128)(2,1)S(1)}, bf16[32,8,384]{2,1,0:T(8,128)(2,1)S(1)}, u32[]{:S(2)}, u32[]{:S(2)}) collective-permute-start(bf16[32,8,384]{2,1,0:T(8,128)(2,1)S(1)} %get-tuple-element.27), channel_id=1, source_target_pairs={{0,1},{1,0},{2,3},{3,2},{4,5},{5,4},{6,7},{7,6},{8,9},{9,8},{10,11... | collective-permute-start | bytes 589832 | tf_op jit(solution)/shard_map/ppermute | solution.py:306
  70.1 1.4 collective-permute-done
  71.6 17.0 %all_to_all.53.got_ref = bf16[32,8,384]{2,1,0:T(8,128)(2,1)S(1)} all-to-all(bf16[32,8,384]{2,1,0:T(8,128)(2,1)S(1)} %add_convert_fusion), channel_id=1, replica_groups=mesh['yl'=2,'x'=4,'yh'=4,'zh'=2,'zl'=4,'c'=2] {'yh','zh','zl'}, dimensions={0} | all-to-all | bytes 393216 | tf_op jit(solution)/shard_map/all_to_all | solution.py:281
  88.7 17.3 %all_to_all.54.own_ref = bf16[32,8,384]{2,1,0:T(8,128)(2,1)S(1)} all-to-all(bf16[32,8,384]{2,1,0:T(8,128)(2,1)S(1)} %resid.1), channel_id=1, replica_groups=mesh['yl'=2,'x'=4,'yh'=4,'zh'=2,'zl'=4,'c'=2] {'yh','zh','zl'}, dimensions={0} | all-to-all | bytes 393216 | tf_op jit(solution)/shard_map/all_to_all | solution.py:281
  106.0 1.9 %collective-permute-start.1 = (bf16[32,8,384]{2,1,0:T(8,128)(2,1)S(1)}, bf16[32,8,384]{2,1,0:T(8,128)(2,1)S(1)}, u32[]{:S(2)}, u32[]{:S(2)}) collective-permute-start(bf16[32,8,384]{2,1,0:T(8,128)(2,1)S(1)} %all_to_all.54.own_ref), channel_id=1, source_target_pairs={{0,1},{1,0},{2,3},{3,2},{4,5},{5,4},{6,7},{7,6},{8,9},{9,8},{10,11... | collective-permute-start | bytes 589832 | tf_op jit(solution)/shard_map/ppermute | solution.py:368
  107.9 1.4 collective-permute-done.1.other_ref
  109.3 0.6 gate_parts.1
  110.0 11.3 %all_to_all.55.got_ref = bf16[8,32,640]{2,1,0:T(8,128)(2,1)S(1)} all-to-all(bf16[8,32,640]{2,1,0:T(8,128)(2,1)S(1)} %get-tuple-element.29), channel_id=1, replica_groups=mesh['yl'=2,'x'=4,'yh'=4,'zh'=2,'zl'=4,'c'=2] {'yl','x'}, dimensions={0} | all-to-all | bytes 655360 | tf_op jit(solution)/shard_map/all_to_all | solution.py:281
  121.3 0.5 hidden.1
  121.8 9.3 %all_to_all.56.got_ref = bf16[8,32,384]{2,1,0:T(8,128)(2,1)S(1)} all-to-all(bf16[8,32,384]{2,1,0:T(8,128)(2,1)S(1)} %hidden.1), channel_id=1, replica_groups=mesh['yl'=2,'x'=4,'yh'=4,'zh'=2,'zl'=4,'c'=2] {'yl','x'}, dimensions={0} | all-to-all | bytes 393216 | tf_op jit(solution)/shard_map/all_to_all | solution.py:281
  131.0 0.6 down_parts.1
  131.6 12.1 %all_to_all.57 = bf16[16,4,24,128]{3,2,1,0:T(8,128)(2,1)S(1)} all-to-all(bf16[16,4,24,128]{3,2,1,0:T(8,128)(2,1)S(1)} %bitcast.25), channel_id=1, replica_groups=mesh['yl'=2,'x'=4,'yh'=4,'zh'=2,'zl'=4,'c'=2] {'yl','x','c'}, dimensions={0} | all-to-all | bytes 786432 | tf_op jit(solution)/shard_map/all_to_all | solution.py:281
  143.7 17.2 %all_to_all.58.got_ref = bf16[32,24,128]{2,1,0:T(8,128)(2,1)S(1)} all-to-all(bf16[32,24,128]{2,1,0:T(8,128)(2,1)S(1)} %bitcast.21), channel_id=1, replica_groups=mesh['yl'=2,'x'=4,'yh'=4,'zh'=2,'zl'=4,'c'=2] {'yh','zh','zl'}, dimensions={0} | all-to-all | bytes 393216 | tf_op jit(solution)/shard_map/all_to_all | solution.py:281
  161.0 0.8 layer_out.1
  (21 shorter events, 0.2 us)
Async XLA Ops:
  0.0 57.4 %copy-start = (f32[32,1,128,128]{3,2,1,0:T(8,128)S(1)}, f32[32,1,128,128]{3,2,1,0:T(8,128)}, u32[]{:S(2)}) copy-start(f32[32,1,128,128]{3,2,1,0:T(8,128)} %param.28) | copy-start | bytes 6291460
  30.5 13.9 %all-to-all-start.1 = ((bf16[16,4,24,128]{3,2,1,0:T(8,128)(2,1)}), bf16[16,4,24,128]{3,2,1,0:T(8,128)(2,1)S(1)}, u32[]{:S(2)}, u32[]{:S(2)}) async-start(bf16[16,4,24,128]{3,2,1,0:T(8,128)(2,1)} %bitcast.3), calls=%async_computation.1 | async-start | bytes 786432 | tf_op jit(solution)/shard_map/all_to_all | solution.py:281
  44.4 23.5 %copy-start.5 = (bf16[768,128]{1,0:T(8,128)(2,1)S(1)}, bf16[768,128]{1,0:T(8,128)(2,1)}, u32[]{:S(2)}) copy-start(bf16[768,128]{1,0:T(8,128)(2,1)} %weight_ref.1) | copy-start | bytes 589828
  57.4 52.0 %copy-start.1 = (bf16[768,288]{0,1:T(8,128)(2,1)S(1)}, bf16[768,288]{0,1:T(8,128)(2,1)}, u32[]{:S(2)}) copy-start(bf16[768,288]{0,1:T(8,128)(2,1)} %param.21) | copy-start | bytes 1327108
  57.4 52.0 %copy-start.2 = (bf16[768,288]{0,1:T(8,128)(2,1)S(1)}, bf16[768,288]{0,1:T(8,128)(2,1)}, u32[]{:S(2)}) copy-start(bf16[768,288]{0,1:T(8,128)(2,1)} %param.22) | copy-start | bytes 1327108
  57.4 52.0 %copy-start.4 = (bf16[6144,32]{0,1:T(8,128)(2,1)S(1)}, bf16[6144,32]{0,1:T(8,128)(2,1)}, u32[]{:S(2)}) copy-start(bf16[6144,32]{0,1:T(8,128)(2,1)} %param.24) | copy-start | bytes 1179652
  57.4 52.0 %copy-start.6 = (f32[6144]{0:T(1024)S(1)}, f32[6144]{0:T(1024)}, u32[]{:S(2)}) copy-start(f32[6144]{0:T(1024)} %param.26) | copy-start | bytes 73732
  68.2 3.3 %collective-permute-start = (bf16[32,8,384]{2,1,0:T(8,128)(2,1)S(1)}, bf16[32,8,384]{2,1,0:T(8,128)(2,1)S(1)}, u32[]{:S(2)}, u32[]{:S(2)}) collective-permute-start(bf16[32,8,384]{2,1,0:T(8,128)(2,1)S(1)} %get-tuple-element.27), channel_id=1, source_target_pairs={{0,1},{1,0},{2,3},{3,2},{4,5},{5,4},{6,7},{7,6},{8,9},{9,8},{10,11... | collective-permute-start | bytes 589832 | tf_op jit(solution)/shard_map/ppermute | solution.py:306
  71.5 49.7 %copy-start.7 = (s32[32]{0:T(128)S(1)}, s32[32]{0:T(128)}, u32[]{:S(2)}) copy-start(s32[32]{0:T(128)} %param.30) | copy-start | bytes 388
  71.5 49.7 %copy-start.8 = (s32[32,2]{0,1:T(2,128)S(1)}, s32[32,2]{0,1:T(2,128)}, u32[]{:S(2)}) copy-start(s32[32,2]{0,1:T(2,128)} %param.29) | copy-start | bytes 772
  88.6 42.4 %copy-start.3 = (bf16[768,288]{0,1:T(8,128)(2,1)S(1)}, bf16[768,288]{0,1:T(8,128)(2,1)}, u32[]{:S(2)}) copy-start(bf16[768,288]{0,1:T(8,128)(2,1)} %param.23) | copy-start | bytes 1327108
  106.0 3.3 %collective-permute-start.1 = (bf16[32,8,384]{2,1,0:T(8,128)(2,1)S(1)}, bf16[32,8,384]{2,1,0:T(8,128)(2,1)S(1)}, u32[]{:S(2)}, u32[]{:S(2)}) collective-permute-start(bf16[32,8,384]{2,1,0:T(8,128)(2,1)S(1)} %all_to_all.54.own_ref), channel_id=1, source_target_pairs={{0,1},{1,0},{2,3},{3,2},{4,5},{5,4},{6,7},{7,6},{8,9},{9,8},{10,11... | collective-permute-start | bytes 589832 | tf_op jit(solution)/shard_map/ppermute | solution.py:368
